TPU v7x, 32 devices: a whole 2x2x4 slice. The times are simulated.
32 devices in a mesh: dp: 16 (over z, y, core), chan: 2 (over x).
Axes of the slice: x: 2, y: 2, z: 4, core: 2. Of those that a mesh axis runs over, the one named last changes fastest.
Arguments:
- hidden_in: bfloat16 [65536, 768], P(('dp', 'chan')), may hold values from -6 to 6
- norm_gain: float32 [768], replicated, may hold values from 0.5 to 1.5
- gate_value_weight: bfloat16 [768, 24, 128], P(None, 'chan'), may hold values from -0.21875 to 0.21875
- state_weight: bfloat16 [768, 128], replicated, may hold values from -0.21875 to 0.21875
- step_weight: bfloat16 [768, 24], P(None, 'chan'), may hold values from -0.21875 to 0.21875
- value_conv: float32 [4, 1536], P(None, 'chan'), may hold values from -3 to 3
- state_conv: float32 [4, 128], replicated, may hold values from -3 to 3
- step_bias: float32 [24], P('chan'), may hold values from -6 to -2
- decay_log: float32 [24], P('chan'), may hold values from 0 to 2.77
- skip_gain: float32 [24], P('chan'), may hold values from 0.5 to 1.5
- gate_gain: float32 [1536], P('chan'), may hold values from 0.5 to 1.5
- out_weight: bfloat16 [1536, 768], P('chan'), may hold values from -0.15625 to 0.15625
- seq_length: int32 [16], P('dp'), may hold values from 1024 to 4096, as said below
- seq_count: int32 [16], P('dp'), may hold values from 1 to 4, as said below
- out_grad: bfloat16 [65536, 768], P(('dp', 'chan')), may hold values from -6 to 6
Outputs:
- output: bfloat16 [65536, 768], P(('dp', 'chan'))
- input_grad: bfloat16 [65536, 768], P(('dp', 'chan'))
- norm_gain_grad: float32 [768], replicated
- gate_value_weight_grad: float32 [768, 24, 128], P(None, 'chan')
- state_weight_grad: float32 [768, 128], replicated
- step_weight_grad: float32 [768, 24], P(None, 'chan')
- value_conv_grad: float32 [4, 1536], P(None, 'chan')
- state_conv_grad: float32 [4, 128], replicated
- step_bias_grad: float32 [24], P('chan')
- decay_log_grad: float32 [24], P('chan')
- skip_gain_grad: float32 [24], P('chan')
- gate_gain_grad: float32 [1536], P('chan')
- out_weight_grad: float32 [1536, 768], P('chan')
Inputs may be any that keep to these rules, and one draw needn't show every extreme that they name: `seq_length`: each index of dp holds sequences of one length, 1024, 2048 or 4096, laid end to end from its first slot. The first seq_count sequences of an index are live; its later slots are padding.
All inputs are finite; a program needn't handle non-finite values.
Results may differ from a plain program's by a relative error of at most 0.011.
Values may be sent and summed in bfloat16 or wider, within the bound.
A program may use at most 512 MiB of HBM per device.

v0:
```python
import jax
import jax.numpy as jnp
from jax import lax
from jax.sharding import PartitionSpec as P

HEADS = 24
HEAD_DIM = 64
SPAN = 128


eps = 1e-05
highest = lax.Precision.HIGHEST


def causal_conv(values, kernel, places):
    length = values.shape[0]
    result = values * kernel[-1]
    for offset in range(1, kernel.shape[0]):
        shifted = jnp.pad(values, ((offset, 0), (0, 0)))[:length]
        inside = (places >= offset).astype(values.dtype)[:, None]
        result = result + shifted * inside * kernel[-1 - offset]
    return result


def direction_pass(
    reverse, value_blocks, in_blocks, out_blocks, step_blocks, decay_blocks, reset_flags
):
    if reverse:
        summed = jnp.flip(jnp.cumsum(jnp.flip(decay_blocks, 1), axis=1), 1)
        edge_sum = summed[:, 0]
    else:
        summed = jnp.cumsum(decay_blocks, axis=1)
        edge_sum = summed[:, -1]
    block_rows = decay_blocks.shape[1]
    row_ids = lax.broadcasted_iota(jnp.int32, (block_rows, block_rows), 0)
    col_ids = lax.broadcasted_iota(jnp.int32, (block_rows, block_rows), 1)
    if reverse:
        allowed = row_ids < col_ids
    else:
        allowed = row_ids > col_ids
    allowed = allowed[None, None, :, :]
    summed_heads = jnp.transpose(summed, (0, 2, 1))
    step_heads = jnp.transpose(step_blocks, (0, 2, 1))
    spread = summed_heads[:, :, :, None] - summed_heads[:, :, None, :]
    factors = jnp.where(allowed, jnp.exp(jnp.where(allowed, spread, 0.0)), 0.0)
    affinity = jnp.einsum("bin,bjn->bij", out_blocks, in_blocks, precision=highest)
    weighted = factors * affinity[:, None, :, :] * step_heads[:, :, None, :]
    within = jnp.einsum("bhij,bjhp->bihp", weighted, value_blocks, precision=highest)
    edge_weights = jnp.exp(edge_sum[:, :, None] - summed_heads) * step_heads
    fresh = jnp.einsum(
        "bhj,bjn,bjhp->bhnp", edge_weights, in_blocks, value_blocks, precision=highest
    )
    block_decay = jnp.exp(edge_sum)

    def carry_fn(state, inputs):
        fresh_block, decay_block, flag_block = inputs
        state_in = state * (1.0 - flag_block)
        return (decay_block[:, None, None] * state_in + fresh_block, state_in)

    zero_state = jnp.zeros(fresh.shape[1:], fresh.dtype)
    last_state, states_in = lax.scan(
        carry_fn, zero_state, (fresh, block_decay, reset_flags), reverse=reverse
    )
    carried = (
        jnp.einsum("bin,bhnp->bihp", out_blocks, states_in, precision=highest)
        * jnp.exp(summed)[:, :, :, None]
    )
    return within + carried


def mix_core(
    gate_in, proj_value, state_act, proj_step, value_conv, step_bias, decay_log, skip_gain, seq_len
):
    tokens = proj_value.shape[0]
    head_count = proj_step.shape[1]
    state_dim = state_act.shape[1] // 2
    head_dim = proj_value.shape[1] // head_count
    blocks = tokens // SPAN
    places = jnp.arange(tokens, dtype=jnp.int32) % seq_len
    value_act = jax.nn.silu(causal_conv(proj_value, value_conv, places))
    step_size = jax.nn.softplus(proj_step + step_bias)
    log_decay = -step_size * jnp.exp(decay_log)
    value_blocks = value_act.reshape(blocks, SPAN, head_count, head_dim)
    in_blocks = state_act[:, :state_dim].reshape(blocks, SPAN, state_dim)
    out_blocks = state_act[:, state_dim:].reshape(blocks, SPAN, state_dim)
    step_blocks = step_size.reshape(blocks, SPAN, head_count)
    decay_blocks = log_decay.reshape(blocks, SPAN, head_count)
    starts = jnp.arange(blocks, dtype=jnp.int32) * SPAN
    first_flag = (starts % seq_len == 0).astype(value_act.dtype)
    last_flag = ((starts + SPAN) % seq_len == 0).astype(value_act.dtype)
    ahead_out = direction_pass(
        False, value_blocks, in_blocks, out_blocks, step_blocks, decay_blocks, first_flag
    )
    behind_out = direction_pass(
        True, value_blocks, in_blocks, out_blocks, step_blocks, decay_blocks, last_flag
    )
    direct = value_act.reshape(tokens, head_count, head_dim) * skip_gain[:, None]
    mixed_out = (
        ahead_out.reshape(tokens, head_count, head_dim)
        + behind_out.reshape(tokens, head_count, head_dim)
        + direct
    )
    return mixed_out.reshape(tokens, head_count * head_dim) * jax.nn.silu(gate_in)


def contract(left, right, left_dim, right_dim):
    return lax.dot_general(
        left, right, (((left_dim,), (right_dim,)), ((), ())), preferred_element_type=jnp.float32
    )


def on_device(
    hidden_in,
    norm_gain,
    gate_value_weight,
    state_weight,
    step_weight,
    value_conv,
    state_conv,
    step_bias,
    decay_log,
    skip_gain,
    gate_gain,
    out_weight,
    seq_length,
    seq_count,
    out_grad,
):
    own_tokens = hidden_in.shape[0]
    width = norm_gain.shape[0]
    inner_width = HEADS * HEAD_DIM
    channel = lax.axis_index("chan")
    rows_all = own_tokens * lax.axis_size("chan")
    own_start = channel * own_tokens
    length = seq_length[0]
    positions = jnp.arange(rows_all, dtype=jnp.int32)
    live_rows = (positions // length < seq_count[0]).astype(jnp.float32)[:, None]
    places = positions % length
    live_own = lax.dynamic_slice_in_dim(live_rows, own_start, own_tokens, 0)
    full_rows = lax.all_gather(hidden_in, "chan", axis=0, tiled=True).astype(jnp.float32)
    row_scale = lax.rsqrt(jnp.mean(full_rows * full_rows, axis=1, keepdims=True) + eps)
    unit_rows = full_rows * row_scale
    normed = (unit_rows * norm_gain).astype(jnp.bfloat16)
    local_heads = gate_value_weight.shape[1]
    head_dim = gate_value_weight.shape[2] // 2
    local_inner = local_heads * head_dim
    pair_width = local_heads * 2 * head_dim
    joined_weight = jnp.concatenate(
        [gate_value_weight.reshape(width, pair_width), step_weight], axis=1
    )
    joined_proj = jnp.dot(normed, joined_weight, preferred_element_type=jnp.float32)
    paired = joined_proj[:, :pair_width].reshape(rows_all, local_heads, 2, head_dim)
    gate_in = paired[:, :, 0].reshape(rows_all, local_inner)
    proj_value = paired[:, :, 1].reshape(rows_all, local_inner)
    proj_step = joined_proj[:, pair_width:]
    proj_state = jnp.dot(normed, state_weight, preferred_element_type=jnp.float32)

    def state_local(proj_input, kernel):
        return jax.nn.silu(causal_conv(proj_input, kernel, places))

    state_act, state_pull = jax.vjp(state_local, proj_state, state_conv)

    def core_local(
        gate_part, value_part, state_part, step_part, conv_part, bias_part, decay_part, skip_part
    ):
        return mix_core(
            gate_part,
            value_part,
            state_part,
            step_part,
            conv_part,
            bias_part,
            decay_part,
            skip_part,
            length,
        )

    gated_out, core_pull = jax.vjp(
        core_local,
        gate_in,
        proj_value,
        state_act,
        proj_step,
        value_conv,
        step_bias,
        decay_log,
        skip_gain,
    )
    local_squares = jnp.sum(gated_out * gated_out, axis=1)
    total_squares = lax.psum(local_squares, "chan")
    gate_scale = lax.rsqrt(total_squares / inner_width + eps)[:, None]
    gate_unit = gated_out * gate_scale
    gated_norm = (gate_unit * gate_gain).astype(jnp.bfloat16)
    partial_out = jnp.dot(gated_norm, out_weight, preferred_element_type=jnp.float32)
    mixed_out = lax.psum_scatter(
        partial_out.astype(jnp.bfloat16), "chan", scatter_dimension=0, tiled=True
    ).astype(jnp.float32)
    output = (hidden_in.astype(jnp.float32) + live_own * mixed_out).astype(jnp.bfloat16)
    cot_rows = lax.all_gather(out_grad, "chan", axis=0, tiled=True)
    cot_live = cot_rows * live_rows.astype(jnp.bfloat16)
    out_weight_grad = contract(gated_norm, cot_live, 0, 0)
    norm_grad_in = contract(cot_live, out_weight, 1, 1)
    gate_gain_grad = jnp.sum(norm_grad_in * gate_unit, axis=0)
    unit_grad = norm_grad_in * gate_gain
    local_dot = jnp.sum(unit_grad * gate_unit, axis=1)
    total_dot = lax.psum(local_dot, "chan")
    gated_grad = gate_scale * (unit_grad - gate_unit * (total_dot / inner_width)[:, None])
    (
        gate_in_grad,
        value_grad,
        state_act_grad,
        step_grad,
        value_conv_grad,
        step_bias_grad,
        decay_log_grad,
        skip_gain_grad,
    ) = core_pull(gated_grad)
    state_total = lax.psum(state_act_grad.astype(jnp.bfloat16), "chan").astype(jnp.float32)
    state_proj_grad, state_conv_grad = state_pull(state_total)
    paired_grad = jnp.stack(
        [
            gate_in_grad.reshape(rows_all, local_heads, head_dim),
            value_grad.reshape(rows_all, local_heads, head_dim),
        ],
        axis=2,
    ).reshape(rows_all, pair_width)
    joined_grad = jnp.concatenate([paired_grad, step_grad], axis=1).astype(jnp.bfloat16)
    state_low = state_proj_grad.astype(jnp.bfloat16)
    joined_weight_grad = contract(normed, joined_grad, 0, 0)
    state_weight_grad = contract(normed, state_low, 0, 0)
    owner = (channel == 0).astype(jnp.float32)
    back_local = contract(joined_grad, joined_weight, 1, 1) + owner * contract(
        state_low, state_weight, 1, 1
    )
    normed_part = lax.psum_scatter(
        back_local.astype(jnp.bfloat16), "chan", scatter_dimension=0, tiled=True
    ).astype(jnp.float32)
    unit_own = lax.dynamic_slice_in_dim(unit_rows, own_start, own_tokens, 0)
    scale_own = lax.dynamic_slice_in_dim(row_scale, own_start, own_tokens, 0)
    scaled_own = normed_part * norm_gain
    norm_dot = jnp.sum(scaled_own * unit_own, axis=1)
    gain_part = jnp.sum(normed_part * unit_own, axis=0)
    norm_gain_grad = lax.psum(gain_part, "chan")
    input_grad = (
        out_grad.astype(jnp.float32)
        + scale_own * (scaled_own - unit_own * (norm_dot / width)[:, None])
    ).astype(jnp.bfloat16)
    gate_value_weight_grad = joined_weight_grad[:, :pair_width].reshape(
        width, local_heads, 2 * head_dim
    )
    step_weight_grad = joined_weight_grad[:, pair_width:]
    all_sums = lax.psum(
        (
            norm_gain_grad,
            gate_value_weight_grad,
            state_weight_grad,
            step_weight_grad,
            value_conv_grad,
            state_conv_grad,
            step_bias_grad,
            decay_log_grad,
            skip_gain_grad,
            gate_gain_grad,
            out_weight_grad,
        ),
        "dp",
    )
    return (
        output,
        input_grad,
        all_sums[0],
        all_sums[1],
        all_sums[2],
        all_sums[3],
        all_sums[4],
        all_sums[5],
        all_sums[6],
        all_sums[7],
        all_sums[8],
        all_sums[9],
        all_sums[10],
    )


def solution(mesh):
    in_specs = (
        P(("dp", "chan"), None),
        P(),
        P(None, "chan", None),
        P(),
        P(None, "chan"),
        P(None, "chan"),
        P(),
        P("chan"),
        P("chan"),
        P("chan"),
        P("chan"),
        P("chan", None),
        P("dp"),
        P("dp"),
        P(("dp", "chan"), None),
    )
    out_specs = (
        P(("dp", "chan"), None),
        P(("dp", "chan"), None),
        P(),
        P(None, "chan", None),
        P(),
        P(None, "chan"),
        P(None, "chan"),
        P(),
        P("chan"),
        P("chan"),
        P("chan"),
        P("chan"),
        P("chan", None),
    )
    return jax.shard_map(
        on_device, mesh=mesh, in_specs=in_specs, out_specs=out_specs, check_vma=False
    )
```

profile of v0, /device:TPU:1, one launch (start us, length us, event | category | flops | bytes accessed | tf_op | source)
XLA Modules:
  0.0 2404.2 jit_solution(15566387435467132165)
XLA Ops:
  23.0 69.1 %all-gather.3.cloned.1.call-done = bf16[4096,768]{1,0:T(8,128)(2,1)} async-done(((bf16[2048,768]{1,0:T(8,128)(2,1)}), bf16[4096,768]{1,0:T(8,128)(2,1)}) %all-gather.3.cloned.1.call-update) | async-done | bytes 6291472 | tf_op jit(solution)/shard_map/all_gather | solution.py:140
  207.9 29.4 %fusion.75 = (f32[4096,768]{1,0:T(8,128)}, f32[4096,768]{1,0:T(8,128)}) fusion(f32[768]{0:T(1024)S(1)} %copy-done.84, f32[4096]{0:T(1024)S(1)} %fusion.197, f32[4096,768]{1,0:T(8,128)} %copy.478, f32[768]{0:T(1024)S(1)} %copy-done.85, f32[4096]{0:T(1024)S(1)} %copy-done.47, f32[768]{0:T(1024)S(1)} %copy-done.83, f32[4096]{0:T(1024)S(1)} %copy-done.44, ...), kind=kLoop, calls=%fused_computation.141 | loop fusion | flops 44040192 | bytes 37810176 | tf_op jit(solution)/shard_map/jvp(jit(silu))/mul | solution.py:80
  266.2 26.2 %fusion.26 = f32[32,12,64,64]{3,2,1,0:T(8,128)} fusion(f32[32,128,12,64]{1,0,3,2:T(8,128)} %bitcast.372, f32[32,128,12]{1,2,0:T(8,128)S(1)} %copy.505, f32[32,128,64]{1,2,0:T(8,128)} %copy.491), kind=kOutput, calls=%fused_computation.54 | convolution fusion | flops 2419064832 | bytes 20119552 | tf_op jit(solution)/shard_map/jvp(bhj,bjn,bjhp->bhnp)/dot_general | solution.py:50
  298.6 223.9 %while.73 = (s32[]{:T(128)}, f32[12,64,64]{2,1,0:T(8,128)}, f32[32,12,64,64]{3,2,1,0:T(8,128)}, f32[32]{0:T(128)S(1)}, f32[32,12,1,1]{1,3,2,0:T(1,128)S(1)}, /*i...) while((s32[]{:T(128)}, f32[12,64,64]{2,1,0:T(8,128)}, ...), condition=%wide.region_6.7_spmd.clone, body=%wide.region_5.6_spmd.clone.sunk | while | flops 294917 | bytes 1378280 | solution.py:61
  550.5 26.1 %fusion.30 = f32[32,12,64,64]{3,2,1,0:T(8,128)} fusion(f32[32,128,12,64]{1,0,3,2:T(8,128)} %bitcast.373, f32[32,128,12]{1,2,0:T(8,128)S(1)} %copy.493, f32[32,128,64]{1,2,0:T(8,128)S(1)} %copy-done.5), kind=kOutput, calls=%fused_computation.58 | convolution fusion | flops 2419064832 | bytes 20119552 | tf_op jit(solution)/shard_map/jvp(bhj,bjn,bjhp->bhnp)/dot_general | solution.py:50
  582.7 223.2 %while.72 = (s32[]{:T(128)}, f32[12,64,64]{2,1,0:T(8,128)}, f32[32,12,64,64]{3,2,1,0:T(8,128)}, f32[32]{0:T(128)S(1)}, f32[32,12,1,1]{1,3,2,0:T(1,128)S(1)}, /*i...) while((s32[]{:T(128)}, f32[12,64,64]{2,1,0:T(8,128)}, ...), condition=%wide.region_3.4_spmd.clone, body=%wide.region_2.3_spmd.clone.sunk | while | flops 294916 | bytes 1378260 | solution.py:61
  838.1 55.4 %fusion.15 = f32[32,12,64,128]{3,2,1,0:T(8,128)} fusion(f32[32,12,128]{2,1,0:T(8,128)} %copy.501, f32[32,12,128]{2,1,0:T(8,128)} %copy.489, f32[32,128,128]{2,1,0:T(8,128)} %fusion.224, pred[128,128]{1,0:T(8,128)(4,1)S(1)} %copy-done.95, f32[32,128,12,64]{1,0,3,2:T(8,128)} %bitcast.374), kind=kOutput, calls=%fused_computation.43 | convolution fusion | flops 4863295488 | bytes 27672576 | tf_op jit(solution)/shard_map/jvp(bhij,bjhp->bihp)/dot_general | solution.py:48
  893.5 57.9 %fusion.53 = f32[32,128,12,64]{1,3,2,0:T(8,128)} fusion(f32[32,12,64,128]{3,2,1,0:T(8,128)} %fusion.15, f32[32,128,12,64]{1,3,2,0:T(8,128)S(1)} %bitcast.392, f32[32,128,12,64]{1,3,2,0:T(8,128)} %bitcast.393, f32[32,128,12]{1,2,0:T(8,128)S(1)} %copy.509, f32[32,128,12]{1,2,0:T(8,128)S(1)} %copy-done.31, f32[32,12,128]{2,1,0:T(8,128)S(1)} %copy-done.64, ...), kind=kOutput, calls=%fused_computation.98 | convolution fusion | flops 4879024128 | bytes 65814528 | tf_op jit(solution)/shard_map/jvp(bhij,bjhp->bihp)/dot_general | solution.py:48
  1065.9 29.3 %multiply_reduce_fusion.5 = (f32[768]{0:T(1024)}, f32[4096,768]{1,0:T(8,128)}, bf16[4096,768]{1,0:T(8,128)(2,1)}) fusion(f32[4096,768]{1,0:T(8,128)} %get-tuple-element.786, f32[4096,768]{1,0:T(8,128)} %copy.514, f32[4096]{0:T(1024)S(1)} %broadcast_multiply_fusion, f32[4096,768]{1,0:T(8,128)} %get-tuple-element.784, f32[4096,768]{1,0:T(8,128)} %get-tuple-element.820, ...), kind=kLoop, calls=%fused_computation.101 | loop fusion | flops 81788160 | bytes 81830912 | tf_op jit(solution)/shard_map/transpose(jvp())/reduce_sum | solution.py:97
  1157.1 100.6 %fusion.33 = (f32[32,12,128]{2,1,0:T(8,128)}, f32[32,12,128]{2,1,0:T(8,128)}, f32[32,12,128]{2,1,0:T(8,128)}, f32[32,12,128]{2,1,0:T(8,128)}, f32[32,12,128]{2,1...) fusion(f32[32,12,128]{2,1,0:T(8,128)S(1)} %copy-done.63, ...), kind=kOutput, calls=%fused_computation.63 | convolution fusion | flops 5006655488 | bytes 33259520 | tf_op jit(solution)/shard_map/transpose(jvp(bhij,bjhp->bihp))/dot_general | solution.py:48
  1257.7 36.8 %fusion.20 = f32[32,12,64,128]{3,2,1,0:T(8,128)} fusion(f32[32,12,128]{2,1,0:T(8,128)S(1)} %copy-done.65, f32[32,128,128]{2,1,0:T(8,128)S(1)} %copy-done.40, f32[32,12,128]{2,1,0:T(8,128)S(1)} %copy-done.62, pred[128,128]{1,0:T(8,128)(4,1)S(1)} %copy-done.98, f32[32,12,64,128]{3,0,2,1:T(8,128)S(1)} %bitcast.368), kind=kOutput, calls=%fused_computation.48 | convolution fusion | flops 4863295488 | bytes 27672576 | tf_op jit(solution)/shard_map/transpose(jvp(bhij,bjhp->bihp))/dot_general | solution.py:48
  1294.5 37.4 %fusion.13 = f32[32,12,64,128]{3,2,1,0:T(8,128)} fusion(f32[32,12,128]{2,1,0:T(8,128)S(1)} %copy-done.63, f32[32,12,128]{2,1,0:T(8,128)S(1)} %copy-done.65, f32[32,128,128]{2,1,0:T(8,128)S(1)} %copy-done.41, pred[128,128]{1,0:T(8,128)(4,1)S(1)} %copy-done.96, f32[32,12,64,128]{3,0,2,1:T(8,128)S(1)} %bitcast.369), kind=kOutput, calls=%fused_computation.42 | convolution fusion | flops 4863295488 | bytes 27672576 | tf_op jit(solution)/shard_map/transpose(jvp(bhij,bjhp->bihp))/dot_general | solution.py:48
  1331.9 26.2 %fusion.156 = f32[32,128,64]{1,2,0:T(8,128)} fusion(f32[32,12,64,64]{3,2,1,0:T(8,128)} %get-tuple-element.1115, f32[32,128,12,64]{1,0,3,2:T(8,128)S(1)} %bitcast.370, f32[32,128,12]{1,2,0:T(8,128)S(1)} %copy-done.32), kind=kOutput, calls=%fused_computation.241 | convolution fusion | flops 2419064832 | bytes 20119552 | tf_op jit(solution)/shard_map/transpose(jvp(bin,bhnp->bihp))/dot_general | solution.py:65
  1358.2 26.8 %fusion.153 = f32[32,128,64]{1,2,0:T(8,128)} fusion(f32[32,12,64,64]{3,2,1,0:T(8,128)} %get-tuple-element.1148, f32[32,128,12,64]{1,0,3,2:T(8,128)S(1)} %bitcast.371, f32[32,128,12]{1,2,0:T(8,128)S(1)} %copy.509), kind=kOutput, calls=%fused_computation.240 | convolution fusion | flops 2419064832 | bytes 20119552 | tf_op jit(solution)/shard_map/transpose(jvp(bin,bhnp->bihp))/dot_general | solution.py:65
  1391.1 163.4 %while.75 = (s32[]{:T(128)}, f32[12,64,64]{2,1,0:T(8,128)S(1)}, f32[32,12,64,64]{3,2,1,0:T(8,128)}, f32[32,12]{1,0:T(8,128)S(1)}, f32[32,12,64,64]{2,3,1,0:T(8,1...) while((s32[]{:T(128)}, f32[12,64,64]{2,1,0:T(8,128)S(1)}, ...), condition=%wide.region_17.18_spmd.clone, body=%wide.region_15.17_spmd.clone.sunk | while | flops 344056 | bytes 2163152 | solution.py:61
  1554.5 31.0 %fusion.49 = (f32[32,128,64]{1,2,0:T(8,128)}, f32[32,12,64,128]{3,2,1,0:T(8,128)}) fusion(f32[32,128,12]{1,2,0:T(8,128)S(1)} %copy-done.19, f32[32,12,64,64]{3,2,1,0:T(8,128)} %get-tuple-element.430, f32[32,128,12,64]{1,0,3,2:T(8,128)} %bitcast.376), kind=kOutput, calls=%fused_computation.90 | convolution fusion | flops 2421948416 | bytes 32702464 | tf_op jit(solution)/shard_map/transpose(jvp(bhj,bjn,bjhp->bhnp))/dot_general | solution.py:50
  1591.6 163.3 %while.74 = (s32[]{:T(128)}, f32[12,64,64]{2,1,0:T(8,128)S(1)}, f32[32,12,64,64]{3,2,1,0:T(8,128)}, f32[32,12]{1,0:T(8,128)S(1)}, f32[32,12,64,64]{2,3,1,0:T(8,1...) while((s32[]{:T(128)}, f32[12,64,64]{2,1,0:T(8,128)S(1)}, ...), condition=%wide.region_14.15_spmd.clone, body=%wide.region_12.14_spmd.clone.sunk | while | flops 344055 | bytes 2163132 | solution.py:61
  1754.9 24.1 %fusion.24 = f32[32,12,64,128]{3,2,1,0:T(8,128)} fusion(f32[32,12,64,64]{3,2,1,0:T(8,128)} %get-tuple-element.427, f32[32,128,12]{1,2,0:T(8,128)} %copy-done.21, f32[32,128,64]{1,2,0:T(8,128)S(1)} %copy-done.6), kind=kOutput, calls=%fused_computation.52 | convolution fusion | flops 2419064832 | bytes 20119552 | tf_op jit(solution)/shard_map/transpose(jvp(bhj,bjn,bjhp->bhnp))/dot_general | solution.py:50
  1779.1 32.9 %fusion.52 = (f32[32,128,12]{1,2,0:T(8,128)S(1)}, f32[32,128,12]{1,2,0:T(8,128)S(1)}, f32[32,12,64,128]{3,2,1,0:T(8,128)}) fusion(f32[32,128,64]{1,2,0:T(8,128)S(1)} %copy-done.6, f32[32,12,64,128]{3,2,1,0:T(8,128)} %get-tuple-element.823, f32[32,12,64,64]{3,2,1,0:T(8,128)} %get-tuple-element.427, f32[32,128,12,64]{1,0,3,2:T(8,128)} %bitcast.377), kind=kOutput, calls=%fused_computation.96 | convolution fusion | flops 2428403712 | bytes 45481984 | tf_op jit(solution)/shard_map/transpose(jvp(bhj,bjn,bjhp->bhnp))/dot_general | solution.py:50
  1816.3 29.3 %add_bitcast_fusion = f32[32,128,12,64]{1,3,2,0:T(8,128)} fusion(f32[32,12,64,128]{3,2,1,0:T(8,128)} %fusion.20, f32[32,12,64,128]{3,2,1,0:T(8,128)} %fusion.24, f32[32,12,64,128]{3,2,1,0:T(8,128)} %fusion.13, f32[32,12,64,64]{3,2,1,0:T(8,128)} %get-tuple-element.430, f32[32,128,12]{1,2,0:T(8,128)S(1)} %copy-done.20, f32[32,128,64]{1,2,0:T(8,128)S(1)} %copy-done.6), kind=kOutput, calls=%fused_computation.112 | convolution fusion | flops 2428502016 | bytes 57868288 | tf_op jit(solution)/shard_map/transpose(jvp(bhj,bjn,bjhp->bhnp))/dot_general | solution.py:50
  1897.8 38.6 %multiply_reduce_fusion.9 = (f32[768]{0:T(1024)}, f32[768]{0:T(1024)}, f32[768]{0:T(1024)}, f32[768]{0:T(1024)}, f32[4096,768]{1,0:T(8,128)}) fusion(f32[4096,768]{1,0:T(8,128)} %copy.478, f32[4096]{0:T(1024)S(1)} %copy-done.43, f32[4096]{0:T(1024)S(1)} %copy-done.45, f32[4096]{0:T(1024)S(1)} %copy-done.48, f32[4096,768]{1,0:T(8,128)} %get-tuple-element.786, ...), kind=kLoop, calls=%fused_computation.105 | loop fusion | flops 69202944 | bytes 62979072 | tf_op jit(solution)/shard_map/transpose(jvp())/reduce_sum | solution.py:21
  2012.0 26.1 %fusion.223 = f32[32,128,12]{2,0,1:T(8,128)S(1)} fusion(f32[32,128,12]{2,0,1:T(8,128)S(1)} %copy.556), kind=kOutput, calls=%fused_computation.356 | output fusion | flops 6242304 | bytes 393216 | tf_op jit(solution)/shard_map/transpose(jvp(jit(cumsum)))/reduce_window_sum | solution.py:32
  2232.5 62.1 %all-reduce.24 = (f32[768]{0:T(1024)}, f32[768,12]{0,1:T(8,128)}, f32[4,768]{1,0:T(4,128)}, f32[4,128]{1,0:T(4,128)}, f32[12]{0:T(128)}, /*index=5*/f32[12]{0:T(128)}, f32[12]{0:T(128)}, f32[768]{0:T(1024)}) all-reduce(f32[768]{0:T(1024)S(1)} %psum.108, f32[768,12]{0,1:T(8,128)S(1)} %slice-done.8, ...), channel_id=1, replica_groups=mesh['dp'=16,'chan'=2] {'dp'}, use_global_device_ids=true, to_apply=%region_37.38 | all-reduce | flops 14372 | bytes 114976 | tf_op jit(solution)/shard_map/psum | solution.py:252
  2301.2 85.9 %all-reduce.31.cloned.1.call-done = (f32[768,12,128]{2,0,1:T(8,128)}, f32[768,128]{1,0:T(8,128)}, f32[768,768]{1,0:T(8,128)}) async-done(((f32[768,12,128]{2,0,1:T(8,128)}, f32[768,128]{1,0:T(8,128)}, f32[768,768]{1,0:T(8,128)}), (f32[768,12,128]{2,0,1:T(8,128)}, f32[768,128]{1,0:T(8,128)}, f32[768,768]{1,0:T(8,128)})) %all-reduce.31.cloned.1.call-update) | async-done | bytes 7471120 | tf_op jit(solution)/shard_map/psum | solution.py:252
  (1214 shorter events, 1532.9 us)
Async XLA Ops:
  7.2 1037.5 %copy-start = (bf16[768,768]{1,0:T(8,128)(2,1)S(1)}, bf16[768,768]{1,0:T(8,128)(2,1)}, u32[]{:S(2)}) copy-start(bf16[768,768]{1,0:T(8,128)(2,1)} %param.34) | copy-start | bytes 3538948
  7.2 84.9 %all-gather.3.cloned.1.call-start = ((), (), s32[]{:S(2)}) async-start(), calls=%async_computation.2 | async-start | bytes 9437184 | tf_op jit(solution)/shard_map/all_gather | solution.py:140
  7.9 1036.7 %all-gather.5.cloned.1.call-start = ((), (), s32[]{:S(2)}) async-start(), calls=%async_computation.4 | async-start | bytes 9437184 | tf_op jit(solution)/shard_map/all_gather | solution.py:199
  8.7 2119.6 %all-reduce.29.cloned.1.call-start = ((), (), s32[]{:S(2)}) async-start(), calls=%async_computation.5 | async-start | bytes 2097152 | tf_op jit(solution)/shard_map/psum | solution.py:218
  9.6 198.3 %copy-start.42 = (f32[4096]{0:T(1024)}, f32[4096]{0:T(1024)S(1)}, u32[]{:S(2)}) copy-start(f32[4096]{0:T(1024)S(1)} %fusion.197) | copy-start | bytes 49156
  14.6 98.8 %copy-start.37 = (bf16[768,12,128]{0,2,1:T(8,128)(2,1)}, bf16[768,12,128]{0,2,1:T(8,128)(2,1)S(1)}, u32[]{:S(2)}) copy-start(bf16[768,12,128]{0,2,1:T(8,128)(2,1)S(1)} %copy.476) | copy-start | bytes 7077892
  169.4 94.8 %copy-start.16 = (f32[32,128,12]{1,0,2:T(8,128)}, f32[32,128,12]{1,0,2:T(8,128)S(1)}, u32[]{:S(2)}) copy-start(f32[32,128,12]{1,0,2:T(8,128)S(1)} %rev.15) | copy-start | bytes 589828
  184.0 954.0 %copy-start.2 = (f32[4096,64]{1,0:T(8,128)}, f32[4096,64]{1,0:T(8,128)S(1)}, u32[]{:S(2)}) copy-start(f32[4096,64]{1,0:T(8,128)S(1)} %get-tuple-element.809) | copy-start | bytes 3145732
  838.0 55.4 %copy-start.4 = (f32[32,128,768]{1,2,0:S(1)}, f32[32,128,768]{1,2,0}, u32[]{:S(2)}) copy-start(f32[32,128,768]{1,2,0} %fusion.226) | copy-start | bytes 37748740
  838.0 55.4 %copy-start.31 = (f32[32,128,12]{1,2,0:T(8,128)S(1)}, f32[32,128,12]{1,2,0:T(8,128)}, u32[]{:S(2)}) copy-start(f32[32,128,12]{1,2,0:T(8,128)} %copy.498) | copy-start | bytes 589828
  838.0 55.4 %copy-start.39 = (f32[32,128,128]{2,1,0:T(8,128)S(1)}, f32[32,128,128]{2,1,0:T(8,128)}, u32[]{:S(2)}) copy-start(f32[32,128,128]{2,1,0:T(8,128)} %fusion.224) | copy-start | bytes 6291460
  838.0 55.4 %copy-start.61 = (f32[32,12,128]{2,1,0:T(8,128)S(1)}, f32[32,12,128]{2,1,0:T(8,128)}, u32[]{:S(2)}) copy-start(f32[32,12,128]{2,1,0:T(8,128)} %copy.485) | copy-start | bytes 589828
  838.0 55.4 %copy-start.64 = (f32[32,12,128]{2,1,0:T(8,128)S(1)}, f32[32,12,128]{2,1,0:T(8,128)}, u32[]{:S(2)}) copy-start(f32[32,12,128]{2,1,0:T(8,128)} %copy.489) | copy-start | bytes 589828
  838.1 55.4 %copy-start.97 = (pred[128,128]{1,0:T(8,128)(4,1)S(1)}, pred[128,128]{1,0:T(8,128)(4,1)}, u32[]{:S(2)}) copy-start(pred[128,128]{1,0:T(8,128)(4,1)} %get-tuple-element.829) | copy-start | bytes 49156
  1157.1 100.6 %copy-start.40 = (f32[32,128,128]{2,1,0:T(8,128)S(1)}, f32[32,128,128]{2,1,0:T(8,128)}, u32[]{:S(2)}) copy-start(f32[32,128,128]{2,1,0:T(8,128)} %fusion.224) | copy-start | bytes 6291460
  1294.5 37.4 %copy-start.32 = (f32[32,128,12]{1,2,0:T(8,128)S(1)}, f32[32,128,12]{1,2,0:T(8,128)}, u32[]{:S(2)}) copy-start(f32[32,128,12]{1,2,0:T(8,128)} %copy.498) | copy-start | bytes 589828
  1391.0 163.4 %copy-start.19 = (f32[32,128,12]{1,2,0:T(8,128)S(1)}, f32[32,128,12]{1,2,0:T(8,128)}, u32[]{:S(2)}) copy-start(f32[32,128,12]{1,2,0:T(8,128)} %copy-done.18) | copy-start | bytes 589828
  1591.6 163.3 %copy-start.6 = (f32[32,128,64]{1,2,0:T(8,128)S(1)}, f32[32,128,64]{1,2,0:T(8,128)}, u32[]{:S(2)}) copy-start(f32[32,128,64]{1,2,0:T(8,128)} %copy.491) | copy-start | bytes 3145732
  1779.1 37.3 %copy-start.20 = (f32[32,128,12]{1,2,0:T(8,128)S(1)}, f32[32,128,12]{1,2,0:T(8,128)}, u32[]{:S(2)}) copy-start(f32[32,128,12]{1,2,0:T(8,128)} %copy-done.18) | copy-start | bytes 589828
  1897.8 38.6 %copy-start.22 = (f32[32,128,12]{1,2,0:T(8,128)S(1)}, f32[32,128,12]{1,2,0:T(8,128)}, u32[]{:S(2)}) copy-start(f32[32,128,12]{1,2,0:T(8,128)} %copy-done.21) | copy-start | bytes 589828
  1973.2 226.3 %reduce-scatter.3.cloned.1.call-start = ((), (), s32[]{:S(2)}) async-start(), calls=%async_computation.3 | async-start | bytes 9437184 | tf_op jit(solution)/shard_map/reduce_scatter | solution.py:195
  1983.2 240.3 %reduce-scatter.5.cloned.1.call-start = ((), (), s32[]{:S(2)}) async-start(), calls=%async_computation.6 | async-start | bytes 9437184 | tf_op jit(solution)/shard_map/reduce_scatter | solution.py:235
  2142.6 244.6 %all-reduce.31.cloned.1.call-start = ((), (), s32[]{:S(2)}) async-start(), calls=%async_computation.7 | async-start | bytes 14942208 | tf_op jit(solution)/shard_map/psum | solution.py:252
  2199.5 95.1 %dynamic-slice-start = ((f32[4096]{0:T(1024)}, s32[]{:T(128)}), f32[2048]{0:T(1024)S(1)}, s32[]{:S(2)}) async-start(f32[4096]{0:T(1024)} %copy-done.73, s32[]{:T(128)} %select_n.84), calls=%async_computation.17 | async-start | bytes 16896 | tf_op jit(solution)/shard_map/dynamic-slice.1
  (120 other events, 1934.0 us)
Sparse Core Ops, SparseCore 0:
  9.6 82.4 all-gather.2
  93.6 80.3 all-gather.4
  1973.3 44.3 all-reduce.28
  2020.0 77.0 reduce-scatter.2
  2142.7 80.6 reduce-scatter.4
  2228.9 158.2 all-reduce.30
where the time goes:
time: 2430 us; the launch traced here: 2400 us
  other arithmetic  805 us (33%)
  matrix products  711 us (29%)
  local copies, waits for them, and re-layouts  614 us (25%)
  waiting for transfers between devices  175 us (7%)
  blocking collectives  79.6 us (3%)
    dot_general x5, matrix products, direction_pass(): jnp.einsum('bhij,bjhp->bihp', weighted, value_blocks, precision=highest)  288 us
    dynamic_update_slice x192, other arithmetic, direction_pass(): lax.scan(carry_fn, zero_state, (fresh, block_decay, reset_flags), reverse...  243 us
    dot_general x6, matrix products, direction_pass(): jnp.einsum('bhj,bjn,bjhp->bhnp', edge_weights, in_blocks, value_blocks, p...  170 us
    add x64, other arithmetic, carry_fn(): return (decay_block[:, None, None] * state_in + fresh_block, state_in)  166 us
    reduce_sum x64, other arithmetic, carry_fn(): return (decay_block[:, None, None] * state_in + fresh_block, state_in)  118 us
    dynamic_slice x192, local copies, waits for them, and re-layouts, direction_pass(): lax.scan(carry_fn, zero_state, (fresh, block_decay, reset_flags), reverse...  113 us
    dot_general x4, matrix products, direction_pass(): jnp.einsum('bin,bhnp->bihp', out_blocks, states_in, precision=highest)  90.2 us
    unnamed x284, local copies, waits for them, and re-layouts  86.7 us
  transfers between devices with their start and end apart: 6, of which 3 were waited for; matrix products, arithmetic and copies ran while one was open for 50% of the time, Pallas kernels for 0%

commit v1 on v0

v1 whole, which is shorter than its diff:
```python
import functools

import jax
import jax.numpy as jnp
import numpy as np
from jax import lax
from jax.experimental import pallas as pl
from jax.experimental.pallas import tpu as pltpu
from jax.sharding import PartitionSpec as P

HEAD_DIM = 64
STATE = 64
SPAN = 128
PAD = 16
GROUP = 32
TAPS = 4
EPS = 1e-05
LOG2E = float(np.log2(np.e))
BF = jnp.bfloat16
F32 = jnp.float32


def dot(a, b):
    return jnp.dot(a, b, preferred_element_type=F32)


def dot_nt(a, b):
    return lax.dot_general(a, b, (((1,), (1,)), ((), ())), preferred_element_type=F32)


def dot_tn(a, b):
    return lax.dot_general(a, b, (((0,), (0,)), ((), ())), preferred_element_type=F32)


def sigmoid(v):
    return 0.5 + 0.5 * jnp.tanh(0.5 * v)


def lanes_of(rows):
    return lax.broadcasted_iota(jnp.int32, (rows, 128), 1)


def shifted(ext, offset, rows):
    return ext[offset : offset + rows]


def full(shape):
    rank = len(shape)
    return pl.BlockSpec(shape, lambda i: (0,) * rank)


SMEM = pl.BlockSpec(memory_space=pltpu.SMEM)


def expanders(heads):
    channel = np.arange(heads * HEAD_DIM) // HEAD_DIM
    lane = np.arange(128)[:, None]
    return [np.asarray(lane == GROUP * g + channel[None], np.float32) for g in range(4)]


def project_kernel(
    tile, chunk, sc, hid, halo, edge, gain, wg, wv, ws, wst, cv, cs, bias, nal, tri, e0, e1,
    normed_o, gate_o, v_o, xpre_o, ps_o, pspre_o, bc_o, col_o, row_o, ff_o, sb_o, pb_o,
    sft_o, sbt_o, pft_o, pbt_o, vh_o, psh_o,
    sb_s, pb_s, sf_s, pf_s,
):
    step = pl.program_id(0)
    tiles = pl.num_programs(0)
    at = tiles - 1 - step
    length = sc[1]
    start = sc[0] + at * tile
    width = e0.shape[1]
    blocks = tile // SPAN

    @pl.when(step == 0)
    def _():
        sb_s[...] = jnp.zeros_like(sb_s)
        sf_s[...] = jnp.zeros_like(sf_s)
        pb_s[...] = jnp.ones_like(pb_s)
        pf_s[...] = jnp.ones_like(pf_s)

    before = jnp.where(at == 0, edge[...].astype(F32), halo[...].astype(F32))
    rows = jnp.concatenate([before, hid[...].astype(F32)], axis=0)
    scale = lax.rsqrt(jnp.mean(rows * rows, axis=1, keepdims=True) + EPS)
    normed = (rows * scale * gain[...]).astype(BF)
    own = normed[PAD:]
    normed_o[...] = own
    keep = jnp.where(lax.rem(start, length) == 0, 0.0, 1.0)
    row_id = lax.broadcasted_iota(jnp.int32, (tile + PAD, 1), 0)
    keep_rows = jnp.where(row_id < PAD, keep, 1.0)

    ps = dot(normed, ws[...]) * keep_rows
    ps_o[...] = ps[PAD:]
    pspre = ps[PAD:] * cs[TAPS - 1 : TAPS]
    for j in range(1, TAPS):
        pspre = pspre + shifted(ps, PAD - j, tile) * cs[TAPS - 1 - j : TAPS - j]
    pspre_o[...] = pspre
    bc = pspre * sigmoid(pspre)
    bc_o[...] = bc.astype(BF)

    z = dot(own, wst[...]) + bias[...]
    dt = jnp.maximum(z, 0.0) + jnp.log1p(jnp.exp(-jnp.abs(z)))
    sig = sigmoid(z)
    a2 = dt * nal[...]
    lane = lanes_of(SPAN)
    firsts, wmix, bts = [], [], []
    for b in range(blocks):
        sl = slice(b * SPAN, (b + 1) * SPAN)
        ab = a2[sl]
        ca = jnp.dot(tri[...], ab, precision=lax.Precision.HIGHEST, preferred_element_type=F32)
        ce = ca - ab
        col = jnp.where(lane < 32, ca, jnp.where(lane < 64, ce, jnp.where(lane < 96, dt[sl], sig[sl])))
        col_o[sl, :] = col
        row_o[sl, :] = jnp.transpose(col)
        end = ca[SPAN - 1 : SPAN]
        w = jnp.exp2(jnp.where(lane < 32, end - ca, ce)) * dt[sl]
        dec = jnp.broadcast_to(jnp.exp2(end), (8, 128))
        high = dec.astype(BF).astype(F32)
        wmix.append(jnp.concatenate([w, high, dec - high], axis=0).astype(BF))
        bts.append(jnp.transpose(bc[sl])[:STATE].astype(BF))

    for c in range(width // chunk):
        cl = slice(c * chunk, (c + 1) * chunk)
        gate_o[:, cl] = dot(own, wg[:, cl]).astype(BF)
        v = dot(normed, wv[:, cl]) * keep_rows
        v_o[:, cl] = v[PAD:].astype(BF)

        @pl.when(at == 0)
        def _():
            vh_o[:, cl] = v[:PAD]

        xpre = v[PAD:] * cv[TAPS - 1 : TAPS, cl]
        for j in range(1, TAPS):
            xpre = xpre + shifted(v, PAD - j, tile) * cv[TAPS - 1 - j : TAPS - j, cl]
        xpre_o[:, cl] = xpre.astype(BF)
        x = xpre * sigmoid(xpre)
        for b in reversed(range(blocks)):
            sl = slice(b * SPAN, (b + 1) * SPAN)
            we = dot(wmix[b], e0[:, cl])
            wbe = dot(wmix[b][:SPAN], e1[:, cl])
            dec = we[SPAN : SPAN + 1] + we[SPAN + 8 : SPAN + 9]
            xb = x[sl]
            fresh_f = dot(bts[b], (xb * we[:SPAN]).astype(BF))
            fresh_b = dot(bts[b], (xb * wbe).astype(BF))
            place = start + b * SPAN
            first = jnp.where(lax.rem(place, length) == 0, 0.0, 1.0)
            last = jnp.where(lax.rem(place + SPAN, length) == 0, 0.0, 1.0)
            ff_o[b, :, cl] = fresh_f.astype(BF)
            pf = pf_s[0:1, cl]
            sf_s[:, cl] = sf_s[:, cl] + pf * fresh_f
            pf_s[:, cl] = jnp.broadcast_to(pf * dec * first, (8, chunk))
            held = sb_s[:, cl] * last
            pb = pb_s[0:1, cl] * last
            sb_o[b, :, cl] = held.astype(BF)
            pb_o[b, :, cl] = jnp.broadcast_to(pb, (8, chunk))
            sb_s[:, cl] = held * dec + fresh_b
            pb_s[:, cl] = jnp.broadcast_to(pb * dec, (8, chunk))

    @pl.when(at == 0)
    def _():
        psh_o[...] = ps[:PAD]
        sft_o[...] = sf_s[...]
        sbt_o[...] = sb_s[...]
        pft_o[...] = pf_s[...]
        pbt_o[...] = pb_s[...]


def project(sc, hidden, edge, gain, wg, wv, ws, wst, cv, cs, bias, nal):
    tokens, width_in = hidden.shape
    width = wg.shape[1]
    heads = width // HEAD_DIM
    tile = min(256, tokens)
    tiles = tokens // tile
    per = tile // SPAN
    blocks = tokens // SPAN
    chunk = 256 if width % 256 == 0 else 128
    e0, e1, _, _ = expanders(heads)
    tri = np.tril(np.ones((SPAN, SPAN), np.float32))

    def back(shape):
        rank = len(shape)
        return pl.BlockSpec(shape, lambda i: (tiles - 1 - i,) + (0,) * (rank - 1))

    sds = jax.ShapeDtypeStruct
    outs = [
        (sds((tokens, width_in), BF), back((tile, width_in))),
        (sds((tokens, width), BF), back((tile, width))),
        (sds((tokens, width), BF), back((tile, width))),
        (sds((tokens, width), BF), back((tile, width))),
        (sds((tokens, 128), F32), back((tile, 128))),
        (sds((tokens, 128), F32), back((tile, 128))),
        (sds((tokens, 128), BF), back((tile, 128))),
        (sds((tokens, 128), F32), back((tile, 128))),
        (sds((tokens, 128), F32), back((tile, 128))),
        (sds((blocks, STATE, width), BF), back((per, STATE, width))),
        (sds((blocks, STATE, width), BF), back((per, STATE, width))),
        (sds((blocks, 8, width), F32), back((per, 8, width))),
        (sds((STATE, width), F32), full((STATE, width))),
        (sds((STATE, width), F32), full((STATE, width))),
        (sds((8, width), F32), full((8, width))),
        (sds((8, width), F32), full((8, width))),
        (sds((PAD, width), F32), full((PAD, width))),
        (sds((PAD, 128), F32), full((PAD, 128))),
    ]
    steps = tile // PAD
    in_specs = [
        SMEM,
        back((tile, width_in)),
        pl.BlockSpec((PAD, width_in), lambda i: (jnp.maximum((tiles - 1 - i) * steps - 1, 0), 0)),
        full((PAD, width_in)),
        full(gain.shape),
        full(wg.shape),
        full(wv.shape),
        full(ws.shape),
        full(wst.shape),
        full(cv.shape),
        full(cs.shape),
        full(bias.shape),
        full(nal.shape),
        full(tri.shape),
        full(e0.shape),
        full(e1.shape),
    ]
    return pl.pallas_call(
        functools.partial(project_kernel, tile, chunk),
        grid=(tiles,),
        in_specs=in_specs,
        out_specs=[spec for _, spec in outs],
        out_shape=[shape for shape, _ in outs],
        scratch_shapes=[
            pltpu.VMEM((STATE, width), F32),
            pltpu.VMEM((8, width), F32),
            pltpu.VMEM((STATE, width), F32),
            pltpu.VMEM((8, width), F32),
        ],
        compiler_params=pltpu.CompilerParams(vmem_limit_bytes=58 * 1024 * 1024),
        name="project",
    )(
        sc, hidden, hidden, edge, gain, wg, wv, ws, wst, cv, cs, bias, nal, tri,
        jnp.asarray(e0, BF), jnp.asarray(e1, BF),
    )


def mix_kernel(
    sc, gate, xpre, bc_r, col_r, row_r, ff, sbl, pb, sfd, sbd, hid, gout, ow, owt, ggain, skip,
    e0, e1, e2,
    out_o, gnorm_o, dy_o, dgate_o, sf_o, sb_o, gbl_o, pg_o, dff_o,
    gft_o, gbt_o, pgf_o, pgb_o, ggain_o, skip_o,
    sf_s, gb_s, gf_s, pg_s, q_s, y_s, dgn_s, exp_s,
):
    i = pl.program_id(0)
    length = sc[1]
    place = sc[0] + i * SPAN
    first = jnp.where(lax.rem(place, length) == 0, 0.0, 1.0)
    last = jnp.where(lax.rem(place + SPAN, length) == 0, 0.0, 1.0)
    live = jnp.where(lax.div(place, length) < sc[2], 1.0, 0.0)
    width = e0.shape[1]
    pairs = width // 128

    @pl.when(i == 0)
    def _():
        sf_s[...] = sfd[...].astype(F32)
        gb_s[...] = jnp.zeros_like(gb_s)
        gf_s[...] = jnp.zeros_like(gf_s)
        pg_s[...] = jnp.ones_like(pg_s)
        q_s[...] = jnp.ones_like(q_s)
        ggain_o[...] = jnp.zeros_like(ggain_o)
        skip_o[...] = jnp.zeros_like(skip_o)

    glow = gout[...].astype(F32) * live
    gl = glow.astype(BF)
    dgn_s[...] = dot(gl, owt[...])

    lane = lanes_of(SPAN)
    low_half = lane < HEAD_DIM
    col = col_r[...]
    row = row_r[...]
    end = jnp.broadcast_to(col[SPAN - 1 : SPAN], (8, 128))
    end1 = pltpu.roll(end, GROUP, 1)
    w = jnp.where(lane < 64, jnp.exp2(jnp.where(lane < 32, col, end1[0:1] - col)), col)
    dec = jnp.exp2(end)
    high = dec.astype(BF).astype(F32)
    wmix = jnp.concatenate([w, high, dec - high], axis=0).astype(BF)
    wtok = wmix[:SPAN]
    bc = bc_r[...]
    bm, cm = bc[:, :STATE], bc[:, STATE:]
    ct = jnp.transpose(bc.astype(F32))[STATE:].astype(BF)
    square_r = lax.broadcasted_iota(jnp.int32, (SPAN, SPAN), 0)
    aff = jnp.where(square_r == lane, 0.0, dot_nt(cm, bm))

    squares = jnp.zeros((SPAN, 128), F32)
    for p in range(pairs):
        sl = slice(p * 128, (p + 1) * 128)
        efd = dot(wmix, e0[:, sl])
        ef = efd[:SPAN]
        eb = dot(wtok, e1[:, sl])
        dte = dot(wtok, e2[:, sl])
        exp_s[0, :, sl] = ef
        exp_s[1, :, sl] = eb
        decay = efd[SPAN : SPAN + 1] + efd[SPAN + 8 : SPAN + 9]
        exp_s[2, 0:8, sl] = jnp.broadcast_to(decay, (8, 128))
        sf = sf_s[:, sl] * first
        sfb = sf.astype(BF)
        sf_o[0, :, sl] = sfb
        sb = (sbl[0, :, sl].astype(F32) + pb[0, 0:1, sl] * sbd[:, sl].astype(F32)) * last
        sbb = sb.astype(BF)
        sb_o[0, :, sl] = sbb
        sf_s[:, sl] = sf * decay + ff[0, :, sl].astype(F32)
        xp = xpre[:, sl].astype(F32)
        x = xp * sigmoid(xp)
        xd = x * dte
        bd = jnp.concatenate(
            [jnp.where(low_half, xd, 0.0), jnp.where(low_half, 0.0, xd)], axis=0
        ).astype(BF)
        ms = []
        for h in (2 * p, 2 * p + 1):
            spread = jnp.minimum(
                col[:, h : h + 1] - row[h : h + 1, :],
                row[GROUP + h : GROUP + h + 1, :] - col[:, GROUP + h : GROUP + h + 1],
            )
            ms.append((aff * jnp.exp2(spread)).astype(BF))
        y = dot(jnp.concatenate(ms, axis=1), bd)
        y = y + ef * dot(cm, sfb) + eb * dot(cm, sbb) + skip[:, sl] * x
        y_s[:, sl] = y
        g = gate[:, sl].astype(F32)
        gated = y * (g * sigmoid(g))
        squares = squares + gated * gated

    gsc = lax.rsqrt(jnp.sum(squares, axis=1, keepdims=True) * (1.0 / width) + EPS)
    inner = jnp.zeros((SPAN, 128), F32)
    for p in range(pairs):
        sl = slice(p * 128, (p + 1) * 128)
        g = gate[:, sl].astype(F32)
        gunit = y_s[:, sl] * (g * sigmoid(g)) * gsc
        gnorm_o[:, sl] = (gunit * ggain[:, sl]).astype(BF)
        dgn = dgn_s[:, sl]
        dgu = dgn * gunit
        ggain_o[:, sl] += jnp.sum(dgu, axis=0, keepdims=True)
        inner = inner + dgu * ggain[:, sl]
    mean = jnp.sum(inner, axis=1, keepdims=True) * (1.0 / width)
    out_o[...] = (hid[...].astype(F32) + live * dot(gnorm_o[...], ow[...])).astype(BF)

    for p in range(pairs):
        sl = slice(p * 128, (p + 1) * 128)
        g = gate[:, sl].astype(F32)
        sg = sigmoid(g)
        act = g * sg
        y = y_s[:, sl]
        gunit = y * act * gsc
        dgated = gsc * (dgn_s[:, sl] * ggain[:, sl] - gunit * mean)
        dy = dgated * act
        dy_o[:, sl] = dy.astype(BF)
        dgate_o[:, sl] = (dgated * y * (sg * (1.0 + g * (1.0 - sg)))).astype(BF)
        xp = xpre[:, sl].astype(F32)
        skip_o[:, sl] += jnp.sum(dy * (xp * sigmoid(xp)), axis=0, keepdims=True)
        decay = exp_s[2, 0:1, sl]
        dff = dot(ct, (exp_s[0, :, sl] * dy).astype(BF))
        dfb = dot(ct, (exp_s[1, :, sl] * dy).astype(BF))
        dff_o[0, :, sl] = dff.astype(BF)
        q = q_s[0:1, sl]
        gf_s[:, sl] = gf_s[:, sl] + q * dff
        q_s[:, sl] = jnp.broadcast_to(q * decay * last, (8, 128))
        gb = gb_s[:, sl] * first
        pg = pg_s[0:1, sl] * first
        gbl_o[0, :, sl] = gb.astype(BF)
        pg_o[0, :, sl] = jnp.broadcast_to(pg, (8, 128))
        gb_s[:, sl] = gb * decay + dfb
        pg_s[:, sl] = jnp.broadcast_to(pg * decay, (8, 128))

    @pl.when(i == pl.num_programs(0) - 1)
    def _():
        gft_o[...] = gf_s[...]
        gbt_o[...] = gb_s[...]
        pgf_o[...] = q_s[...]
        pgb_o[...] = pg_s[...]


def mix(sc, gate, xpre, bc, col, row, ff, sbl, pb, sfd, sbd, hidden, out_grad, ow, owt, ggain, skip):
    tokens, width_in = hidden.shape
    width = gate.shape[1]
    blocks = tokens // SPAN
    e0, e1, e2, _ = expanders(width // HEAD_DIM)

    def ahead(shape):
        rank = len(shape)
        return pl.BlockSpec(shape, lambda i: (i,) + (0,) * (rank - 1))

    sds = jax.ShapeDtypeStruct
    state = (1, STATE, width)
    outs = [
        (sds((tokens, width_in), BF), ahead((SPAN, width_in))),
        (sds((tokens, width), BF), ahead((SPAN, width))),
        (sds((tokens, width), BF), ahead((SPAN, width))),
        (sds((tokens, width), BF), ahead((SPAN, width))),
        (sds((blocks, STATE, width), BF), ahead(state)),
        (sds((blocks, STATE, width), BF), ahead(state)),
        (sds((blocks, STATE, width), BF), ahead(state)),
        (sds((blocks, 8, width), F32), ahead((1, 8, width))),
        (sds((blocks, STATE, width), BF), ahead(state)),
        (sds((STATE, width), F32), full((STATE, width))),
        (sds((STATE, width), F32), full((STATE, width))),
        (sds((8, width), F32), full((8, width))),
        (sds((8, width), F32), full((8, width))),
        (sds((1, width), F32), full((1, width))),
        (sds((1, width), F32), full((1, width))),
    ]
    in_specs = [
        SMEM,
        ahead((SPAN, width)),
        ahead((SPAN, width)),
        ahead((SPAN, 128)),
        ahead((SPAN, 128)),
        ahead((SPAN, 128)),
        ahead(state),
        ahead(state),
        ahead((1, 8, width)),
        full((STATE, width)),
        full((STATE, width)),
        ahead((SPAN, width_in)),
        ahead((SPAN, width_in)),
        full(ow.shape),
        full(owt.shape),
        full(ggain.shape),
        full(skip.shape),
        full(e0.shape),
        full(e0.shape),
        full(e0.shape),
    ]
    return pl.pallas_call(
        mix_kernel,
        grid=(blocks,),
        in_specs=in_specs,
        out_specs=[spec for _, spec in outs],
        out_shape=[shape for shape, _ in outs],
        scratch_shapes=[
            pltpu.VMEM((STATE, width), F32),
            pltpu.VMEM((STATE, width), F32),
            pltpu.VMEM((STATE, width), F32),
            pltpu.VMEM((8, width), F32),
            pltpu.VMEM((8, width), F32),
            pltpu.VMEM((SPAN, width), F32),
            pltpu.VMEM((SPAN, width), F32),
            pltpu.VMEM((3, SPAN, width), F32),
        ],
        compiler_params=pltpu.CompilerParams(vmem_limit_bytes=58 * 1024 * 1024),
        name="mix",
    )(
        sc, gate, xpre, bc, col, row, ff, sbl, pb, sfd, sbd, hidden, out_grad, ow, owt, ggain, skip,
        jnp.asarray(e0, BF), jnp.asarray(e1, BF), jnp.asarray(e2, BF),
    )


def back_kernel(
    heads, sc, xpre, v_r, dy_r, bc_r, ps_r, pspre_r, col_r, row_r, sf_r, sb_r, gbl, pg, dff, gfd, gbd,
    skip, cv, cs, nad, e0, e1, e2, seg, tris, rect,
    dv_o, dst_o, dz_o, cvg_o, csg_o, head_o, edge_o, edges_o,
    gf_s, edge_s, edges_s, da_s,
):
    step = pl.program_id(0)
    blocks = pl.num_programs(0)
    i = blocks - 1 - step
    length = sc[1]
    place = sc[0] + i * SPAN
    last = jnp.where(lax.rem(place + SPAN, length) == 0, 0.0, 1.0)
    width = e0.shape[1]
    pairs = width // 128

    @pl.when(step == 0)
    def _():
        gf_s[...] = gfd[...].astype(F32)
        edge_s[...] = jnp.zeros_like(edge_s)
        edges_s[...] = jnp.zeros_like(edges_s)
        da_s[...] = jnp.zeros_like(da_s)
        cvg_o[...] = jnp.zeros_like(cvg_o)
        csg_o[...] = jnp.zeros_like(csg_o)
        head_o[...] = jnp.zeros_like(head_o)

    lane = lanes_of(SPAN)
    low_half = lane < HEAD_DIM
    col = col_r[...]
    row = row_r[...]
    end = jnp.broadcast_to(col[SPAN - 1 : SPAN], (8, 128))
    end1 = pltpu.roll(end, GROUP, 1)
    w = jnp.where(lane < 64, jnp.exp2(jnp.where(lane < 32, col, end1[0:1] - col)), col)
    dec = jnp.exp2(end)
    high = dec.astype(BF).astype(F32)
    wmix = jnp.concatenate([w, high, dec - high], axis=0).astype(BF)
    wtok = wmix[:SPAN]
    winn = jnp.exp2(jnp.where(lane < 32, end[0:1] - col, col)).astype(BF)
    bc = bc_r[...]
    bm, cm = bc[:, :STATE], bc[:, STATE:]
    square_r = lax.broadcasted_iota(jnp.int32, (SPAN, SPAN), 0)
    off = square_r != lane
    aff = jnp.where(off, dot_nt(bm, cm), 0.0)

    daff = jnp.zeros((SPAN, SPAN), F32)
    red = jnp.zeros((SPAN, 128), F32)
    ddt = jnp.zeros((SPAN, 128), F32)
    span_sum = jnp.zeros((8, 128), F32)
    dc = jnp.zeros((SPAN, STATE), F32)
    db = jnp.zeros((SPAN, STATE), F32)
    for p in range(pairs):
        sl = slice(p * 128, (p + 1) * 128)
        efd = dot(wmix, e0[:, sl])
        ef = efd[:SPAN]
        decay = efd[SPAN : SPAN + 1] + efd[SPAN + 8 : SPAN + 9]
        eb = dot(wtok, e1[:, sl])
        dte = dot(wtok, e2[:, sl])
        wf = dot(winn, e0[:, sl])
        wb = dot(winn, e1[:, sl])
        sf, sb = sf_r[0, :, sl], sb_r[0, :, sl]
        gf32 = gf_s[:, sl] * last
        gb32 = gbl[0, :, sl].astype(F32) + pg[0, 0:1, sl] * gbd[:, sl].astype(F32)
        gf, gb = gf32.astype(BF), gb32.astype(BF)
        gf_s[:, sl] = gf32 * decay + dff[0, :, sl].astype(F32)
        cross = (sf.astype(F32) * gf32 + sb.astype(F32) * gb32) * decay
        crossed = jnp.broadcast_to(jnp.sum(cross, axis=0, keepdims=True), (8, 128))
        span_sum = span_sum + dot(crossed.astype(BF), seg[4, sl, :])
        xp = xpre[:, sl].astype(F32)
        sg = sigmoid(xp)
        x = xp * sg
        xd = x * dte
        dy = dy_r[:, sl].astype(F32)
        efdy, ebdy = ef * dy, eb * dy
        wfxd, wbxd = wf * xd, wb * xd
        cf = wf * dot(bm, gf)
        cb = wb * dot(bm, gb)
        dc = dc + dot_nt(efdy.astype(BF), sf) + dot_nt(ebdy.astype(BF), sb)
        db = db + dot_nt(wfxd.astype(BF), gf) + dot_nt(wbxd.astype(BF), gb)
        red = red + dot((efdy * dot(cm, sf)).astype(BF), seg[0, sl, :])
        red = red + dot((ebdy * dot(cm, sb)).astype(BF), seg[1, sl, :])
        red = red + dot((xd * cf).astype(BF), seg[2, sl, :])
        red = red + dot((xd * cb).astype(BF), seg[3, sl, :])
        bd = jnp.concatenate(
            [jnp.where(low_half, dy, 0.0), jnp.where(low_half, 0.0, dy)], axis=0
        ).astype(BF)
        dm = dot_nt(xd.astype(BF), bd)
        ms = []
        for k in range(2):
            h = 2 * p + k
            spread = jnp.minimum(
                row[h : h + 1, :] - col[:, h : h + 1],
                col[:, GROUP + h : GROUP + h + 1] - row[GROUP + h : GROUP + h + 1, :],
            )
            f = jnp.exp2(spread)
            m = aff * f
            ms.append(m.astype(BF))
            dmh = dm[:, k * 128 : (k + 1) * 128]
            daff = daff + f * dmh
            sums = dot((m * dmh).astype(BF), rect[...])
            inside = jnp.where(
                square_r < lane, sums[:, :SPAN], jnp.where(off, sums[:, SPAN:], 0.0)
            )
            da_s[h : h + 1, :] = jnp.sum(inside, axis=0, keepdims=True)
        dxd = dot(jnp.concatenate(ms, axis=1), bd) + cf + cb
        ddt = ddt + dot((x * dxd).astype(BF), seg[4, sl, :])
        dx = dte * dxd + skip[:, sl] * dy
        dxp = dx * (sg * (1.0 + xp * (1.0 - sg)))
        ext = jnp.concatenate([dxp, edge_s[:, sl] * last], axis=0)
        edge_s[:, sl] = dxp[:8]
        v = v_r[:, sl].astype(F32)
        dv = jnp.zeros((SPAN, 128), F32)
        for j in range(TAPS):
            moved = shifted(ext, j, SPAN)
            k = TAPS - 1 - j
            dv = dv + moved * cv[k : k + 1, sl]
            cvg_o[k : k + 1, sl] += jnp.sum(v * moved, axis=0, keepdims=True)
        dv_o[:, sl] = dv.astype(BF)

    dafb = jnp.where(off, daff, 0.0).astype(BF)
    db = db + dot(dafb, cm)
    dc = dc + dot_tn(dafb, bm)
    dbc = jnp.concatenate([db, dc], axis=1)
    pp = pspre_r[...]
    sp = sigmoid(pp)
    dpp = dbc * (sp * (1.0 + pp * (1.0 - sp)))
    ext = jnp.concatenate([dpp, edges_s[...] * last], axis=0)
    edges_s[...] = dpp[:8]
    ps = ps_r[...]
    dst = jnp.zeros((SPAN, 128), F32)
    for j in range(TAPS):
        moved = shifted(ext, j, SPAN)
        k = TAPS - 1 - j
        dst = dst + moved * cs[k : k + 1, :]
        csg_o[k : k + 1, :] += jnp.sum(ps * moved, axis=0, keepdims=True)
    dst_o[...] = dst.astype(BF)

    hi = red.astype(BF)
    lo = (red - hi.astype(F32)).astype(BF)
    summed = dot(tris[...], hi) + dot(tris[...], lo)
    parts = [summed[g * SPAN : (g + 1) * SPAN] for g in range(4)]
    picked = jnp.where(
        lane < 32, parts[0], jnp.where(lane < 64, parts[1], jnp.where(lane < 96, parts[2], parts[3]))
    )
    picked = picked + jnp.transpose(da_s[...])
    total = picked + pltpu.roll(picked, 64, 1)
    total = total + pltpu.roll(total, 32, 1)
    da = total + span_sum[0:1]
    dz = (ddt + da * nad[...]) * col
    dz = jnp.where((lane >= 96) & (lane < 96 + heads), dz, 0.0)
    dz_o[...] = dz.astype(BF)
    head_o[0:1, :] += jnp.sum(da * col * nad[...], axis=0, keepdims=True)
    head_o[1:2, :] += jnp.sum(dz, axis=0, keepdims=True)

    @pl.when(i == 0)
    def _():
        edge_o[...] = edge_s[...]
        edges_o[...] = edges_s[...]


def back(
    heads, sc, xpre, v, dy, bc, ps, pspre, col, row, sf, sb, gbl, pg, dff, gfd, gbd, skip, cv, cs, nad
):
    tokens, width = xpre.shape
    blocks = tokens // SPAN
    maps = expanders(width // HEAD_DIM)
    every = sum(maps)
    seg = np.stack([m.T for m in maps] + [every.T])
    at = np.arange(SPAN)
    row_at, col_at = at[:, None], at[None, :]
    tris = np.concatenate(
        [col_at >= row_at, col_at <= row_at, col_at < row_at, col_at > row_at], axis=0
    ).astype(np.float32)
    rect = np.concatenate([row_at >= col_at, row_at <= col_at], axis=1).astype(np.float32)

    def rev(shape):
        rank = len(shape)
        return pl.BlockSpec(shape, lambda i: (blocks - 1 - i,) + (0,) * (rank - 1))

    sds = jax.ShapeDtypeStruct
    state = (1, STATE, width)
    outs = [
        (sds((tokens, width), BF), rev((SPAN, width))),
        (sds((tokens, 128), BF), rev((SPAN, 128))),
        (sds((tokens, 128), BF), rev((SPAN, 128))),
        (sds((TAPS, width), F32), full((TAPS, width))),
        (sds((TAPS, 128), F32), full((TAPS, 128))),
        (sds((8, 128), F32), full((8, 128))),
        (sds((8, width), F32), full((8, width))),
        (sds((8, 128), F32), full((8, 128))),
    ]
    in_specs = [
        SMEM,
        rev((SPAN, width)),
        rev((SPAN, width)),
        rev((SPAN, width)),
        rev((SPAN, 128)),
        rev((SPAN, 128)),
        rev((SPAN, 128)),
        rev((SPAN, 128)),
        rev((SPAN, 128)),
        rev(state),
        rev(state),
        rev(state),
        rev((1, 8, width)),
        rev(state),
        full((STATE, width)),
        full((STATE, width)),
        full(skip.shape),
        full(cv.shape),
        full(cs.shape),
        full(nad.shape),
        full((128, width)),
        full((128, width)),
        full((128, width)),
        full(seg.shape),
        full(tris.shape),
        full(rect.shape),
    ]
    return pl.pallas_call(
        functools.partial(back_kernel, heads),
        grid=(blocks,),
        in_specs=in_specs,
        out_specs=[spec for _, spec in outs],
        out_shape=[shape for shape, _ in outs],
        scratch_shapes=[
            pltpu.VMEM((STATE, width), F32),
            pltpu.VMEM((8, width), F32),
            pltpu.VMEM((8, 128), F32),
            pltpu.VMEM((128, 128), F32),
        ],
        compiler_params=pltpu.CompilerParams(vmem_limit_bytes=58 * 1024 * 1024),
        name="back",
    )(
        sc, xpre, v, dy, bc, ps, pspre, col, row, sf, sb, gbl, pg, dff, gfd, gbd, skip, cv, cs, nad,
        jnp.asarray(maps[0], BF), jnp.asarray(maps[1], BF), jnp.asarray(maps[2], BF),
        jnp.asarray(seg, BF), jnp.asarray(tris, BF), jnp.asarray(rect, BF),
    )


def spread_heads(v):
    padded = jnp.zeros((GROUP,), F32).at[: v.shape[0]].set(v)
    return jnp.tile(padded, 4)[None]


def handed(total, passed, shards, up):
    pairs = [(k, k + 1) if up else (k + 1, k) for k in range(shards - 1)]
    entering = lax.ppermute(total.astype(BF), "chan", pairs)
    for _ in range(shards - 2):
        now = total + passed[0:1] * entering.astype(F32)
        entering = lax.ppermute(now.astype(BF), "chan", pairs)
    return entering


def on_device(
    hidden_in, norm_gain, gate_value_weight, state_weight, step_weight, value_conv, state_conv,
    step_bias, decay_log, skip_gain, gate_gain, out_weight, seq_length, seq_count, out_grad,
):
    tokens, width_in = hidden_in.shape
    channel = lax.axis_index("chan")
    shards = lax.axis_size("chan")
    length, count = seq_length[0], seq_count[0]
    sc = jnp.stack([channel * tokens, length, count, 0]).astype(jnp.int32)
    local_heads = gate_value_weight.shape[1]
    local = local_heads * HEAD_DIM

    def gather(v, axis):
        return lax.all_gather(v, "chan", axis=axis, tiled=True)

    wg = gather(gate_value_weight[:, :, :HEAD_DIM].reshape(width_in, local), 1)
    wv = gather(gate_value_weight[:, :, HEAD_DIM:].reshape(width_in, local), 1)
    ow = gather(out_weight, 0)
    heads = local_heads * shards
    width = heads * HEAD_DIM
    small = jnp.concatenate(
        [value_conv.reshape(-1), gate_gain, step_bias, decay_log, skip_gain]
    )
    small = gather(small[None], 0)
    cuts = np.cumsum([TAPS * local, local, local_heads, local_heads])
    cv = small[:, : cuts[0]].reshape(shards, TAPS, local).transpose(1, 0, 2).reshape(TAPS, width)
    ggain = small[:, cuts[0] : cuts[1]].reshape(1, width)
    bias_all = small[:, cuts[1] : cuts[2]].reshape(heads)
    dlog_all = small[:, cuts[2] : cuts[3]].reshape(heads)
    skip_all = small[:, cuts[3] :].reshape(heads)
    wstep = gather(step_weight, 1)
    wst = jnp.tile(jnp.pad(wstep, ((0, 0), (0, GROUP - heads))), (1, 4))
    skip = jnp.repeat(skip_all, HEAD_DIM)[None]
    nad = -jnp.exp(dlog_all)
    gain = norm_gain[None]

    ups = [(k, k + 1) for k in range(shards - 1)]
    downs = [(k + 1, k) for k in range(shards - 1)]
    edge = lax.ppermute(hidden_in[tokens - PAD :], "chan", ups)

    (
        normed, gate, v, xpre, ps, pspre, bc, col, row, ff, sbl, pb, sft, sbt, pft, pbt, vh, psh,
    ) = project(
        sc, hidden_in, edge, gain, wg, wv, state_weight, wst, cv, state_conv,
        spread_heads(bias_all), spread_heads(nad * LOG2E),
    )
    sfd = handed(sft, pft, shards, True)
    sbd = handed(sbt, pbt, shards, False)
    (
        output, gnorm, dy, dgate, sf, sb, gbl, pg, dff, gft, gbt, pgf, pgb, ggain_grad, skip_grad,
    ) = mix(
        sc, gate, xpre, bc, col, row, ff, sbl, pb, sfd, sbd, hidden_in, out_grad, ow, ow.T, ggain, skip
    )
    gfd = handed(gft, pgf, shards, False)
    gbd = handed(gbt, pgb, shards, True)
    dv, dst, dz, cvg, csg, head_sums, edge_g, edges_g = back(
        heads, sc, xpre, v, dy, bc, ps, pspre, col, row, sf, sb, gbl, pg, dff, gfd, gbd, skip, cv,
        state_conv, spread_heads(nad),
    )

    joined = jnp.concatenate([edge_g, edges_g], axis=1)
    kernel = jnp.concatenate([cv, state_conv], axis=1)
    past = jnp.concatenate([vh, psh], axis=1)
    reach = TAPS - 1
    after = lax.ppermute(joined, "chan", downs)[:reach]
    after = after * jnp.where(((channel + 1) * tokens) % length == 0, 0.0, 1.0)
    patch = jnp.zeros((reach, joined.shape[1]), F32)
    taps = []
    for j in range(TAPS):
        moved = jnp.zeros_like(patch).at[reach - j :].set(after[:j]) if j else jnp.zeros_like(patch)
        patch = patch + moved * kernel[TAPS - 1 - j][None]
        own = joined[:j] * past[PAD - j :]
        taps.append(jnp.sum(own, axis=0))
    cross_taps = jnp.stack(taps[::-1])
    tail = jnp.pad(patch, ((PAD - reach, 0), (0, 0)))
    dv = dv.at[tokens - PAD :].add(tail[:, :width].astype(BF))
    dst = dst.at[tokens - PAD :].add(tail[:, width:].astype(BF))
    cvg = cvg + cross_taps[:, :width]
    csg = csg + cross_taps[:, width:]

    gl_scale = jnp.where(
        (channel * tokens + jnp.arange(tokens, dtype=jnp.int32)) // length < count, 1.0, 0.0
    )[:, None]
    gl = (out_grad * gl_scale.astype(BF)).astype(BF)
    ow_grad = dot_tn(gnorm, gl)
    dwg = dot_tn(normed, dgate)
    dwv = dot_tn(normed, dv)
    dws = dot_tn(normed, dst)
    dwst = dot_tn(normed, dz)[:, 96 : 96 + heads]
    wst_tail = jnp.pad(wstep, ((0, 0), (96, GROUP - heads)))
    dn = dot_nt(dgate, wg) + dot_nt(dv, wv) + dot_nt(dst, state_weight) + dot_nt(dz, wst_tail)
    u = hidden_in.astype(F32)
    scale = lax.rsqrt(jnp.mean(u * u, axis=1, keepdims=True) + EPS)
    unit = u * scale
    norm_gain_grad = jnp.sum(dn * unit, axis=0)
    du = dn * gain
    inner = jnp.mean(du * unit, axis=1, keepdims=True)
    input_grad = (out_grad.astype(F32) + scale * (du - unit * inner)).astype(BF)

    gvw = jnp.stack(
        [dwg.reshape(width_in, heads, HEAD_DIM), dwv.reshape(width_in, heads, HEAD_DIM)], axis=2
    ).reshape(width_in, heads, 2 * HEAD_DIM)
    gvw = lax.psum(
        lax.psum_scatter(gvw.astype(BF), "chan", scatter_dimension=1, tiled=True), "dp"
    ).astype(F32)
    owg = lax.psum(
        lax.psum_scatter(ow_grad.astype(BF), "chan", scatter_dimension=0, tiled=True), "dp"
    ).astype(F32)
    smalls = (
        norm_gain_grad, dws, dwst, cvg, csg, head_sums[1, 96 : 96 + heads],
        head_sums[0, 64 : 64 + heads], skip_grad.reshape(heads, HEAD_DIM).sum(axis=1), ggain_grad[0],
    )
    sizes = [int(np.prod(s.shape)) for s in smalls]
    flat = lax.psum(jnp.concatenate([s.reshape(-1) for s in smalls]), ("dp", "chan"))
    pieces, offset = [], 0
    for s, size in zip(smalls, sizes):
        pieces.append(flat[offset : offset + size].reshape(s.shape))
        offset += size
    ngg, dws, dwst, cvg, csg, sbg, dlg, skg, ggg = pieces

    def mine(v, count_local, axis):
        return lax.dynamic_slice_in_dim(v, channel * count_local, count_local, axis)

    return (
        output,
        input_grad,
        ngg,
        gvw,
        dws,
        mine(dwst, local_heads, 1),
        mine(cvg, local, 1),
        csg,
        mine(sbg, local_heads, 0),
        mine(dlg, local_heads, 0),
        mine(skg, local_heads, 0),
        mine(ggg, local, 0),
        owg,
    )


def solution(mesh):
    in_specs = (
        P(("dp", "chan"), None),
        P(),
        P(None, "chan", None),
        P(),
        P(None, "chan"),
        P(None, "chan"),
        P(),
        P("chan"),
        P("chan"),
        P("chan"),
        P("chan"),
        P("chan", None),
        P("dp"),
        P("dp"),
        P(("dp", "chan"), None),
    )
    out_specs = (
        P(("dp", "chan"), None),
        P(("dp", "chan"), None),
        P(),
        P(None, "chan", None),
        P(),
        P(None, "chan"),
        P(None, "chan"),
        P(),
        P("chan"),
        P("chan"),
        P("chan"),
        P("chan"),
        P("chan", None),
    )
    return jax.shard_map(
        on_device, mesh=mesh, in_specs=in_specs, out_specs=out_specs, check_vma=False
    )
```

time: 2430 us -> 747 us (0.31)
  other arithmetic: 805 us -> 21.9 us
  matrix products: 711 us -> 57.9 us
  local copies, waits for them, and re-layouts: 614 us -> 73 us
  Pallas kernels: 0 us -> 258 us
  waiting for transfers between devices: 175 us -> 283 us
  blocking collectives: 79.6 us -> 10.9 us
    dot_general x29 -> x8, matrix products: 680 us -> 54.7 us  [the longest x4 31.7 us: dot_tn(): lax.dot_general(a, b, (((0,), (0,)), ((), ())), preferred_element_type=F32)]
    pallas_call x0 -> x3, Pallas kernels: none -> 258 us  [the longest x1 133 us: back(): pl.pallas_call(functools.partial(back_kernel, heads), grid=(blocks,), in_...]
    dynamic_update_slice x192 -> x0, other arithmetic: 243 us -> none  [direction_pass(): lax.scan(carry_fn, zero_state, (fresh, block_decay, reset_flags), reverse...]
    reduce_sum x74 -> x4, other arithmetic: 241 us -> 1.37 us  [the longest x1 0.68 us: on_device(): scale = lax.rsqrt(jnp.mean(u * u, axis=1, keepdims=True) + EPS)]
    add x64 -> x2, other arithmetic: 166 us -> 0.05 us  [the longest x1 0.04 us: on_device(): patch = patch + moved * kernel[TAPS - 1 - j][None]]
    psum x2, waiting for transfers between devices: 85.9 us -> 224 us  [the longest x1 127 us: on_device(): lax.psum(jnp.concatenate([s.reshape(-1) for s in smalls]), ('dp', 'chan'))]
    mul x135 -> x0, local copies, waits for them, and re-layouts: 114 us -> none  [the longest x128 84.1 us: carry_fn(): return (decay_block[:, None, None] * state_in + fresh_block, state_in)]
    dynamic_slice x192 -> x6, local copies, waits for them, and re-layouts: 113 us -> 3.18 us  [mine(): return lax.dynamic_slice_in_dim(v, channel * count_local, count_local, axis)]
  transfers between devices with their start and end apart: 6 -> 13, of which waited for: 3 -> 6; matrix products, arithmetic and copies ran while one was open for 50% -> 18% of each run, Pallas kernels for 0% -> 25%
where the time goes in v1:
time: 747 us; the launch traced here: 737 us
  waiting for transfers between devices  283 us (38%)
  Pallas kernels  258 us (35%)
  local copies, waits for them, and re-layouts  73 us (10%)
  matrix products  57.9 us (8%)
  other arithmetic  21.9 us (3%)
  between operations  17.1 us (2%)
  starting transfers between devices  15.4 us (2%)
  blocking collectives  10.9 us (1%)
    pallas_call x1, Pallas kernels, back(): pl.pallas_call(functools.partial(back_kernel, heads), grid=(blocks,), in_...  133 us
    psum x1, waiting for transfers between devices, on_device(): lax.psum(jnp.concatenate([s.reshape(-1) for s in smalls]), ('dp', 'chan'))  127 us
    psum x1, waiting for transfers between devices, on_device(): lax.psum(lax.psum_scatter(gvw.astype(BF), 'chan', scatter_dimension=1, ti...  97 us
    pallas_call x1, Pallas kernels, mix(): pl.pallas_call(mix_kernel, grid=(blocks,), in_specs=in_specs, out_specs=[...  75.5 us
    pallas_call x1, Pallas kernels, project(): pl.pallas_call(functools.partial(project_kernel, tile, chunk), grid=(tile...  48.9 us
    all_gather x3, waiting for transfers between devices, gather(): return lax.all_gather(v, 'chan', axis=axis, tiled=True)  48.6 us
    dot_general x4, matrix products, dot_tn(): lax.dot_general(a, b, (((0,), (0,)), ((), ())), preferred_element_type=F32)  31.7 us
    dot_general x4, matrix products, dot_nt(): lax.dot_general(a, b, (((1,), (1,)), ((), ())), preferred_element_type=F32)  22.9 us
  transfers between devices with their start and end apart: 13, of which 6 were waited for; matrix products, arithmetic and copies ran while one was open for 18% of the time, Pallas kernels for 25%

profile of v1, /device:TPU:1, one launch (start us, length us, event | category | flops | bytes accessed | tf_op | source)
XLA Modules:
  0.0 737.3 jit_solution(14472170309649534149)
XLA Ops:
  7.2 4.7 fusion.29
  21.1 3.9 collective-permute-start
  28.1 6.6 all-reduce.8
  37.7 4.2 all-gather.1
  45.4 10.3 %all-gather.6.cloned.1.call-done.wg = bf16[768,1536]{1,0:T(8,128)(2,1)} async-done(((bf16[768,768]{1,0:T(8,128)(2,1)}), bf16[768,1536]{1,0:T(8,128)(2,1)}) %all-gather.6.cloned.1.call-update) | async-done | bytes 2359312 | tf_op jit(solution)/shard_map/all_gather | solution.py:718
  55.7 38.2 %all-gather.8.cloned.1.call-done.wv = bf16[768,1536]{1,0:T(8,128)(2,1)} async-done(((bf16[768,768]{1,0:T(8,128)(2,1)}), bf16[768,1536]{1,0:T(8,128)(2,1)}) %all-gather.8.cloned.1.call-update) | async-done | bytes 2359312 | tf_op jit(solution)/shard_map/all_gather | solution.py:718
  93.9 48.9 %project.1 = (bf16[2048,768]{1,0:T(8,128)(2,1)}, bf16[2048,1536]{1,0:T(8,128)(2,1)}, bf16[2048,1536]{1,0:T(8,128)(2,1)}, bf16[2048,1536]{1,0:T(8,128)(2,1)}, f32...) custom-call(s32[4]{0:T(128)} %pad_add_fusion.sc, ...), custom_call_target="tpu_custom_call" | custom-call | tf_op jit(solution)/shard_map/project/pallas_call | solution.py:224
  148.9 4.3 copy.68.ow
  155.3 75.5 %mix.1 = (bf16[2048,768]{1,0:T(8,128)(2,1)}, bf16[2048,1536]{1,0:T(8,128)(2,1)}, bf16[2048,1536]{1,0:T(8,128)(2,1)}, bf16[2048,1536]{1,0:T(8,128)(2,1)}, bf16[16...) custom-call(s32[4]{0:T(128)} %pad_add_fusion.sc, ...), custom_call_target="tpu_custom_call" | custom-call | tf_op jit(solution)/shard_map/mix/pallas_call | solution.py:429
  234.1 4.0 collective-permute-start.4
  238.1 10.4 %convolution_convert_fusion = bf16[1536,768]{1,0:T(8,128)(2,1)} fusion(bf16[2048,1536]{1,0:T(8,128)(2,1)} %get-tuple-element.190, bf16[2048,768]{1,0:T(8,128)(2,1)S(1)} %copy-done.1, bf16[2048]{0:T(1024)(128)(2,1)S(1)} %select_convert_fusion), kind=kOutput, calls=%fused_computation.15 | convolution fusion | flops 4834590720 | bytes 11800576 | tf_op jit(solution)/shard_map/dot_general | solution.py:32
  250.2 133.4 %back.1 = (bf16[2048,1536]{1,0:T(8,128)(2,1)}, bf16[2048,128]{1,0:T(8,128)(2,1)}, bf16[2048,128]{1,0:T(8,128)(2,1)}, f32[4,1536]{1,0:T(4,128)}, f32[4,128]{1,0:T...) custom-call(s32[4]{0:T(128)} %pad_add_fusion.sc, bf16[2048,1536]{1,0:T(8,128)(2,1)} %get-tuple-element.155.xpre, ...), custom_call_target="tpu_custom_call" | custom-call | tf_op jit(solution)/shard_map/back/pallas_call | solution.py:670
  386.6 9.1 %convolution_convert_fusion.2 = bf16[768,1536]{1,0:T(8,128)(2,1)} fusion(bf16[2048,768]{1,0:T(8,128)(2,1)S(1)} %copy-done.3, bf16[2048,1536]{1,0:T(8,128)(2,1)} %get-tuple-element.165), kind=kOutput, calls=%fused_computation.17 | convolution fusion | flops 4833017856 | bytes 11796480 | tf_op jit(solution)/shard_map/dot_general | solution.py:32
  400.1 9.2 %convolution_convert_fusion.1 = bf16[768,1536]{1,0:T(8,128)(2,1)} fusion(bf16[2048,768]{1,0:T(8,128)(2,1)} %get-tuple-element.182, bf16[2048,1536]{1,0:T(8,128)(2,1)} %fusion.18), kind=kOutput, calls=%fused_computation.16 | convolution fusion | flops 4833017856 | bytes 11796480 | tf_op jit(solution)/shard_map/dot_general | solution.py:32
  409.3 4.3 copy.71
  423.0 9.6 %fusion.32 = f32[2048,768]{1,0:T(8,128)} fusion(bf16[2048,1536]{1,0:T(8,128)(2,1)} %get-tuple-element.165, bf16[768,1536]{1,0:T(8,128)(2,1)} %all-gather.6.cloned.1.call-done.wg), kind=kOutput, calls=%fused_computation.76 | convolution fusion | flops 4831838208 | bytes 14942208 | tf_op jit(solution)/shard_map/dot_general | solution.py:28
  446.9 7.4 %fusion.33 = f32[2048,768]{1,0:T(8,128)S(1)} fusion(bf16[2048,1536]{1,0:T(8,128)(2,1)} %fusion.18, bf16[768,1536]{1,0:T(8,128)(2,1)S(1)} %copy-done.4), kind=kOutput, calls=%fused_computation.77 | convolution fusion | flops 4831838208 | bytes 14942208 | tf_op jit(solution)/shard_map/dot_general | solution.py:28
  454.4 4.9 fusion.8
  459.3 12.9 %concatenate.36 = f32[125768]{0:T(1024)} concatenate(f32[768]{0:T(1024)S(1)} %get-tuple-element.217, f32[98304]{0:T(1024)S(1)} %convolution_bitcast_fusion, f32[18432]{0:T(1024)} %reshape.321, f32[6144]{0:T(1024)} %reshape.322, f32[512]{0:T(512)} %fusion.26, f32[24]{0:T(128)} %get-tuple-element.234, f32[24]{0:T(128)} %get-tuple-element.233, f32[24]{0:T(128)} %reduce_sum.63, ...), dimensions={0} | concatenate | bytes 1006144 | tf_op jit(solution)/shard_map/concatenate | solution.py:818
  472.9 9.4 %reduce-scatter.3.cloned.1.call-done = bf16[768,12,128]{0,2,1:T(8,128)(2,1)} async-done(((bf16[768,24,128]{0,2,1:T(8,128)(2,1)}), bf16[768,12,128]{0,2,1:T(8,128)(2,1)}) %reduce-scatter.3.cloned.1.call-update) | async-done | bytes 2359312 | tf_op jit(solution)/shard_map/reduce_scatter | solution.py:808
  482.4 5.9 fusion.7
  488.2 126.9 %all-reduce.13.cloned.1.call-done = f32[125768]{0:T(1024)} async-done(((f32[125768]{0:T(1024)}), f32[125768]{0:T(1024)}) %all-reduce.13.cloned.1.call-update) | async-done | bytes 503088 | tf_op jit(solution)/shard_map/psum | solution.py:818
  627.0 97.0 %all-reduce.15.cloned.1.call-done = (bf16[768,12,128]{0,2,1:T(8,128)(2,1)}, bf16[768,768]{1,0:T(8,128)(2,1)}) async-done(((bf16[768,12,128]{0,2,1:T(8,128)(2,1)}, bf16[768,768]{1,0:T(8,128)(2,1)}), (bf16[768,12,128]{0,2,1:T(8,128)(2,1)}, bf16[768,768]{1,0:T(8,128)(2,1)})) %all-reduce.15.cloned.1.call-update) | async-done | bytes 3538960 | tf_op jit(solution)/shard_map/psum | solution.py:807
  724.0 4.6 copy.73
  (204 shorter events, 74.5 us)
Async XLA Ops:
  7.2 48.5 %all-gather.6.cloned.1.call-start = ((), (), s32[]{:S(2)}) async-start(), calls=%async_computation.2 | async-start | bytes 3538944 | tf_op jit(solution)/shard_map/all_gather | solution.py:718
  16.2 77.8 %all-gather.8.cloned.1.call-start = ((), (), s32[]{:S(2)}) async-start(), calls=%async_computation.3 | async-start | bytes 3538944 | tf_op jit(solution)/shard_map/all_gather | solution.py:718
  17.3 10.4 %copy-start.32 = (f32[768]{0:T(1024)S(1)}, f32[768]{0:T(1024)}, u32[]{:S(2)}) copy-start(f32[768]{0:T(1024)} %param.55) | copy-start | bytes 9220
  17.3 10.4 %copy-start.33 = (f32[12]{0:T(128)S(1)}, f32[12]{0:T(128)}, u32[]{:S(2)}) copy-start(f32[12]{0:T(128)} %param.52) | copy-start | bytes 148
  17.3 10.4 %copy-start.34 = (f32[12]{0:T(128)S(1)}, f32[12]{0:T(128)}, u32[]{:S(2)}) copy-start(f32[12]{0:T(128)} %param.53) | copy-start | bytes 148
  17.3 10.4 %copy-start.35 = (f32[12]{0:T(128)S(1)}, f32[12]{0:T(128)}, u32[]{:S(2)}) copy-start(f32[12]{0:T(128)} %param.54) | copy-start | bytes 148
  18.8 18.9 %copy-start.25 = (bf16[768,12]{0,1:T(8,128)(2,1)S(1)}, bf16[768,12]{0,1:T(8,128)(2,1)}, u32[]{:S(2)}) copy-start(bf16[768,12]{0,1:T(8,128)(2,1)} %param.49) | copy-start | bytes 55300
  18.8 24.6 %copy-start.22 = (f32[768]{0:T(1024)S(1)}, f32[768]{0:T(1024)}, u32[]{:S(2)}) copy-start(f32[768]{0:T(1024)} %param.46) | copy-start | bytes 9220
  18.8 130.1 %all-gather.10.cloned.1.call-start = ((), (), s32[]{:S(2)}) async-start(), calls=%async_computation.4 | async-start | bytes 3538944 | tf_op jit(solution)/shard_map/all_gather | solution.py:718
  20.3 452.6 %reduce-scatter.5.cloned.1.call-start = ((), (), s32[]{:S(2)}) async-start(), calls=%async_computation.7 | async-start | bytes 3538944 | tf_op jit(solution)/shard_map/reduce_scatter | solution.py:811
  21.1 24.3 %collective-permute-start = (bf16[16,768]{1,0:T(8,128)(2,1)S(1)}, bf16[16,768]{1,0:T(8,128)(2,1)S(1)}, u32[]{:S(2)}, u32[]{:S(2)}) collective-permute-start(bf16[16,768]{1,0:T(8,128)(2,1)S(1)} %slice.230), channel_id=1, source_target_pairs={{0,1},{2,3},{4,5},{6,7},{8,9},{10,11},{12,13},{14,15},{16,17},{18,... | collective-permute-start | bytes 73736 | tf_op jit(solution)/shard_map/ppermute | solution.py:743
  45.4 48.6 %copy-start.24 = (bf16[16,768]{1,0:T(8,128)(2,1)}, bf16[16,768]{1,0:T(8,128)(2,1)S(1)}, u32[]{:S(2)}) copy-start(bf16[16,768]{1,0:T(8,128)(2,1)S(1)} %collective-permute-done.edge) | copy-start | bytes 73732
  93.9 54.9 %copy-start.9 = (f32[1,4,2,768]{3,1,2,0:T(4,128)S(1)}, f32[1,4,2,768]{3,1,2,0:T(4,128)}, u32[]{:S(2)}) copy-start(f32[1,4,2,768]{3,1,2,0:T(4,128)} %copy.77) | copy-start | bytes 73732
  143.9 9.3 %collective-permute-start.1 = (bf16[64,1536]{1,0:T(8,128)(2,1)S(1)}, bf16[64,1536]{1,0:T(8,128)(2,1)S(1)}, u32[]{:S(2)}, u32[]{:S(2)}) collective-permute-start(bf16[64,1536]{1,0:T(8,128)(2,1)S(1)} %convert_element_type.50), channel_id=1, source_target_pairs={{0,1},{2,3},{4,5},{6,7},{8,9},{10,11},{12,13},{14,15},{16,17},{18,... | collective-permute-start | bytes 589832 | tf_op jit(solution)/shard_map/ppermute | solution.py:698
  147.0 7.5 %collective-permute-start.2 = (bf16[64,1536]{1,0:T(8,128)(2,1)S(1)}, bf16[64,1536]{1,0:T(8,128)(2,1)S(1)}, u32[]{:S(2)}, u32[]{:S(2)}) collective-permute-start(bf16[64,1536]{1,0:T(8,128)(2,1)S(1)} %convert_element_type.51), channel_id=1, source_target_pairs={{1,0},{3,2},{5,4},{7,6},{9,8},{11,10},{13,12},{15,14},{17,16},{19,... | collective-permute-start | bytes 589832 | tf_op jit(solution)/shard_map/ppermute | solution.py:698
  155.3 82.9 %copy-start.1 = (bf16[2048,768]{1,0:T(8,128)(2,1)S(1)}, bf16[2048,768]{1,0:T(8,128)(2,1)}, u32[]{:S(2)}) copy-start(bf16[2048,768]{1,0:T(8,128)(2,1)} %gout.1) | copy-start | bytes 9437188
  231.8 17.7 %collective-permute-start.3 = (bf16[64,1536]{1,0:T(8,128)(2,1)S(1)}, bf16[64,1536]{1,0:T(8,128)(2,1)S(1)}, u32[]{:S(2)}, u32[]{:S(2)}) collective-permute-start(bf16[64,1536]{1,0:T(8,128)(2,1)S(1)} %convert_element_type.54), channel_id=1, source_target_pairs={{1,0},{3,2},{5,4},{7,6},{9,8},{11,10},{13,12},{15,14},{17,16},{19,... | collective-permute-start | bytes 589832 | tf_op jit(solution)/shard_map/ppermute | solution.py:698
  234.1 15.4 %collective-permute-start.4 = (bf16[64,1536]{1,0:T(8,128)(2,1)S(1)}, bf16[64,1536]{1,0:T(8,128)(2,1)S(1)}, u32[]{:S(2)}, u32[]{:S(2)}) collective-permute-start(bf16[64,1536]{1,0:T(8,128)(2,1)S(1)} %convert_element_type.55), channel_id=1, source_target_pairs={{0,1},{2,3},{4,5},{6,7},{8,9},{10,11},{12,13},{14,15},{16,17},{18,... | collective-permute-start | bytes 589832 | tf_op jit(solution)/shard_map/ppermute | solution.py:698
  238.1 10.6 %copy-start.27 = (f32[4,128]{1,0:T(4,128)S(1)}, f32[4,128]{1,0:T(4,128)}, u32[]{:S(2)}) copy-start(f32[4,128]{1,0:T(4,128)} %cs.3) | copy-start | bytes 6148
  248.5 233.8 %reduce-scatter.3.cloned.1.call-start = ((), (), s32[]{:S(2)}) async-start(), calls=%async_computation.6 | async-start | bytes 7077888 | tf_op jit(solution)/shard_map/reduce_scatter | solution.py:808
  250.2 136.4 %copy-start.3 = (bf16[2048,768]{1,0:T(8,128)(2,1)S(1)}, bf16[2048,768]{1,0:T(8,128)(2,1)}, u32[]{:S(2)}) copy-start(bf16[2048,768]{1,0:T(8,128)(2,1)} %get-tuple-element.182) | copy-start | bytes 9437188
  385.1 13.5 %collective-permute-start.5 = (f32[8,1664]{1,0:T(8,128)S(1)}, f32[8,1664]{1,0:T(8,128)S(1)}, u32[]{:S(2)}, u32[]{:S(2)}) collective-permute-start(f32[8,1664]{1,0:T(8,128)S(1)} %constant_dynamic-update-slice_fusion.2), channel_id=1, source_target_pairs={{1,0},{3,2},{5,4},{7,6},{9,8},{11,10},{13,12},{15,14},{17,16},{19,... | collective-permute-start | bytes 159752 | tf_op jit(solution)/shard_map/ppermute | solution.py:769
  418.5 196.6 %all-reduce.13.cloned.1.call-start = ((), (), s32[]{:S(2)}) async-start(), calls=%async_computation.5 | async-start | bytes 1007616 | tf_op jit(solution)/shard_map/psum | solution.py:818
  472.2 251.8 %all-reduce.15.cloned.1.call-start = ((), (), s32[]{:S(2)}) async-start(), calls=%async_computation.8 | async-start | bytes 7077888 | tf_op jit(solution)/shard_map/psum | solution.py:807
  (28 other events, 117.3 us)
Sparse Core Ops, SparseCore 0:
  16.3 39.3 all-gather.5
  57.8 36.0 all-gather.7
  96.1 36.1 all-gather.9
  248.6 36.3 reduce-scatter.4
  418.6 63.7 reduce-scatter.2
  488.1 126.9 all-reduce.12
  619.3 104.6 all-reduce.14

commit v2 on v1

--- a/solution.py
+++ b/solution.py
@@ -32,6 +32,12 @@
     return lax.dot_general(a, b, (((0,), (0,)), ((), ())), preferred_element_type=F32)
 
 
+def fine_nt(a, b):
+    return lax.dot_general(
+        a, b, (((1,), (1,)), ((), ())), precision=lax.Precision.HIGHEST, preferred_element_type=F32
+    )
+
+
 def sigmoid(v):
     return 0.5 + 0.5 * jnp.tanh(0.5 * v)
 
@@ -58,12 +64,24 @@
     return [np.asarray(lane == GROUP * g + channel[None], np.float32) for g in range(4)]
 
 
-def project_kernel(
-    tile, chunk, sc, hid, halo, edge, gain, wg, wv, ws, wst, cv, cs, bias, nal, tri, e0, e1,
-    normed_o, gate_o, v_o, xpre_o, ps_o, pspre_o, bc_o, col_o, row_o, ff_o, sb_o, pb_o,
-    sft_o, sbt_o, pft_o, pbt_o, vh_o, psh_o,
-    sb_s, pb_s, sf_s, pf_s,
-):
+def project_kernel(fresh, final, tile, chunk, *refs):
+    refs = list(refs)
+
+    def take(count):
+        return [refs.pop(0) for _ in range(count)]
+
+    sc, tokens_r, halo, edge, wg, wv, wst, cv, bias, nal, tri, e0, e1 = take(13)
+    if fresh:
+        gain, ws, cs = take(3)
+    else:
+        (bc_r,) = take(1)
+    gate_o, v_o, xpre_o, ff_o, sb_o, pb_o, sft_o, sbt_o, pft_o, pbt_o, hand_o, vh_o = take(12)
+    if fresh:
+        normed_o, nedge_o, ps_o, pspre_o, bc_o, psh_o = take(6)
+    if final:
+        col_o, row_o = take(2)
+    sb_s, pb_s, sf_s, pf_s = take(4)
+
     step = pl.program_id(0)
     tiles = pl.num_programs(0)
     at = tiles - 1 - step
@@ -80,38 +98,53 @@
         pf_s[...] = jnp.ones_like(pf_s)
 
     before = jnp.where(at == 0, edge[...].astype(F32), halo[...].astype(F32))
-    rows = jnp.concatenate([before, hid[...].astype(F32)], axis=0)
-    scale = lax.rsqrt(jnp.mean(rows * rows, axis=1, keepdims=True) + EPS)
-    normed = (rows * scale * gain[...]).astype(BF)
-    own = normed[PAD:]
-    normed_o[...] = own
+    rows = jnp.concatenate([before, tokens_r[...].astype(F32)], axis=0)
     keep = jnp.where(lax.rem(start, length) == 0, 0.0, 1.0)
     row_id = lax.broadcasted_iota(jnp.int32, (tile + PAD, 1), 0)
     keep_rows = jnp.where(row_id < PAD, keep, 1.0)
-
-    ps = dot(normed, ws[...]) * keep_rows
-    ps_o[...] = ps[PAD:]
-    pspre = ps[PAD:] * cs[TAPS - 1 : TAPS]
-    for j in range(1, TAPS):
-        pspre = pspre + shifted(ps, PAD - j, tile) * cs[TAPS - 1 - j : TAPS - j]
-    pspre_o[...] = pspre
-    bc = pspre * sigmoid(pspre)
-    bc_o[...] = bc.astype(BF)
+    if fresh:
+        scale = lax.rsqrt(jnp.mean(rows * rows, axis=1, keepdims=True) + EPS)
+        normed = (rows * scale * gain[...]).astype(BF)
+        own = normed[PAD:]
+        normed_o[...] = own
+
+        ps = dot(normed, ws[...]) * keep_rows
+        ps_o[...] = ps[PAD:]
+        pspre = ps[PAD:] * cs[TAPS - 1 : TAPS]
+        for j in range(1, TAPS):
+            pspre = pspre + shifted(ps, PAD - j, tile) * cs[TAPS - 1 - j : TAPS - j]
+        pspre_o[...] = pspre
+        bc = pspre * sigmoid(pspre)
+        bc_o[...] = bc
+
+        @pl.when(at == 0)
+        def _():
+            nedge_o[...] = normed[:PAD]
+            psh_o[...] = ps[:PAD]
+
+    else:
+        normed = rows.astype(BF)
+        own = tokens_r[...]
+        bc = bc_r[...]
 
     z = dot(own, wst[...]) + bias[...]
     dt = jnp.maximum(z, 0.0) + jnp.log1p(jnp.exp(-jnp.abs(z)))
-    sig = sigmoid(z)
     a2 = dt * nal[...]
     lane = lanes_of(SPAN)
-    firsts, wmix, bts = [], [], []
+    if final:
+        sig = sigmoid(z)
+    wmix, bts = [], []
     for b in range(blocks):
         sl = slice(b * SPAN, (b + 1) * SPAN)
         ab = a2[sl]
         ca = jnp.dot(tri[...], ab, precision=lax.Precision.HIGHEST, preferred_element_type=F32)
         ce = ca - ab
-        col = jnp.where(lane < 32, ca, jnp.where(lane < 64, ce, jnp.where(lane < 96, dt[sl], sig[sl])))
-        col_o[sl, :] = col
-        row_o[sl, :] = jnp.transpose(col)
+        if final:
+            col = jnp.where(
+                lane < 32, ca, jnp.where(lane < 64, ce, jnp.where(lane < 96, dt[sl], sig[sl]))
+            )
+            col_o[sl, :] = col
+            row_o[sl, :] = jnp.transpose(col)
         end = ca[SPAN - 1 : SPAN]
         w = jnp.exp2(jnp.where(lane < 32, end - ca, ce)) * dt[sl]
         dec = jnp.broadcast_to(jnp.exp2(end), (8, 128))
@@ -158,23 +191,22 @@
 
     @pl.when(at == 0)
     def _():
-        psh_o[...] = ps[:PAD]
         sft_o[...] = sf_s[...]
         sbt_o[...] = sb_s[...]
         pft_o[...] = pf_s[...]
         pbt_o[...] = pb_s[...]
-
-
-def project(sc, hidden, edge, gain, wg, wv, ws, wst, cv, cs, bias, nal):
-    tokens, width_in = hidden.shape
+        hand_o[...] = jnp.where(sc[0] == 0, sf_s[...], sb_s[...]).astype(BF)
+
+
+def project(sc, source, edge, wg, wv, wst, cv, bias, nal, e0, e1, maps=None, bc=None, final=True):
+    fresh = maps is not None
+    tokens, width_in = source.shape
     width = wg.shape[1]
-    heads = width // HEAD_DIM
     tile = min(256, tokens)
     tiles = tokens // tile
     per = tile // SPAN
     blocks = tokens // SPAN
     chunk = 256 if width % 256 == 0 else 128
-    e0, e1, _, _ = expanders(heads)
     tri = np.tril(np.ones((SPAN, SPAN), np.float32))
 
     def back(shape):
@@ -182,47 +214,40 @@
         return pl.BlockSpec(shape, lambda i: (tiles - 1 - i,) + (0,) * (rank - 1))
 
     sds = jax.ShapeDtypeStruct
-    outs = [
-        (sds((tokens, width_in), BF), back((tile, width_in))),
-        (sds((tokens, width), BF), back((tile, width))),
-        (sds((tokens, width), BF), back((tile, width))),
-        (sds((tokens, width), BF), back((tile, width))),
-        (sds((tokens, 128), F32), back((tile, 128))),
-        (sds((tokens, 128), F32), back((tile, 128))),
-        (sds((tokens, 128), BF), back((tile, 128))),
-        (sds((tokens, 128), F32), back((tile, 128))),
-        (sds((tokens, 128), F32), back((tile, 128))),
-        (sds((blocks, STATE, width), BF), back((per, STATE, width))),
-        (sds((blocks, STATE, width), BF), back((per, STATE, width))),
-        (sds((blocks, 8, width), F32), back((per, 8, width))),
-        (sds((STATE, width), F32), full((STATE, width))),
-        (sds((STATE, width), F32), full((STATE, width))),
-        (sds((8, width), F32), full((8, width))),
-        (sds((8, width), F32), full((8, width))),
-        (sds((PAD, width), F32), full((PAD, width))),
-        (sds((PAD, 128), F32), full((PAD, 128))),
-    ]
+    wide = (sds((tokens, width), BF), back((tile, width)))
+    narrow = (sds((tokens, 128), F32), back((tile, 128)))
+    held = (sds((blocks, STATE, width), BF), back((per, STATE, width)))
+    total = (sds((STATE, width), F32), full((STATE, width)))
+    passed = (sds((8, width), F32), full((8, width)))
+    outs = [wide, wide, wide, held, held, (sds((blocks, 8, width), F32), back((per, 8, width)))]
+    outs += [total, total, passed, passed, (sds((STATE, width), BF), full((STATE, width)))]
+    outs += [(sds((PAD, width), F32), full((PAD, width)))]
+    if fresh:
+        outs += [
+            (sds((tokens, width_in), BF), back((tile, width_in))),
+            (sds((PAD, width_in), BF), full((PAD, width_in))),
+            narrow,
+            narrow,
+            narrow,
+            (sds((PAD, 128), F32), full((PAD, 128))),
+        ]
+    if final:
+        outs += [narrow, narrow]
     steps = tile // PAD
+    args = [sc, source, source, edge, wg, wv, wst, cv, bias, nal, tri, e0, e1]
     in_specs = [
         SMEM,
         back((tile, width_in)),
         pl.BlockSpec((PAD, width_in), lambda i: (jnp.maximum((tiles - 1 - i) * steps - 1, 0), 0)),
-        full((PAD, width_in)),
-        full(gain.shape),
-        full(wg.shape),
-        full(wv.shape),
-        full(ws.shape),
-        full(wst.shape),
-        full(cv.shape),
-        full(cs.shape),
-        full(bias.shape),
-        full(nal.shape),
-        full(tri.shape),
-        full(e0.shape),
-        full(e1.shape),
-    ]
+    ] + [full(a.shape) for a in args[3:]]
+    if fresh:
+        args += list(maps)
+        in_specs += [full(a.shape) for a in maps]
+    else:
+        args += [bc]
+        in_specs += [back((tile, 128))]
     return pl.pallas_call(
-        functools.partial(project_kernel, tile, chunk),
+        functools.partial(project_kernel, fresh, final, tile, chunk),
         grid=(tiles,),
         in_specs=in_specs,
         out_specs=[spec for _, spec in outs],
@@ -235,17 +260,31 @@
         ],
         compiler_params=pltpu.CompilerParams(vmem_limit_bytes=58 * 1024 * 1024),
         name="project",
-    )(
-        sc, hidden, hidden, edge, gain, wg, wv, ws, wst, cv, cs, bias, nal, tri,
-        jnp.asarray(e0, BF), jnp.asarray(e1, BF),
-    )
-
-
-def mix_kernel(
-    sc, gate, xpre, bc_r, col_r, row_r, ff, sbl, pb, sfd, sbd, hid, gout, ow, owt, ggain, skip,
-    e0, e1, e2,
+    )(*args)
+
+
+def split_refs(refs, groups, kinds):
+    taken = [[refs.pop(0) for _ in range(groups)] for _ in range(kinds)]
+    return [functools.partial(pick, refs_of) for refs_of in taken]
+
+
+def pick(refs_of, p):
+    per = refs_of[0].shape[-1] // 128
+    return refs_of[p // per], slice((p % per) * 128, (p % per + 1) * 128)
+
+
+def mix_kernel(groups, *refs):
+    refs = list(refs)
+    sc = refs.pop(0)
+    gates, xpres, ffs, sbls, pbs, sfds, sbds = split_refs(refs, groups, 7)
+    mix_body(sc, gates, xpres, ffs, sbls, pbs, sfds, sbds, *refs)
+
+
+def mix_body(
+    sc, gates, xpres, ffs, sbls, pbs, sfds, sbds,
+    bc_r, col_r, row_r, hid, gout, ow, owt, ggain, skip, e0, e1, e2,
     out_o, gnorm_o, dy_o, dgate_o, sf_o, sb_o, gbl_o, pg_o, dff_o,
-    gft_o, gbt_o, pgf_o, pgb_o, ggain_o, skip_o,
+    gft_o, gbt_o, pgf_o, pgb_o, hand_o, ggain_o, skip_o,
     sf_s, gb_s, gf_s, pg_s, q_s, y_s, dgn_s, exp_s,
 ):
     i = pl.program_id(0)
@@ -259,7 +298,10 @@
 
     @pl.when(i == 0)
     def _():
-        sf_s[...] = sfd[...].astype(F32)
+        enters_f = jnp.where(sc[3] == 1, 1.0, 0.0)
+        for p in range(pairs):
+            ref, at = sfds(p)
+            sf_s[:, p * 128 : (p + 1) * 128] = ref[:, at].astype(F32) * enters_f
         gb_s[...] = jnp.zeros_like(gb_s)
         gf_s[...] = jnp.zeros_like(gf_s)
         pg_s[...] = jnp.ones_like(pg_s)
@@ -267,6 +309,7 @@
         ggain_o[...] = jnp.zeros_like(ggain_o)
         skip_o[...] = jnp.zeros_like(skip_o)
 
+    enters_b = jnp.where(sc[4] == 1, 1.0, 0.0)
     glow = gout[...].astype(F32) * live
     gl = glow.astype(BF)
     dgn_s[...] = dot(gl, owt[...])
@@ -283,10 +326,11 @@
     wmix = jnp.concatenate([w, high, dec - high], axis=0).astype(BF)
     wtok = wmix[:SPAN]
     bc = bc_r[...]
-    bm, cm = bc[:, :STATE], bc[:, STATE:]
-    ct = jnp.transpose(bc.astype(F32))[STATE:].astype(BF)
+    bmf, cmf = bc[:, :STATE], bc[:, STATE:]
+    cm = cmf.astype(BF)
+    ct = jnp.transpose(bc)[STATE:].astype(BF)
     square_r = lax.broadcasted_iota(jnp.int32, (SPAN, SPAN), 0)
-    aff = jnp.where(square_r == lane, 0.0, dot_nt(cm, bm))
+    aff = jnp.where(square_r == lane, 0.0, fine_nt(cmf, bmf))
 
     squares = jnp.zeros((SPAN, 128), F32)
     for p in range(pairs):
@@ -302,11 +346,14 @@
         sf = sf_s[:, sl] * first
         sfb = sf.astype(BF)
         sf_o[0, :, sl] = sfb
-        sb = (sbl[0, :, sl].astype(F32) + pb[0, 0:1, sl] * sbd[:, sl].astype(F32)) * last
+        sbl, at = sbls(p)
+        pb, sbd, ff, xpre, gate = (r(p)[0] for r in (pbs, sbds, ffs, xpres, gates))
+        arrived = sbd[:, at].astype(F32) * enters_b
+        sb = (sbl[0, :, at].astype(F32) + pb[0, 0:1, at] * arrived) * last
         sbb = sb.astype(BF)
         sb_o[0, :, sl] = sbb
-        sf_s[:, sl] = sf * decay + ff[0, :, sl].astype(F32)
-        xp = xpre[:, sl].astype(F32)
+        sf_s[:, sl] = sf * decay + ff[0, :, at].astype(F32)
+        xp = xpre[:, at].astype(F32)
         x = xp * sigmoid(xp)
         xd = x * dte
         bd = jnp.concatenate(
@@ -322,7 +369,7 @@
         y = dot(jnp.concatenate(ms, axis=1), bd)
         y = y + ef * dot(cm, sfb) + eb * dot(cm, sbb) + skip[:, sl] * x
         y_s[:, sl] = y
-        g = gate[:, sl].astype(F32)
+        g = gate[:, at].astype(F32)
         gated = y * (g * sigmoid(g))
         squares = squares + gated * gated
 
@@ -330,7 +377,8 @@
     inner = jnp.zeros((SPAN, 128), F32)
     for p in range(pairs):
         sl = slice(p * 128, (p + 1) * 128)
-        g = gate[:, sl].astype(F32)
+        gate, at = gates(p)
+        g = gate[:, at].astype(F32)
         gunit = y_s[:, sl] * (g * sigmoid(g)) * gsc
         gnorm_o[:, sl] = (gunit * ggain[:, sl]).astype(BF)
         dgn = dgn_s[:, sl]
@@ -342,7 +390,8 @@
 
     for p in range(pairs):
         sl = slice(p * 128, (p + 1) * 128)
-        g = gate[:, sl].astype(F32)
+        gate, at = gates(p)
+        g = gate[:, at].astype(F32)
         sg = sigmoid(g)
         act = g * sg
         y = y_s[:, sl]
@@ -351,7 +400,7 @@
         dy = dgated * act
         dy_o[:, sl] = dy.astype(BF)
         dgate_o[:, sl] = (dgated * y * (sg * (1.0 + g * (1.0 - sg)))).astype(BF)
-        xp = xpre[:, sl].astype(F32)
+        xp = xpres(p)[0][:, at].astype(F32)
         skip_o[:, sl] += jnp.sum(dy * (xp * sigmoid(xp)), axis=0, keepdims=True)
         decay = exp_s[2, 0:1, sl]
         dff = dot(ct, (exp_s[0, :, sl] * dy).astype(BF))
@@ -373,13 +422,15 @@
         gbt_o[...] = gb_s[...]
         pgf_o[...] = q_s[...]
         pgb_o[...] = pg_s[...]
-
-
-def mix(sc, gate, xpre, bc, col, row, ff, sbl, pb, sfd, sbd, hidden, out_grad, ow, owt, ggain, skip):
+        hand_o[...] = jnp.where(sc[0] == 0, gb_s[...], gf_s[...]).astype(BF)
+
+
+def mix(sc, split, bc, col, row, hidden, out_grad, ow, owt, ggain, skip, e0, e1, e2):
     tokens, width_in = hidden.shape
-    width = gate.shape[1]
+    groups = len(split[0])
+    width = e0.shape[1]
+    part = width // groups
     blocks = tokens // SPAN
-    e0, e1, e2, _ = expanders(width // HEAD_DIM)
 
     def ahead(shape):
         rank = len(shape)
@@ -401,33 +452,21 @@
         (sds((STATE, width), F32), full((STATE, width))),
         (sds((8, width), F32), full((8, width))),
         (sds((8, width), F32), full((8, width))),
+        (sds((STATE, width), BF), full((STATE, width))),
         (sds((1, width), F32), full((1, width))),
         (sds((1, width), F32), full((1, width))),
     ]
-    in_specs = [
-        SMEM,
-        ahead((SPAN, width)),
-        ahead((SPAN, width)),
-        ahead((SPAN, 128)),
-        ahead((SPAN, 128)),
-        ahead((SPAN, 128)),
-        ahead(state),
-        ahead(state),
-        ahead((1, 8, width)),
-        full((STATE, width)),
-        full((STATE, width)),
-        ahead((SPAN, width_in)),
-        ahead((SPAN, width_in)),
-        full(ow.shape),
-        full(owt.shape),
-        full(ggain.shape),
-        full(skip.shape),
-        full(e0.shape),
-        full(e0.shape),
-        full(e0.shape),
-    ]
+    shared = [ow, owt, ggain, skip, e0, e1, e2]
+    in_specs = [SMEM]
+    for shape in (
+        (SPAN, part), (SPAN, part), (1, STATE, part), (1, STATE, part), (1, 8, part),
+    ):
+        in_specs += [ahead(shape)] * groups
+    in_specs += [full((STATE, part))] * (2 * groups)
+    in_specs += [ahead((SPAN, 128))] * 3 + [ahead((SPAN, width_in))] * 2
+    in_specs += [full(a.shape) for a in shared]
     return pl.pallas_call(
-        mix_kernel,
+        functools.partial(mix_kernel, groups),
         grid=(blocks,),
         in_specs=in_specs,
         out_specs=[spec for _, spec in outs],
@@ -444,14 +483,19 @@
         ],
         compiler_params=pltpu.CompilerParams(vmem_limit_bytes=58 * 1024 * 1024),
         name="mix",
-    )(
-        sc, gate, xpre, bc, col, row, ff, sbl, pb, sfd, sbd, hidden, out_grad, ow, owt, ggain, skip,
-        jnp.asarray(e0, BF), jnp.asarray(e1, BF), jnp.asarray(e2, BF),
-    )
-
-
-def back_kernel(
-    heads, sc, xpre, v_r, dy_r, bc_r, ps_r, pspre_r, col_r, row_r, sf_r, sb_r, gbl, pg, dff, gfd, gbd,
+    )(sc, *[a for kind in split for a in kind], bc, col, row, hidden, out_grad, *shared)
+
+
+def back_kernel(heads, groups, *refs):
+    refs = list(refs)
+    sc = refs.pop(0)
+    xpres, vs, gfds, gbds = split_refs(refs, groups, 4)
+    back_body(heads, sc, xpres, vs, gfds, gbds, *refs)
+
+
+def back_body(
+    heads, sc, xpres, vs, gfds, gbds,
+    dy_r, bc_r, ps_r, pspre_r, col_r, row_r, sf_r, sb_r, gbl, pg, dff,
     skip, cv, cs, nad, e0, e1, e2, seg, tris, rect,
     dv_o, dst_o, dz_o, cvg_o, csg_o, head_o, edge_o, edges_o,
     gf_s, edge_s, edges_s, da_s,
@@ -467,7 +511,10 @@
 
     @pl.when(step == 0)
     def _():
-        gf_s[...] = gfd[...].astype(F32)
+        enters_f = jnp.where(sc[5] == 1, 1.0, 0.0)
+        for p in range(pairs):
+            ref, at = gfds(p)
+            gf_s[:, p * 128 : (p + 1) * 128] = ref[:, at].astype(F32) * enters_f
         edge_s[...] = jnp.zeros_like(edge_s)
         edges_s[...] = jnp.zeros_like(edges_s)
         da_s[...] = jnp.zeros_like(da_s)
@@ -488,10 +535,12 @@
     wtok = wmix[:SPAN]
     winn = jnp.exp2(jnp.where(lane < 32, end[0:1] - col, col)).astype(BF)
     bc = bc_r[...]
-    bm, cm = bc[:, :STATE], bc[:, STATE:]
+    bmf, cmf = bc[:, :STATE], bc[:, STATE:]
+    bm, cm = bmf.astype(BF), cmf.astype(BF)
+    enters_b = jnp.where(sc[6] == 1, 1.0, 0.0)
     square_r = lax.broadcasted_iota(jnp.int32, (SPAN, SPAN), 0)
     off = square_r != lane
-    aff = jnp.where(off, dot_nt(bm, cm), 0.0)
+    aff = jnp.where(off, fine_nt(bmf, cmf), 0.0)
 
     daff = jnp.zeros((SPAN, SPAN), F32)
     red = jnp.zeros((SPAN, 128), F32)
@@ -510,13 +559,15 @@
         wb = dot(winn, e1[:, sl])
         sf, sb = sf_r[0, :, sl], sb_r[0, :, sl]
         gf32 = gf_s[:, sl] * last
-        gb32 = gbl[0, :, sl].astype(F32) + pg[0, 0:1, sl] * gbd[:, sl].astype(F32)
+        gbd, at = gbds(p)
+        arrived = gbd[:, at].astype(F32) * enters_b
+        gb32 = gbl[0, :, sl].astype(F32) + pg[0, 0:1, sl] * arrived
         gf, gb = gf32.astype(BF), gb32.astype(BF)
         gf_s[:, sl] = gf32 * decay + dff[0, :, sl].astype(F32)
         cross = (sf.astype(F32) * gf32 + sb.astype(F32) * gb32) * decay
         crossed = jnp.broadcast_to(jnp.sum(cross, axis=0, keepdims=True), (8, 128))
         span_sum = span_sum + dot(crossed.astype(BF), seg[4, sl, :])
-        xp = xpre[:, sl].astype(F32)
+        xp = xpres(p)[0][:, at].astype(F32)
         sg = sigmoid(xp)
         x = xp * sg
         xd = x * dte
@@ -558,7 +609,7 @@
         dxp = dx * (sg * (1.0 + xp * (1.0 - sg)))
         ext = jnp.concatenate([dxp, edge_s[:, sl] * last], axis=0)
         edge_s[:, sl] = dxp[:8]
-        v = v_r[:, sl].astype(F32)
+        v = vs(p)[0][:, at].astype(F32)
         dv = jnp.zeros((SPAN, 128), F32)
         for j in range(TAPS):
             moved = shifted(ext, j, SPAN)
@@ -608,12 +659,12 @@
         edges_o[...] = edges_s[...]
 
 
-def back(
-    heads, sc, xpre, v, dy, bc, ps, pspre, col, row, sf, sb, gbl, pg, dff, gfd, gbd, skip, cv, cs, nad
-):
-    tokens, width = xpre.shape
+def back(heads, sc, split, dy, bc, ps, pspre, col, row, sf, sb, gbl, pg, dff, skip, cv, cs, nad):
+    tokens, width = dy.shape
+    groups = len(split[0])
+    part = width // groups
     blocks = tokens // SPAN
-    maps = expanders(width // HEAD_DIM)
+    maps = expanders(heads)
     every = sum(maps)
     seg = np.stack([m.T for m in maps] + [every.T])
     at = np.arange(SPAN)
@@ -639,36 +690,15 @@
         (sds((8, width), F32), full((8, width))),
         (sds((8, 128), F32), full((8, 128))),
     ]
-    in_specs = [
-        SMEM,
-        rev((SPAN, width)),
-        rev((SPAN, width)),
-        rev((SPAN, width)),
-        rev((SPAN, 128)),
-        rev((SPAN, 128)),
-        rev((SPAN, 128)),
-        rev((SPAN, 128)),
-        rev((SPAN, 128)),
-        rev(state),
-        rev(state),
-        rev(state),
-        rev((1, 8, width)),
-        rev(state),
-        full((STATE, width)),
-        full((STATE, width)),
-        full(skip.shape),
-        full(cv.shape),
-        full(cs.shape),
-        full(nad.shape),
-        full((128, width)),
-        full((128, width)),
-        full((128, width)),
-        full(seg.shape),
-        full(tris.shape),
-        full(rect.shape),
-    ]
+    shared = [skip, cv, cs, nad]
+    shared += [jnp.asarray(m, BF) for m in (*maps[:3], seg, tris, rect)]
+    in_specs = [SMEM] + [rev((SPAN, part))] * (2 * groups)
+    in_specs += [full((STATE, part))] * (2 * groups)
+    in_specs += [rev((SPAN, width))] + [rev((SPAN, 128))] * 5
+    in_specs += [rev(state)] * 3 + [rev((1, 8, width)), rev(state)]
+    in_specs += [full(a.shape) for a in shared]
     return pl.pallas_call(
-        functools.partial(back_kernel, heads),
+        functools.partial(back_kernel, heads, groups),
         grid=(blocks,),
         in_specs=in_specs,
         out_specs=[spec for _, spec in outs],
@@ -682,10 +712,203 @@
         compiler_params=pltpu.CompilerParams(vmem_limit_bytes=58 * 1024 * 1024),
         name="back",
     )(
-        sc, xpre, v, dy, bc, ps, pspre, col, row, sf, sb, gbl, pg, dff, gfd, gbd, skip, cv, cs, nad,
-        jnp.asarray(maps[0], BF), jnp.asarray(maps[1], BF), jnp.asarray(maps[2], BF),
-        jnp.asarray(seg, BF), jnp.asarray(tris, BF), jnp.asarray(rect, BF),
+        sc, *[a for kind in split for a in kind],
+        dy, bc, ps, pspre, col, row, sf, sb, gbl, pg, dff, *shared,
     )
+
+
+def reduce_kernel(bits, lanes, mats, *refs):
+    n_mats = len(mats)
+    srcs, both, tiny = refs[:n_mats], refs[n_mats], refs[n_mats + 1]
+    outs = refs[n_mats + 2 : 2 * n_mats + 2]
+    both_o, tiny_o = refs[2 * n_mats + 2], refs[2 * n_mats + 3]
+    scratch = refs[2 * n_mats + 4 :]
+    own_r, sent = scratch[0], scratch[1]
+    halves, parts = scratch[2 : 2 + bits], scratch[2 + bits : 1 + 2 * bits]
+    tiny_r, tiny_s, send_s, recv_s, tsend_s, trecv_s = scratch[1 + 2 * bits :]
+    rows = srcs[0].shape[0] if mats[0] == "cols" else srcs[0].shape[0] // 2
+    width = outs[0].shape[1]
+    me = lax.axis_index("dp")
+    chan = lax.axis_index("chan")
+    bit = [lax.rem(lax.div(me, 2**k), 2) for k in range(bits)]
+    partner = [{"dp": me + (1 - 2 * bit[k]) * 2**k} for k in range(bits)]
+    across = {"chan": 1 - chan}
+    stages = [partner[0], across] + partner[1:]
+
+    barrier = pltpu.get_barrier_semaphore()
+    for device in stages:
+        pl.semaphore_signal(barrier, inc=1, device_id=device, device_id_type=pl.DeviceIdType.MESH)
+    pl.semaphore_wait(barrier, bits + 1)
+
+    chunks = [(m, s) for m in range(n_mats) for s in range(0, width, lanes)]
+    extra = len(chunks)
+    n = extra + 1
+    half = rows // 2
+
+    def mult(v):
+        return pl.multiple_of(v, 16)
+
+    def source(c, which, part):
+        if c == extra:
+            return both.at[pl.ds(mult(part * half), half), :]
+        m, s = chunks[c]
+        if mats[m] == "cols":
+            return srcs[m].at[pl.ds(mult(part * half), half), pl.ds(which * width + s, lanes)]
+        return srcs[m].at[pl.ds(mult(which * rows + part * half), half), pl.ds(s, lanes)]
+
+    def target(c, start, size):
+        if c == extra:
+            return both_o.at[pl.ds(mult(start), size), :]
+        m, s = chunks[c]
+        return outs[m].at[pl.ds(mult(start), size), pl.ds(s, lanes)]
+
+    def copy(src, dst, c, k, device):
+        return pltpu.make_async_remote_copy(
+            src_ref=src,
+            dst_ref=dst,
+            send_sem=send_s.at[c, k],
+            recv_sem=recv_s.at[c, k],
+            device_id=device,
+            device_id_type=pl.DeviceIdType.MESH,
+        )
+
+    offset = [bit[0] * half]
+    for k in range(1, bits):
+        offset.append(offset[-1] + bit[k] * (half >> k))
+
+    def first(c, which):
+        if c == extra and which == 0:
+            return None
+        slot = own_r.at[c, which]
+        return copy(source(c, which, 1 - bit[0]), slot, c, which, partner[0])
+
+    def second(c):
+        return copy(sent.at[c], halves[0].at[c], c, 2, across)
+
+    def halving(c, k):
+        size = half >> k
+        src = parts[k - 1].at[c, pl.ds(mult((1 - bit[k]) * size), size), :]
+        return copy(src, halves[k].at[c], c, 2 + k, partner[k])
+
+    def doubling(c, k):
+        size = half >> k
+        place = target(c, offset[k], size)
+        return copy(place, place, c, 2 + bits + k, partner[k])
+
+    def f32(ref):
+        return ref[...].astype(F32)
+
+    def stage(c, s):
+        if s == 0:
+            for which in (0, 1):
+                rdma = first(c, which)
+                if rdma is not None:
+                    rdma.start()
+        elif s == 1:
+            first(c, 1).wait_recv()
+            sent[c] = (f32(source(c, 1, bit[0])) + f32(own_r.at[c, 1])).astype(BF)
+            second(c).start()
+        elif s == 2:
+            second(c).wait_recv()
+            if c == extra:
+                total = f32(sent.at[c]) + f32(halves[0].at[c])
+            else:
+                first(c, 0).wait_recv()
+                total = f32(source(c, 0, bit[0])) + f32(own_r.at[c, 0]) + f32(halves[0].at[c])
+            parts[0][c] = total.astype(BF)
+            halving(c, 1).start()
+        elif s < bits + 2:
+            k = s - 2
+            size = half >> k
+            halving(c, k).wait_recv()
+            kept = parts[k - 1].at[c, pl.ds(mult(bit[k] * size), size), :]
+            total = (f32(kept) + f32(halves[k].at[c])).astype(BF)
+            if k < bits - 1:
+                parts[k][c] = total
+                halving(c, k + 1).start()
+            else:
+                target(c, offset[k], size)[...] = total
+                doubling(c, k).start()
+        else:
+            k = 2 * bits + 1 - s
+            doubling(c, k).wait_recv()
+            if k > 0:
+                doubling(c, k - 1).start()
+
+    def tiny_copy(k):
+        return pltpu.make_async_remote_copy(
+            src_ref=tiny if k == 0 else tiny_s.at[k - 1],
+            dst_ref=tiny_r.at[k],
+            send_sem=tsend_s.at[k],
+            recv_sem=trecv_s.at[k],
+            device_id=stages[k],
+            device_id_type=pl.DeviceIdType.MESH,
+        )
+
+    tiny_copy(0).start()
+    last = 2 * bits + 1
+    for tick in range(n + last):
+        for s in range(last, -1, -1):
+            c = tick - s
+            if 0 <= c < n:
+                stage(c, s)
+        if 1 <= tick <= bits + 1:
+            k = tick - 1
+            tiny_copy(k).wait_recv()
+            before = tiny[...] if k == 0 else tiny_s[k - 1]
+            total = before + tiny_r[k]
+            if k < bits:
+                tiny_s[k] = total
+                tiny_copy(k + 1).start()
+            else:
+                tiny_o[...] = total
+
+    for c in range(n):
+        for which in (0, 1):
+            rdma = first(c, which)
+            if rdma is not None:
+                rdma.wait_send()
+        second(c).wait_send()
+        for k in range(1, bits):
+            halving(c, k).wait_send()
+        for k in range(bits):
+            doubling(c, k).wait_send()
+    for k in range(bits + 1):
+        tiny_copy(k).wait_send()
+
+
+def reduce_all(bits, mats, both, tiny, lanes):
+    kinds = [kind for _, kind in mats]
+    arrays = [a for a, _ in mats]
+    rows = arrays[0].shape[0] if kinds[0] == "cols" else arrays[0].shape[0] // 2
+    width = arrays[0].shape[1] // 2 if kinds[0] == "cols" else arrays[0].shape[1]
+    half = rows // 2
+    n = len(arrays) * (width // lanes) + 1
+    vmem = pl.BlockSpec(memory_space=pltpu.VMEM)
+    sds = jax.ShapeDtypeStruct
+    scratch = [pltpu.VMEM((n, 2, half, lanes), BF), pltpu.VMEM((n, half, lanes), BF)]
+    scratch += [pltpu.VMEM((n, half >> k, lanes), BF) for k in range(bits)]
+    scratch += [pltpu.VMEM((n, half >> k, lanes), BF) for k in range(bits - 1)]
+    scratch += [
+        pltpu.VMEM((bits + 1,) + tiny.shape, F32),
+        pltpu.VMEM((bits,) + tiny.shape, F32),
+        pltpu.SemaphoreType.DMA((n, 2 + 2 * bits)),
+        pltpu.SemaphoreType.DMA((n, 2 + 2 * bits)),
+        pltpu.SemaphoreType.DMA((bits + 1,)),
+        pltpu.SemaphoreType.DMA((bits + 1,)),
+    ]
+    return pl.pallas_call(
+        functools.partial(reduce_kernel, bits, lanes, kinds),
+        out_shape=[sds((rows, width), BF)] * len(arrays)
+        + [sds(both.shape, BF), sds(tiny.shape, F32)],
+        in_specs=[vmem] * (len(arrays) + 2),
+        out_specs=[vmem] * (len(arrays) + 2),
+        scratch_shapes=scratch,
+        compiler_params=pltpu.CompilerParams(
+            collective_id=0, has_side_effects=True, vmem_limit_bytes=58 * 1024 * 1024
+        ),
+        name="reduce_all",
+    )(*arrays, both, tiny)
 
 
 def spread_heads(v):
@@ -702,6 +925,15 @@
     return entering
 
 
+def swap(v):
+    return lax.ppermute(v, "chan", [(0, 1), (1, 0)])
+
+
+def core_swap(v):
+    size = lax.axis_size("dp")
+    return lax.ppermute(v, "dp", [(k, k ^ 1) for k in range(size)])
+
+
 def on_device(
     hidden_in, norm_gain, gate_value_weight, state_weight, step_weight, value_conv, state_conv,
     step_bias, decay_log, skip_gain, gate_gain, out_weight, seq_length, seq_count, out_grad,
@@ -709,90 +941,147 @@
     tokens, width_in = hidden_in.shape
     channel = lax.axis_index("chan")
     shards = lax.axis_size("chan")
+    groups_dp = lax.axis_size("dp")
     length, count = seq_length[0], seq_count[0]
-    sc = jnp.stack([channel * tokens, length, count, 0]).astype(jnp.int32)
     local_heads = gate_value_weight.shape[1]
     local = local_heads * HEAD_DIM
-
-    def gather(v, axis):
-        return lax.all_gather(v, "chan", axis=axis, tiled=True)
-
-    wg = gather(gate_value_weight[:, :, :HEAD_DIM].reshape(width_in, local), 1)
-    wv = gather(gate_value_weight[:, :, HEAD_DIM:].reshape(width_in, local), 1)
-    ow = gather(out_weight, 0)
     heads = local_heads * shards
     width = heads * HEAD_DIM
+    paired = shards == 2 and local % 128 == 0 and groups_dp % 2 == 0
+    one = jnp.ones((), jnp.int32)
+    flags = [channel, 1 - channel, 1 - channel, channel] if paired else [one] * 4
+    sc = jnp.stack([channel * tokens, length, count] + flags).astype(jnp.int32)
+    ups = [(k, k + 1) for k in range(shards - 1)]
+    downs = [(k + 1, k) for k in range(shards - 1)]
+    gain = norm_gain[None]
+
+    wg = gate_value_weight[:, :, :HEAD_DIM].reshape(width_in, local)
+    wv = gate_value_weight[:, :, HEAD_DIM:].reshape(width_in, local)
+    edge = lax.ppermute(hidden_in[tokens - PAD :], "chan", ups)
+    vec = jnp.concatenate([step_bias, decay_log, skip_gain])
     small = jnp.concatenate(
-        [value_conv.reshape(-1), gate_gain, step_bias, decay_log, skip_gain]
+        [
+            value_conv,
+            gate_gain[None],
+            jnp.pad(vec, (0, local - 3 * local_heads))[None],
+        ]
     )
-    small = gather(small[None], 0)
-    cuts = np.cumsum([TAPS * local, local, local_heads, local_heads])
-    cv = small[:, : cuts[0]].reshape(shards, TAPS, local).transpose(1, 0, 2).reshape(TAPS, width)
-    ggain = small[:, cuts[0] : cuts[1]].reshape(1, width)
-    bias_all = small[:, cuts[1] : cuts[2]].reshape(heads)
-    dlog_all = small[:, cuts[2] : cuts[3]].reshape(heads)
-    skip_all = small[:, cuts[3] :].reshape(heads)
-    wstep = gather(step_weight, 1)
-    wst = jnp.tile(jnp.pad(wstep, ((0, 0), (0, GROUP - heads))), (1, 4))
+
+    def step_matrix(steps):
+        return jnp.tile(jnp.pad(steps, ((0, 0), (0, GROUP - steps.shape[1]))), (1, 4))
+
+    e0, e1, e2, _ = [jnp.asarray(e, BF) for e in expanders(heads)]
+    maps = (gain, state_weight, state_conv)
+    if paired:
+        first_core = lax.axis_index("dp") % 2 == 0
+        come = swap(jnp.where(first_core, wg, wv))
+        small_b = swap(small)
+        wstep = jnp.concatenate([step_weight, swap(step_weight)], axis=1)
+        ow_b = swap(out_weight)
+        also = core_swap(come)
+        wgs = [wg, jnp.where(first_core, come, also)]
+        wvs = [wv, jnp.where(first_core, also, come)]
+        smalls = [small, small_b]
+        ow = jnp.concatenate([out_weight, ow_b], axis=0)
+    else:
+        wgs = [lax.all_gather(wg, "chan", axis=1, tiled=True)]
+        wvs = [lax.all_gather(wv, "chan", axis=1, tiled=True)]
+        gathered = lax.all_gather(small, "chan", axis=0)
+        wstep = lax.all_gather(step_weight, "chan", axis=1, tiled=True)
+        smalls = [gathered[k] for k in range(shards)]
+        ow = lax.all_gather(out_weight, "chan", axis=0, tiled=True)
+
+    def heads_row(k, parts):
+        lo, hi = k * local_heads, (k + 1) * local_heads
+        return jnp.concatenate([p[TAPS + 1, lo:hi] for p in parts])
+
+    bias_all, dlog_all, skip_all = (heads_row(k, smalls) for k in range(3))
+    cv = jnp.concatenate([p[:TAPS] for p in smalls], axis=1)
+    ggain = jnp.concatenate([p[TAPS : TAPS + 1] for p in smalls], axis=1)
     skip = jnp.repeat(skip_all, HEAD_DIM)[None]
     nad = -jnp.exp(dlog_all)
-    gain = norm_gain[None]
-
-    ups = [(k, k + 1) for k in range(shards - 1)]
-    downs = [(k + 1, k) for k in range(shards - 1)]
-    edge = lax.ppermute(hidden_in[tokens - PAD :], "chan", ups)
-
+
+    if paired:
+        gate, v, xpre, ff, sbl, pb, _, _, _, _, hand, vh, normed, nedge, ps, pspre, bc, psh = project(
+            sc, hidden_in, edge, wg, wv, step_matrix(step_weight), value_conv,
+            spread_heads(step_bias), spread_heads(-jnp.exp(decay_log) * LOG2E),
+            e0[:, :local], e1[:, :local], maps=maps, final=False,
+        )
+        enter_b = swap(hand)
+        gate2, v2, xpre2, ff2, sbl2, pb2, _, _, _, _, hand2, vh2, col, row = project(
+            sc, normed, nedge, wgs[1], wvs[1], step_matrix(wstep), smalls[1][:TAPS],
+            spread_heads(bias_all), spread_heads(nad * LOG2E),
+            e0[:, local:], e1[:, local:], bc=bc, final=True,
+        )
+        enter = [swap(hand2), enter_b]
+        split = [[gate, gate2], [xpre, xpre2], [ff, ff2], [sbl, sbl2], [pb, pb2], enter, enter]
+        vs, xs = [v, v2], [xpre, xpre2]
+        vh = jnp.concatenate([vh, vh2], axis=1)
+    else:
+        (
+            gate, v, xpre, ff, sbl, pb, sft, sbt, pft, pbt, _, vh, normed, nedge, ps, pspre, bc, psh,
+            col, row,
+        ) = project(
+            sc, hidden_in, edge, wgs[0], wvs[0], step_matrix(wstep), cv, spread_heads(bias_all),
+            spread_heads(nad * LOG2E), e0, e1, maps=maps,
+        )
+        sfd = handed(sft, pft, shards, True)
+        sbd = handed(sbt, pbt, shards, False)
+        split = [[gate], [xpre], [ff], [sbl], [pb], [sfd], [sbd]]
+        vs, xs = [v], [xpre]
     (
-        normed, gate, v, xpre, ps, pspre, bc, col, row, ff, sbl, pb, sft, sbt, pft, pbt, vh, psh,
-    ) = project(
-        sc, hidden_in, edge, gain, wg, wv, state_weight, wst, cv, state_conv,
-        spread_heads(bias_all), spread_heads(nad * LOG2E),
-    )
-    sfd = handed(sft, pft, shards, True)
-    sbd = handed(sbt, pbt, shards, False)
-    (
-        output, gnorm, dy, dgate, sf, sb, gbl, pg, dff, gft, gbt, pgf, pgb, ggain_grad, skip_grad,
-    ) = mix(
-        sc, gate, xpre, bc, col, row, ff, sbl, pb, sfd, sbd, hidden_in, out_grad, ow, ow.T, ggain, skip
-    )
-    gfd = handed(gft, pgf, shards, False)
-    gbd = handed(gbt, pgb, shards, True)
+        output, gnorm, dy, dgate, sf, sb, gbl, pg, dff, gft, gbt, pgf, pgb, hand, ggain_grad, skip_grad,
+    ) = mix(sc, split, bc, col, row, hidden_in, out_grad, ow, ow.T, ggain, skip, e0, e1, e2)
+    if paired:
+        enter = swap(hand)
+        enter = [enter[:, local:], enter[:, :local]]
+        gfds = gbds = enter
+    else:
+        gfds = [handed(gft, pgf, shards, False)]
+        gbds = [handed(gbt, pgb, shards, True)]
+
+    own_ids = channel * tokens + jnp.arange(tokens, dtype=jnp.int32)
+    live = jnp.where(own_ids // length < count, 1.0, 0.0)[:, None].astype(BF)
+    ow_grad = dot_tn(gnorm, out_grad * live).astype(BF)
+    dwg = dot_tn(normed, dgate).astype(BF)
+
     dv, dst, dz, cvg, csg, head_sums, edge_g, edges_g = back(
-        heads, sc, xpre, v, dy, bc, ps, pspre, col, row, sf, sb, gbl, pg, dff, gfd, gbd, skip, cv,
+        heads, sc, [xs, vs, gfds, gbds], dy, bc, ps, pspre, col, row, sf, sb, gbl, pg, dff, skip, cv,
         state_conv, spread_heads(nad),
     )
 
-    joined = jnp.concatenate([edge_g, edges_g], axis=1)
+    if paired:
+        turned = jnp.concatenate([edge_g[:, local:], edge_g[:, :local]], axis=1)
+    else:
+        turned = edge_g
     kernel = jnp.concatenate([cv, state_conv], axis=1)
     past = jnp.concatenate([vh, psh], axis=1)
     reach = TAPS - 1
-    after = lax.ppermute(joined, "chan", downs)[:reach]
+    after = lax.ppermute(jnp.concatenate([turned, edges_g], axis=1), "chan", downs)[:reach]
+    joined = jnp.concatenate([edge_g, edges_g], axis=1)
     after = after * jnp.where(((channel + 1) * tokens) % length == 0, 0.0, 1.0)
     patch = jnp.zeros((reach, joined.shape[1]), F32)
     taps = []
     for j in range(TAPS):
-        moved = jnp.zeros_like(patch).at[reach - j :].set(after[:j]) if j else jnp.zeros_like(patch)
-        patch = patch + moved * kernel[TAPS - 1 - j][None]
-        own = joined[:j] * past[PAD - j :]
-        taps.append(jnp.sum(own, axis=0))
+        if j:
+            moved = jnp.pad(after[:j], ((reach - j, 0), (0, 0)))
+            patch = patch + moved * kernel[TAPS - 1 - j][None]
+        taps.append(jnp.sum(joined[:j] * past[PAD - j :], axis=0))
     cross_taps = jnp.stack(taps[::-1])
-    tail = jnp.pad(patch, ((PAD - reach, 0), (0, 0)))
-    dv = dv.at[tokens - PAD :].add(tail[:, :width].astype(BF))
-    dst = dst.at[tokens - PAD :].add(tail[:, width:].astype(BF))
+    tail = jnp.pad(patch, ((PAD - reach, 0), (0, 0))).astype(BF)
+    dv = dv.at[tokens - PAD :].add(tail[:, :width])
+    dst = dst.at[tokens - PAD :].add(tail[:, width:])
     cvg = cvg + cross_taps[:, :width]
     csg = csg + cross_taps[:, width:]
 
-    gl_scale = jnp.where(
-        (channel * tokens + jnp.arange(tokens, dtype=jnp.int32)) // length < count, 1.0, 0.0
-    )[:, None]
-    gl = (out_grad * gl_scale.astype(BF)).astype(BF)
-    ow_grad = dot_tn(gnorm, gl)
-    dwg = dot_tn(normed, dgate)
-    dwv = dot_tn(normed, dv)
+    dwv = dot_tn(normed, dv).astype(BF)
     dws = dot_tn(normed, dst)
     dwst = dot_tn(normed, dz)[:, 96 : 96 + heads]
     wst_tail = jnp.pad(wstep, ((0, 0), (96, GROUP - heads)))
-    dn = dot_nt(dgate, wg) + dot_nt(dv, wv) + dot_nt(dst, state_weight) + dot_nt(dz, wst_tail)
+    dn = dot_nt(dst, state_weight) + dot_nt(dz, wst_tail)
+    for k, (a, b) in enumerate(zip(wgs, wvs)):
+        cut = slice(k * a.shape[1], (k + 1) * a.shape[1])
+        dn = dn + dot_nt(dgate[:, cut], a) + dot_nt(dv[:, cut], b)
     u = hidden_in.astype(F32)
     scale = lax.rsqrt(jnp.mean(u * u, axis=1, keepdims=True) + EPS)
     unit = u * scale
@@ -801,43 +1090,72 @@
     inner = jnp.mean(du * unit, axis=1, keepdims=True)
     input_grad = (out_grad.astype(F32) + scale * (du - unit * inner)).astype(BF)
 
+    bias_sum = head_sums[1, 96 : 96 + heads]
+    dlog_sum = head_sums[0, 64 : 64 + heads]
+    skip_sum = skip_grad.reshape(heads, HEAD_DIM).sum(axis=1)
+
+    def by_shard(k):
+        cut, hcut = slice(k * local, (k + 1) * local), slice(k * local_heads, (k + 1) * local_heads)
+        return jnp.concatenate(
+            [cvg[:, cut].reshape(-1), ggain_grad[0, cut], bias_sum[hcut], dlog_sum[hcut], skip_sum[hcut]]
+        )
+
+    def absolute(parts, axis):
+        if not paired:
+            return jnp.concatenate(parts, axis=axis)
+        a = jnp.concatenate(parts, axis=axis)
+        b = jnp.concatenate(parts[::-1], axis=axis)
+        return jnp.where(channel == 0, a, b)
+
+    each = (TAPS + 1) * local + 3 * local_heads
+    pad_each = -each % 128
+    tiny = absolute([jnp.pad(by_shard(k), (0, pad_each)) for k in range(shards)], 0)
+    tiny = jnp.concatenate([tiny, norm_gain_grad, csg.reshape(-1)])
+    tiny = jnp.pad(tiny, (0, -tiny.shape[0] % 1024)).reshape(-1, 128)
+    dwst = absolute([dwst[:, k * local_heads : (k + 1) * local_heads] for k in range(shards)], 1)
+    both = jnp.concatenate([dws, jnp.pad(dwst, ((0, 0), (0, 128 - heads)))], axis=1).astype(BF)
+
+    bits = groups_dp.bit_length() - 1
+    if paired and groups_dp == 2**bits and bits >= 2 and width_in % (16 * groups_dp) == 0:
+        dwg, dwv, owg, both, tiny = reduce_all(
+            bits, [(dwg, "cols"), (dwv, "cols"), (ow_grad, "rows")], both, tiny, 256
+        )
+        dwg, dwv, owg = dwg.astype(F32), dwv.astype(F32), owg.astype(F32)
+    else:
+
+        def shared(v, axis):
+            if paired:
+                parts = jnp.split(v, 2, axis=axis)
+                v = absolute(parts, axis)
+            v = lax.psum_scatter(v, "chan", scatter_dimension=axis, tiled=True)
+            return lax.psum(v, "dp").astype(F32)
+
+        dwg, dwv, owg = shared(dwg, 1), shared(dwv, 1), shared(ow_grad, 0)
+        both, tiny = lax.psum((both, tiny), ("dp", "chan"))
+
     gvw = jnp.stack(
-        [dwg.reshape(width_in, heads, HEAD_DIM), dwv.reshape(width_in, heads, HEAD_DIM)], axis=2
-    ).reshape(width_in, heads, 2 * HEAD_DIM)
-    gvw = lax.psum(
-        lax.psum_scatter(gvw.astype(BF), "chan", scatter_dimension=1, tiled=True), "dp"
-    ).astype(F32)
-    owg = lax.psum(
-        lax.psum_scatter(ow_grad.astype(BF), "chan", scatter_dimension=0, tiled=True), "dp"
-    ).astype(F32)
-    smalls = (
-        norm_gain_grad, dws, dwst, cvg, csg, head_sums[1, 96 : 96 + heads],
-        head_sums[0, 64 : 64 + heads], skip_grad.reshape(heads, HEAD_DIM).sum(axis=1), ggain_grad[0],
-    )
-    sizes = [int(np.prod(s.shape)) for s in smalls]
-    flat = lax.psum(jnp.concatenate([s.reshape(-1) for s in smalls]), ("dp", "chan"))
-    pieces, offset = [], 0
-    for s, size in zip(smalls, sizes):
-        pieces.append(flat[offset : offset + size].reshape(s.shape))
-        offset += size
-    ngg, dws, dwst, cvg, csg, sbg, dlg, skg, ggg = pieces
-
-    def mine(v, count_local, axis):
-        return lax.dynamic_slice_in_dim(v, channel * count_local, count_local, axis)
-
+        [dwg.reshape(width_in, local_heads, HEAD_DIM), dwv.reshape(width_in, local_heads, HEAD_DIM)],
+        axis=2,
+    ).reshape(width_in, local_heads, 2 * HEAD_DIM)
+    both = both.astype(F32)
+    flat = tiny.reshape(-1)
+    base = (each + pad_each) * shards
+    mine = lax.dynamic_slice_in_dim(flat, channel * (each + pad_each), each, 0)
+    cuts = np.cumsum([TAPS * local, local, local_heads, local_heads])
+    dwst = lax.dynamic_slice_in_dim(both[:, 128:], channel * local_heads, local_heads, 1)
     return (
         output,
         input_grad,
-        ngg,
+        flat[base : base + width_in],
         gvw,
-        dws,
-        mine(dwst, local_heads, 1),
-        mine(cvg, local, 1),
-        csg,
-        mine(sbg, local_heads, 0),
-        mine(dlg, local_heads, 0),
-        mine(skg, local_heads, 0),
-        mine(ggg, local, 0),
+        both[:, :128],
+        dwst,
+        mine[: cuts[0]].reshape(TAPS, local),
+        flat[base + width_in : base + width_in + TAPS * 128].reshape(TAPS, 128),
+        mine[cuts[1] : cuts[2]],
+        mine[cuts[2] : cuts[3]],
+        mine[cuts[3] :],
+        mine[cuts[0] : cuts[1]],
         owg,
     )
 

time: 747 us -> 561 us (0.75)
  waiting for transfers between devices: 283 us -> 16.1 us
  Pallas kernels: 258 us -> 358 us
  between operations: 17.1 us -> 2.92 us
  local copies, waits for them, and re-layouts: 73 us -> 60.9 us
  other arithmetic: 21.9 us -> 33.6 us
  blocking collectives: 10.9 us -> 0 us
  matrix products: 57.9 us -> 67.3 us
    psum x2 -> x0, waiting for transfers between devices: 224 us -> none  [the longest x1 127 us: on_device(): lax.psum(jnp.concatenate([s.reshape(-1) for s in smalls]), ('dp', 'chan'))]
    pallas_call x3 -> x5, Pallas kernels: 258 us -> 358 us  [the longest x1 131 us: back(): pl.pallas_call(functools.partial(back_kernel, heads, groups), grid=(block...]
    all_gather x3 -> x0, waiting for transfers between devices: 48.6 us -> none  [gather(): return lax.all_gather(v, 'chan', axis=axis, tiled=True)]
    dot_general x4 -> x6, matrix products: 22.9 us -> 42.2 us  [dot_nt(): lax.dot_general(a, b, (((1,), (1,)), ((), ())), preferred_element_type=F32)]
    ppermute x5 -> x9, waiting for transfers between devices: 1.38 us -> 16.1 us  [the longest x7 14.2 us: swap(): return lax.ppermute(v, 'chan', [(0, 1), (1, 0)])]
    concatenate x3 -> x5, local copies, waits for them, and re-layouts: 13 us -> 3.4 us  [the longest x1 2.46 us: on_device(): ow = jnp.concatenate([out_weight, ow_b], axis=0)]
    reduce_scatter x2 -> x0, waiting for transfers between devices: 9.4 us -> none  [the longest x1 9.4 us: on_device(): lax.psum_scatter(gvw.astype(BF), 'chan', scatter_dimension=1, tiled=True)]
    another operation x7 -> x5, local copies, waits for them, and re-layouts: 10.7 us -> 2.26 us  [the longest x4 1.64 us: step_matrix(): jnp.tile(jnp.pad(steps, ((0, 0), (0, GROUP - steps.shape[1]))), (1, 4))]
  transfers between devices with their start and end apart: 13 -> 10, of which waited for: 6 -> 3; matrix products, arithmetic and copies ran while one was open for 18% -> 8% of each run, Pallas kernels for 25% -> 11%
where the time goes in v2:
time: 561 us; the launch traced here: 551 us
  Pallas kernels  358 us (64%)
  matrix products  67.3 us (12%)
  local copies, waits for them, and re-layouts  60.9 us (11%)
  other arithmetic  33.6 us (6%)
  waiting for transfers between devices  16.1 us (3%)
  starting transfers between devices  12.2 us (2%)
    pallas_call x1, Pallas kernels, back(): pl.pallas_call(functools.partial(back_kernel, heads, groups), grid=(block...  131 us
    pallas_call x1, Pallas kernels, reduce_all(): pl.pallas_call(functools.partial(reduce_kernel, bits, lanes, kinds), out_...  94.1 us
    pallas_call x1, Pallas kernels, mix(): pl.pallas_call(functools.partial(mix_kernel, groups), grid=(blocks,), in_...  75.2 us
    pallas_call x2, Pallas kernels, project(): pl.pallas_call(functools.partial(project_kernel, fresh, final, tile, chun...  58.3 us
    dot_general x6, matrix products, dot_nt(): lax.dot_general(a, b, (((1,), (1,)), ((), ())), preferred_element_type=F32)  42.2 us
    dot_general x5, matrix products, dot_tn(): lax.dot_general(a, b, (((0,), (0,)), ((), ())), preferred_element_type=F32)  25.1 us
    unnamed x95, local copies, waits for them, and re-layouts  20 us
    ppermute x7, waiting for transfers between devices, swap(): return lax.ppermute(v, 'chan', [(0, 1), (1, 0)])  14.2 us
  transfers between devices with their start and end apart: 10, of which 3 were waited for; matrix products, arithmetic and copies ran while one was open for 8% of the time, Pallas kernels for 11%

profile of v2, /device:TPU:1, one launch (start us, length us, event | category | flops | bytes accessed | tf_op | source)
XLA Modules:
  0.0 551.3 jit_solution(14957126360918549825)
XLA Ops:
  0.7 4.7 fusion.41
  5.3 2.8 copy.92
  34.6 10.7 %collective-permute-done.4 = f32[6,768]{1,0:T(8,128)S(1)} collective-permute-done((f32[6,768]{1,0:T(8,128)S(1)}, f32[6,768]{1,0:T(8,128)S(1)}, u32[]{:S(2)}, u32[]{:S(2)}) %collective-permute-start.4) | collective-permute-done | bytes 18464 | tf_op jit(solution)/shard_map/ppermute | solution.py:929
  57.9 31.4 %project.2 = (bf16[2048,768]{1,0:T(8,128)(2,1)}, bf16[2048,768]{1,0:T(8,128)(2,1)}, bf16[2048,768]{1,0:T(8,128)(2,1)}, bf16[16,64,768]{2,1,0:T(8,128)(2,1)}, bf1...) custom-call(s32[7]{0:T(128)} %stack.34.refs_0_, ...), custom_call_target="tpu_custom_call" | custom-call | tf_op jit(solution)/shard_map/project/pallas_call | solution.py:249
  93.0 3.0 fusion.39
  98.4 2.8 broadcast_select_fusion
  101.3 26.9 %project.3 = (bf16[2048,768]{1,0:T(8,128)(2,1)}, bf16[2048,768]{1,0:T(8,128)(2,1)}, bf16[2048,768]{1,0:T(8,128)(2,1)}, bf16[16,64,768]{2,1,0:T(8,128)(2,1)}, bf1...) custom-call(s32[7]{0:T(128)} %stack.34.refs_0_, ...), custom_call_target="tpu_custom_call" | custom-call | tf_op jit(solution)/shard_map/project/pallas_call | solution.py:249
  129.1 3.5 collective-permute-done.5.refs_11_.refs_13_
  133.2 75.2 %mix.1 = (bf16[2048,768]{1,0:T(8,128)(2,1)}, bf16[2048,1536]{1,0:T(8,128)(2,1)}, bf16[2048,1536]{1,0:T(8,128)(2,1)}, bf16[2048,1536]{1,0:T(8,128)(2,1)}, bf16[16...) custom-call(s32[7]{0:T(128)} %stack.34.refs_0_, ...), custom_call_target="tpu_custom_call" | custom-call | tf_op jit(solution)/shard_map/mix/pallas_call | solution.py:468
  208.4 7.3 %fusion.15 = f32[2048,768]{1,0:T(8,128)} fusion(bf16[768,768]{1,0:T(8,128)(2,1)S(1)} %copy-done.7, bf16[2048,1536]{1,0:T(8,128)(2,1)} %get-tuple-element.179), kind=kOutput, calls=%fused_computation.21 | convolution fusion | flops 2415919104 | bytes 10616832 | tf_op jit(solution)/shard_map/dot_general | solution.py:28
  215.7 4.5 fusion.17
  220.3 6.5 %convolution_convert_fusion.2.refs_0_ = bf16[768,1536]{1,0:T(8,128)(2,1)} fusion(bf16[2048,768]{1,0:T(8,128)(2,1)S(1)} %copy-done.3, bf16[2048,1536]{1,0:T(8,128)(2,1)S(1)} %copy-done.40), kind=kOutput, calls=%fused_computation.15 | convolution fusion | flops 4833017856 | bytes 11796480 | tf_op jit(solution)/shard_map/dot_general | solution.py:32
  227.3 10.5 %convolution_convert_fusion.refs_2_ = bf16[1536,768]{1,0:T(8,128)(2,1)} fusion(bf16[2048,1536]{1,0:T(8,128)(2,1)} %get-tuple-element.181, bf16[2048,768]{1,0:T(8,128)(2,1)S(1)} %copy-done.2, bf16[2048]{0:T(1024)(128)(2,1)S(1)} %copy-done.33), kind=kOutput, calls=%fused_computation.13 | convolution fusion | flops 4834590720 | bytes 11800576 | tf_op jit(solution)/shard_map/dot_general | solution.py:32
  238.7 130.7 %back.1 = (bf16[2048,1536]{1,0:T(8,128)(2,1)}, bf16[2048,128]{1,0:T(8,128)(2,1)}, bf16[2048,128]{1,0:T(8,128)(2,1)}, f32[4,1536]{1,0:T(4,128)}, f32[4,128]{1,0:T...) custom-call(s32[7]{0:T(128)} %stack.34.refs_0_, ...), custom_call_target="tpu_custom_call" | custom-call | tf_op jit(solution)/shard_map/back/pallas_call | solution.py:700
  371.7 4.8 fusion.24
  388.2 4.9 fusion.49
  394.4 4.7 fusion.12
  399.6 6.5 %convolution_convert_fusion.1.refs_1_ = bf16[768,1536]{1,0:T(8,128)(2,1)} fusion(bf16[2048,768]{1,0:T(8,128)(2,1)S(1)} %copy-done.5, bf16[2048,1536]{1,0:T(8,128)(2,1)S(1)} %fusion.27), kind=kOutput, calls=%fused_computation.14 | convolution fusion | flops 4833017856 | bytes 11796480 | tf_op jit(solution)/shard_map/dot_general | solution.py:32
  406.9 15.9 %fusion.8 = (f32[768]{0:T(1024)S(1)}, f32[2048]{0:T(1024)}, f32[2048,768]{1,0:T(8,128)}) fusion(bf16[2048,768]{1,0:T(8,128)(2,1)S(1)} %copy-done.1, f32[2048]{0:T(1024)S(1)} %copy-done.22, f32[768]{0:T(1024)S(1)} %copy-done.24, bf16[768,768]{1,0:T(8,128)(2,1)S(1)} %copy-done.6, bf16[2048,1536]{1,0:T(8,128)(2,1)} %copy-done.12, f32[2048,768]{1,0:T(8,128)} %fusion.15, ...), kind=kOutput, calls=%fused_computation.10 | convolution fusion | flops 2434790656 | bytes 45242368 | tf_op jit(solution)/shard_map/dot_general | solution.py:28
  423.4 94.1 %reduce_all.1 = (bf16[768,768]{1,0:T(8,128)(2,1)}, bf16[768,768]{1,0:T(8,128)(2,1)}, bf16[768,768]{1,0:T(8,128)(2,1)}, bf16[768,256]{1,0:T(8,128)(2,1)}, f32[72,128]{1,0:T(8,128)}) custom-call(bf16[768,1536]{1,0:T(8,128)(2,1)} %convolution_convert_fusion.2.refs_0_, bf16[768,1536]{1,0:T(8,128)(2,1)} %convolution_convert_fusion.1.refs_1_, ...), custom_call_target="tpu_custom_call" | custom-call | tf_op jit(solution)/shard_map/reduce_all/pallas_call | solution.py:900
  526.8 2.7 copy.88
  529.5 6.0 %copy.89 = f32[768,12,128]{2,0,1:T(8,128)} copy(f32[768,12,128]{0,2,1:T(8,128)} %bitcast.63) | data formatting | bytes 9437184
  535.5 2.9 convert_element_type.63
  543.6 5.9 %fusion.7 = bf16[2048,768]{1,0:T(8,128)(2,1)} fusion(bf16[2048,768]{1,0:T(8,128)(2,1)S(1)} %copy-done.1, bf16[2048,768]{1,0:T(8,128)(2,1)} %refs_19_.1, f32[2048,768]{1,0:T(8,128)} %get-tuple-element.274, f32[2048]{0:T(1024)S(1)} %broadcast_multiply_fusion, f32[768]{0:T(1024)S(1)} %copy-done.24, f32[2048]{0:T(1024)S(1)} %copy-done.22), kind=kLoop, calls=%fused_computation.9 | loop fusion | flops 14155776 | bytes 15748096 | tf_op jit(solution)/shard_map/convert_element_type | solution.py:1091
  (214 shorter events, 79.5 us)
Async XLA Ops:
  11.8 10.1 %copy-start.37 = (f32[12]{0:T(128)S(1)}, f32[12]{0:T(128)}, u32[]{:S(2)}) copy-start(f32[12]{0:T(128)} %param.49) | copy-start | bytes 148
  11.8 10.1 %copy-start.38 = (f32[12]{0:T(128)S(1)}, f32[12]{0:T(128)}, u32[]{:S(2)}) copy-start(f32[12]{0:T(128)} %param.48) | copy-start | bytes 148
  11.8 10.1 %copy-start.39 = (f32[12]{0:T(128)S(1)}, f32[12]{0:T(128)}, u32[]{:S(2)}) copy-start(f32[12]{0:T(128)} %param.47) | copy-start | bytes 148
  11.8 10.2 %copy-start.32 = (f32[768]{0:T(1024)S(1)}, f32[768]{0:T(1024)}, u32[]{:S(2)}) copy-start(f32[768]{0:T(1024)} %param.50) | copy-start | bytes 9220
  11.8 10.2 %copy-start.20 = (f32[4,768]{1,0:T(4,128)S(1)}, f32[4,768]{1,0:T(4,128)}, u32[]{:S(2)}) copy-start(f32[4,768]{1,0:T(4,128)} %refs_7_.1) | copy-start | bytes 36868
  16.7 29.2 %collective-permute-start.1 = (bf16[768,768]{1,0:T(8,128)(2,1)}, bf16[768,768]{1,0:T(8,128)(2,1)}, u32[]{:S(2)}, u32[]{:S(2)}) collective-permute-start(bf16[768,768]{1,0:T(8,128)(2,1)} %broadcast_select_fusion.2), channel_id=1, source_target_pairs={{0,1},{1,0},{2,3},{3,2},{4,5},{5,4},{6,7},{7,6},{8,9},{9,8},{10,11... | collective-permute-start | bytes 3538952 | tf_op jit(solution)/shard_map/ppermute | solution.py:929
  19.4 38.5 %collective-permute-start = (bf16[16,768]{1,0:T(8,128)(2,1)}, bf16[16,768]{1,0:T(8,128)(2,1)}, u32[]{:S(2)}, u32[]{:S(2)}) collective-permute-start(bf16[16,768]{1,0:T(8,128)(2,1)} %slice.300), channel_id=1, source_target_pairs={{0,1},{2,3},{4,5},{6,7},{8,9},{10,11},{12,13},{14,15},{16,17},{18,... | collective-permute-start | bytes 73736 | tf_op jit(solution)/shard_map/ppermute | solution.py:960
  22.0 10.0 %copy-start.23 = (f32[768]{0:T(1024)S(1)}, f32[768]{0:T(1024)}, u32[]{:S(2)}) copy-start(f32[768]{0:T(1024)} %param.41) | copy-start | bytes 9220
  22.0 23.3 %collective-permute-start.4 = (f32[6,768]{1,0:T(8,128)S(1)}, f32[6,768]{1,0:T(8,128)S(1)}, u32[]{:S(2)}, u32[]{:S(2)}) collective-permute-start(f32[6,768]{1,0:T(8,128)S(1)} %pad_maximum_fusion.4), channel_id=1, source_target_pairs={{0,1},{1,0},{2,3},{3,2},{4,5},{5,4},{6,7},{7,6},{8,9},{9,8},{10,11... | collective-permute-start | bytes 55304 | tf_op jit(solution)/shard_map/ppermute | solution.py:929
  22.1 27.4 %collective-permute-start.3 = (bf16[768,12]{0,1:T(8,128)(2,1)}, bf16[768,12]{0,1:T(8,128)(2,1)}, u32[]{:S(2)}, u32[]{:S(2)}) collective-permute-start(bf16[768,12]{0,1:T(8,128)(2,1)} %param.44), channel_id=1, source_target_pairs={{0,1},{1,0},{2,3},{3,2},{4,5},{5,4},{6,7},{7,6},{8,9},{9,8},{10,11... | collective-permute-start | bytes 55304 | tf_op jit(solution)/shard_map/ppermute | solution.py:929
  25.9 67.1 %collective-permute-start.7 = (bf16[768,768]{0,1:T(8,128)(2,1)}, bf16[768,768]{0,1:T(8,128)(2,1)}, u32[]{:S(2)}, u32[]{:S(2)}) collective-permute-start(bf16[768,768]{0,1:T(8,128)(2,1)} %copy.81), channel_id=1, source_target_pairs={{0,1},{1,0},{2,3},{3,2},{4,5},{5,4},{6,7},{7,6},{8,9},{9,8},{10,11... | collective-permute-start | bytes 3538952 | tf_op jit(solution)/shard_map/ppermute | solution.py:929
  45.9 52.5 %collective-permute-start.2 = (bf16[768,768]{1,0:T(8,128)(2,1)}, bf16[768,768]{1,0:T(8,128)(2,1)S(1)}, u32[]{:S(2)}, u32[]{:S(2)}) collective-permute-start(bf16[768,768]{1,0:T(8,128)(2,1)} %collective-permute-done.1), channel_id=1, source_target_pairs={{0,2},{2,0},{4,6},{6,4},{8,10},{10,8},{12,14},{14,12},{16,18},{18,... | collective-permute-start | bytes 3538952 | tf_op jit(solution)/shard_map/ppermute | solution.py:934
  48.8 40.5 %copy-start.19 = (f32[4,768]{1,0:T(4,128)}, f32[4,768]{1,0:T(4,128)S(1)}, u32[]{:S(2)}) copy-start(f32[4,768]{1,0:T(4,128)S(1)} %slice.367.refs_7_) | copy-start | bytes 36868
  57.9 35.1 %copy-start.11 = (bf16[768,768]{0,1:T(8,128)(2,1)S(1)}, bf16[768,768]{0,1:T(8,128)(2,1)}, u32[]{:S(2)}) copy-start(bf16[768,768]{0,1:T(8,128)(2,1)} %copy.81) | copy-start | bytes 3538948
  89.3 39.7 %collective-permute-start.6 = (bf16[64,768]{1,0:T(8,128)(2,1)}, bf16[64,768]{1,0:T(8,128)(2,1)}, u32[]{:S(2)}, u32[]{:S(2)}) collective-permute-start(bf16[64,768]{1,0:T(8,128)(2,1)} %get-tuple-element.160), channel_id=1, source_target_pairs={{0,1},{1,0},{2,3},{3,2},{4,5},{5,4},{6,7},{7,6},{8,9},{9,8},{10,11... | collective-permute-start | bytes 294920 | tf_op jit(solution)/shard_map/ppermute | solution.py:929
  101.3 27.0 %copy-start.21 = (f32[16,1664]{1,0:T(8,128)S(1)}, f32[16,1664]{1,0:T(8,128)}, u32[]{:S(2)}) copy-start(f32[16,1664]{1,0:T(8,128)} %constant_dynamic-update-slice_fusion.4) | copy-start | bytes 319492
  101.3 27.8 %copy-start.29 = (f32[16,128]{1,0:T(8,128)S(1)}, f32[16,128]{1,0:T(8,128)}, u32[]{:S(2)}) copy-start(f32[16,128]{1,0:T(8,128)} %get-tuple-element.185) | copy-start | bytes 24580
  128.1 4.4 collective-permute-start.5
  133.2 75.2 %copy-start.7 = (bf16[768,768]{1,0:T(8,128)(2,1)S(1)}, bf16[768,768]{1,0:T(8,128)(2,1)}, u32[]{:S(2)}) copy-start(bf16[768,768]{1,0:T(8,128)(2,1)} %get-tuple-element.246.refs_4_) | copy-start | bytes 3538948
  226.7 11.3 %collective-permute-start.8 = (bf16[64,1536]{1,0:T(8,128)(2,1)}, bf16[64,1536]{1,0:T(8,128)(2,1)S(1)}, u32[]{:S(2)}, u32[]{:S(2)}) collective-permute-start(bf16[64,1536]{1,0:T(8,128)(2,1)} %get-tuple-element.166), channel_id=1, source_target_pairs={{0,1},{1,0},{2,3},{3,2},{4,5},{5,4},{6,7},{7,6},{8,9},{9,8},{10,11... | collective-permute-start | bytes 589832 | tf_op jit(solution)/shard_map/ppermute | solution.py:929
  238.7 133.0 %copy-start.18 = (bf16[768,24]{0,1:T(8,128)(2,1)S(1)}, bf16[768,24]{0,1:T(8,128)(2,1)}, u32[]{:S(2)}) copy-start(bf16[768,24]{0,1:T(8,128)(2,1)} %copy-done.17) | copy-start | bytes 110596
  380.0 5.2 collective-permute-start.9
  382.4 11.8 %slice-start = ((s8[6291456]{0:T(1024)(128)(4,1)}), s8[4194304]{0:T(1024)(128)(4,1)S(1)}, s32[]{:S(2)}) async-start(s8[6291456]{0:T(1024)(128)(4,1)} %bitcast.70), calls=%async_computation | async-start | bytes 8388608
  406.9 15.9 %copy-start.28 = (f32[512]{0:T(512)S(1)}, f32[512]{0:T(512)}, u32[]{:S(2)}) copy-start(f32[512]{0:T(512)} %fusion.35) | copy-start | bytes 6148
  (29 other events, 134.5 us)

commit v3 on v2

--- a/solution.py
+++ b/solution.py
@@ -14,6 +14,8 @@
 PAD = 16
 GROUP = 32
 TAPS = 4
+LANES = 128
+SLACK = 2
 EPS = 1e-05
 LOG2E = float(np.log2(np.e))
 BF = jnp.bfloat16
@@ -56,6 +58,25 @@
 
 
 SMEM = pl.BlockSpec(memory_space=pltpu.SMEM)
+
+
+def cost(micros):
+    return pl.CostEstimate(flops=int(micros * 1e9), bytes_accessed=1024, transcendentals=0)
+
+
+def side(a, b):
+    return jnp.concatenate([a, b], axis=1)
+
+
+def high_low(v):
+    hi = v.astype(BF)
+    return side(hi, (v - hi.astype(F32)).astype(BF))
+
+
+def by_pairs(maps, axis):
+    pairs = maps[0].shape[axis] // 128
+    pieces = [np.split(m, pairs, axis=axis) for m in maps]
+    return np.concatenate([piece[p] for p in range(pairs) for piece in pieces], axis=axis)
 
 
 def expanders(heads):
@@ -259,6 +280,7 @@
             pltpu.VMEM((8, width), F32),
         ],
         compiler_params=pltpu.CompilerParams(vmem_limit_bytes=58 * 1024 * 1024),
+        cost_estimate=cost(28),
         name="project",
     )(*args)
 
@@ -282,7 +304,7 @@
 
 def mix_body(
     sc, gates, xpres, ffs, sbls, pbs, sfds, sbds,
-    bc_r, col_r, row_r, hid, gout, ow, owt, ggain, skip, e0, e1, e2,
+    bc_r, col_r, row_r, hid, gout, ow, owt, ggain, skip, e01, e2,
     out_o, gnorm_o, dy_o, dgate_o, sf_o, sb_o, gbl_o, pg_o, dff_o,
     gft_o, gbt_o, pgf_o, pgb_o, hand_o, ggain_o, skip_o,
     sf_s, gb_s, gf_s, pg_s, q_s, y_s, dgn_s, exp_s,
@@ -293,7 +315,7 @@
     first = jnp.where(lax.rem(place, length) == 0, 0.0, 1.0)
     last = jnp.where(lax.rem(place + SPAN, length) == 0, 0.0, 1.0)
     live = jnp.where(lax.div(place, length) < sc[2], 1.0, 0.0)
-    width = e0.shape[1]
+    width = e2.shape[1]
     pairs = width // 128
 
     @pl.when(i == 0)
@@ -335,13 +357,12 @@
     squares = jnp.zeros((SPAN, 128), F32)
     for p in range(pairs):
         sl = slice(p * 128, (p + 1) * 128)
-        efd = dot(wmix, e0[:, sl])
-        ef = efd[:SPAN]
-        eb = dot(wtok, e1[:, sl])
+        efd = dot(wmix, e01[:, p * 256 : (p + 1) * 256])
+        ef, eb = efd[:SPAN, :128], efd[:SPAN, 128:]
         dte = dot(wtok, e2[:, sl])
         exp_s[0, :, sl] = ef
         exp_s[1, :, sl] = eb
-        decay = efd[SPAN : SPAN + 1] + efd[SPAN + 8 : SPAN + 9]
+        decay = efd[SPAN : SPAN + 1, :128] + efd[SPAN + 8 : SPAN + 9, :128]
         exp_s[2, 0:8, sl] = jnp.broadcast_to(decay, (8, 128))
         sf = sf_s[:, sl] * first
         sfb = sf.astype(BF)
@@ -367,7 +388,8 @@
             )
             ms.append((aff * jnp.exp2(spread)).astype(BF))
         y = dot(jnp.concatenate(ms, axis=1), bd)
-        y = y + ef * dot(cm, sfb) + eb * dot(cm, sbb) + skip[:, sl] * x
+        carried = dot(cm, side(sfb, sbb))
+        y = y + ef * carried[:, :128] + eb * carried[:, 128:] + skip[:, sl] * x
         y_s[:, sl] = y
         g = gate[:, at].astype(F32)
         gated = y * (g * sigmoid(g))
@@ -403,8 +425,8 @@
         xp = xpres(p)[0][:, at].astype(F32)
         skip_o[:, sl] += jnp.sum(dy * (xp * sigmoid(xp)), axis=0, keepdims=True)
         decay = exp_s[2, 0:1, sl]
-        dff = dot(ct, (exp_s[0, :, sl] * dy).astype(BF))
-        dfb = dot(ct, (exp_s[1, :, sl] * dy).astype(BF))
+        states = dot(ct, side(exp_s[0, :, sl] * dy, exp_s[1, :, sl] * dy).astype(BF))
+        dff, dfb = states[:, :128], states[:, 128:]
         dff_o[0, :, sl] = dff.astype(BF)
         q = q_s[0:1, sl]
         gf_s[:, sl] = gf_s[:, sl] + q * dff
@@ -425,10 +447,10 @@
         hand_o[...] = jnp.where(sc[0] == 0, gb_s[...], gf_s[...]).astype(BF)
 
 
-def mix(sc, split, bc, col, row, hidden, out_grad, ow, owt, ggain, skip, e0, e1, e2):
+def mix(sc, split, bc, col, row, hidden, out_grad, ow, owt, ggain, skip, e01, e2):
     tokens, width_in = hidden.shape
     groups = len(split[0])
-    width = e0.shape[1]
+    width = e2.shape[1]
     part = width // groups
     blocks = tokens // SPAN
 
@@ -456,7 +478,7 @@
         (sds((1, width), F32), full((1, width))),
         (sds((1, width), F32), full((1, width))),
     ]
-    shared = [ow, owt, ggain, skip, e0, e1, e2]
+    shared = [ow, owt, ggain, skip, e01, e2]
     in_specs = [SMEM]
     for shape in (
         (SPAN, part), (SPAN, part), (1, STATE, part), (1, STATE, part), (1, 8, part),
@@ -482,6 +504,7 @@
             pltpu.VMEM((3, SPAN, width), F32),
         ],
         compiler_params=pltpu.CompilerParams(vmem_limit_bytes=58 * 1024 * 1024),
+        cost_estimate=cost(60),
         name="mix",
     )(sc, *[a for kind in split for a in kind], bc, col, row, hidden, out_grad, *shared)
 
@@ -496,9 +519,9 @@
 def back_body(
     heads, sc, xpres, vs, gfds, gbds,
     dy_r, bc_r, ps_r, pspre_r, col_r, row_r, sf_r, sb_r, gbl, pg, dff,
-    skip, cv, cs, nad, e0, e1, e2, seg, tris, rect,
+    skip, cv, cs, nad, e01, seg4, seg2, segs, tris,
     dv_o, dst_o, dz_o, cvg_o, csg_o, head_o, edge_o, edges_o,
-    gf_s, edge_s, edges_s, da_s,
+    gf_s, edge_s, edges_s, da_s, cross_s,
 ):
     step = pl.program_id(0)
     blocks = pl.num_programs(0)
@@ -506,7 +529,7 @@
     length = sc[1]
     place = sc[0] + i * SPAN
     last = jnp.where(lax.rem(place + SPAN, length) == 0, 0.0, 1.0)
-    width = e0.shape[1]
+    width = e01.shape[1] // 2
     pairs = width // 128
 
     @pl.when(step == 0)
@@ -531,9 +554,9 @@
     w = jnp.where(lane < 64, jnp.exp2(jnp.where(lane < 32, col, end1[0:1] - col)), col)
     dec = jnp.exp2(end)
     high = dec.astype(BF).astype(F32)
-    wmix = jnp.concatenate([w, high, dec - high], axis=0).astype(BF)
-    wtok = wmix[:SPAN]
-    winn = jnp.exp2(jnp.where(lane < 32, end[0:1] - col, col)).astype(BF)
+    inner = jnp.exp2(jnp.where(lane < 32, end[0:1] - col, col))
+    steps = pltpu.roll(col, 64, 1)
+    wall = jnp.concatenate([w, inner, steps, high, dec - high], axis=0).astype(BF)
     bc = bc_r[...]
     bmf, cmf = bc[:, :STATE], bc[:, STATE:]
     bm, cm = bmf.astype(BF), cmf.astype(BF)
@@ -544,19 +567,18 @@
 
     daff = jnp.zeros((SPAN, SPAN), F32)
     red = jnp.zeros((SPAN, 128), F32)
+    whole = jnp.zeros((SPAN, 128), F32)
     ddt = jnp.zeros((SPAN, 128), F32)
-    span_sum = jnp.zeros((8, 128), F32)
     dc = jnp.zeros((SPAN, STATE), F32)
     db = jnp.zeros((SPAN, STATE), F32)
     for p in range(pairs):
         sl = slice(p * 128, (p + 1) * 128)
-        efd = dot(wmix, e0[:, sl])
-        ef = efd[:SPAN]
-        decay = efd[SPAN : SPAN + 1] + efd[SPAN + 8 : SPAN + 9]
-        eb = dot(wtok, e1[:, sl])
-        dte = dot(wtok, e2[:, sl])
-        wf = dot(winn, e0[:, sl])
-        wb = dot(winn, e1[:, sl])
+        two = slice(p * 256, (p + 1) * 256)
+        efd = dot(wall, e01[:, two])
+        ef, eb = efd[:SPAN, :128], efd[:SPAN, 128:]
+        wf, wb = efd[SPAN : 2 * SPAN, :128], efd[SPAN : 2 * SPAN, 128:]
+        dte = efd[2 * SPAN : 3 * SPAN, :128]
+        decay = efd[3 * SPAN : 3 * SPAN + 1, :128] + efd[3 * SPAN + 8 : 3 * SPAN + 9, :128]
         sf, sb = sf_r[0, :, sl], sb_r[0, :, sl]
         gf32 = gf_s[:, sl] * last
         gbd, at = gbds(p)
@@ -565,8 +587,7 @@
         gf, gb = gf32.astype(BF), gb32.astype(BF)
         gf_s[:, sl] = gf32 * decay + dff[0, :, sl].astype(F32)
         cross = (sf.astype(F32) * gf32 + sb.astype(F32) * gb32) * decay
-        crossed = jnp.broadcast_to(jnp.sum(cross, axis=0, keepdims=True), (8, 128))
-        span_sum = span_sum + dot(crossed.astype(BF), seg[4, sl, :])
+        cross_s[:, sl] = jnp.broadcast_to(jnp.sum(cross, axis=0, keepdims=True), (8, 128))
         xp = xpres(p)[0][:, at].astype(F32)
         sg = sigmoid(xp)
         x = xp * sg
@@ -574,14 +595,15 @@
         dy = dy_r[:, sl].astype(F32)
         efdy, ebdy = ef * dy, eb * dy
         wfxd, wbxd = wf * xd, wb * xd
-        cf = wf * dot(bm, gf)
-        cb = wb * dot(bm, gb)
-        dc = dc + dot_nt(efdy.astype(BF), sf) + dot_nt(ebdy.astype(BF), sb)
-        db = db + dot_nt(wfxd.astype(BF), gf) + dot_nt(wbxd.astype(BF), gb)
-        red = red + dot((efdy * dot(cm, sf)).astype(BF), seg[0, sl, :])
-        red = red + dot((ebdy * dot(cm, sb)).astype(BF), seg[1, sl, :])
-        red = red + dot((xd * cf).astype(BF), seg[2, sl, :])
-        red = red + dot((xd * cb).astype(BF), seg[3, sl, :])
+        s_both, g_both = side(sf, sb), side(gf, gb)
+        fed = dot(bm, g_both)
+        cf, cb = wf * fed[:, :128], wb * fed[:, 128:]
+        carried = dot(cm, s_both)
+        edy = side(efdy, ebdy)
+        dc = dc + dot_nt(edy.astype(BF), s_both)
+        db = db + dot_nt(side(wfxd, wbxd).astype(BF), g_both)
+        products = side((edy * carried).astype(BF), side(xd * cf, xd * cb).astype(BF))
+        red = red + dot(products, seg4[p * 512 : (p + 1) * 512, :])
         bd = jnp.concatenate(
             [jnp.where(low_half, dy, 0.0), jnp.where(low_half, 0.0, dy)], axis=0
         ).astype(BF)
@@ -598,13 +620,15 @@
             ms.append(m.astype(BF))
             dmh = dm[:, k * 128 : (k + 1) * 128]
             daff = daff + f * dmh
-            sums = dot((m * dmh).astype(BF), rect[...])
-            inside = jnp.where(
-                square_r < lane, sums[:, :SPAN], jnp.where(off, sums[:, SPAN:], 0.0)
-            )
-            da_s[h : h + 1, :] = jnp.sum(inside, axis=0, keepdims=True)
+            q = m * dmh
+            ql = jnp.where(square_r < lane, q, 0.0)
+            qu = q - ql
+            da_s[h : h + 1, :] = jnp.sum(ql, axis=0, keepdims=True)
+            da_s[GROUP + h : GROUP + h + 1, :] = jnp.sum(qu, axis=0, keepdims=True)
+            whole = jnp.where(lane == h, jnp.sum(ql, axis=1, keepdims=True), whole)
+            whole = jnp.where(lane == GROUP + h, jnp.sum(qu, axis=1, keepdims=True), whole)
         dxd = dot(jnp.concatenate(ms, axis=1), bd) + cf + cb
-        ddt = ddt + dot((x * dxd).astype(BF), seg[4, sl, :])
+        ddt = ddt + dot(high_low(x * dxd), seg2[two, :])
         dx = dte * dxd + skip[:, sl] * dy
         dxp = dx * (sg * (1.0 + xp * (1.0 - sg)))
         ext = jnp.concatenate([dxp, edge_s[:, sl] * last], axis=0)
@@ -636,6 +660,7 @@
         csg_o[k : k + 1, :] += jnp.sum(ps * moved, axis=0, keepdims=True)
     dst_o[...] = dst.astype(BF)
 
+    red = red - whole + jnp.transpose(da_s[...])
     hi = red.astype(BF)
     lo = (red - hi.astype(F32)).astype(BF)
     summed = dot(tris[...], hi) + dot(tris[...], lo)
@@ -643,10 +668,12 @@
     picked = jnp.where(
         lane < 32, parts[0], jnp.where(lane < 64, parts[1], jnp.where(lane < 96, parts[2], parts[3]))
     )
-    picked = picked + jnp.transpose(da_s[...])
     total = picked + pltpu.roll(picked, 64, 1)
     total = total + pltpu.roll(total, 32, 1)
-    da = total + span_sum[0:1]
+    crossed = cross_s[...]
+    crossed_hi = crossed.astype(BF)
+    crossed_lo = (crossed - crossed_hi.astype(F32)).astype(BF)
+    da = total + (dot(crossed_hi, segs[...]) + dot(crossed_lo, segs[...]))[0:1]
     dz = (ddt + da * nad[...]) * col
     dz = jnp.where((lane >= 96) & (lane < 96 + heads), dz, 0.0)
     dz_o[...] = dz.astype(BF)
@@ -666,13 +693,15 @@
     blocks = tokens // SPAN
     maps = expanders(heads)
     every = sum(maps)
-    seg = np.stack([m.T for m in maps] + [every.T])
+    seg4 = by_pairs([m.T for m in maps], 0)
+    seg2 = by_pairs([every.T, every.T], 0)
+    segs = every.T
     at = np.arange(SPAN)
     row_at, col_at = at[:, None], at[None, :]
     tris = np.concatenate(
         [col_at >= row_at, col_at <= row_at, col_at < row_at, col_at > row_at], axis=0
     ).astype(np.float32)
-    rect = np.concatenate([row_at >= col_at, row_at <= col_at], axis=1).astype(np.float32)
+    e01 = by_pairs(maps[:2], 1)
 
     def rev(shape):
         rank = len(shape)
@@ -691,7 +720,7 @@
         (sds((8, 128), F32), full((8, 128))),
     ]
     shared = [skip, cv, cs, nad]
-    shared += [jnp.asarray(m, BF) for m in (*maps[:3], seg, tris, rect)]
+    shared += [jnp.asarray(m, BF) for m in (e01, seg4, seg2, segs, tris)]
     in_specs = [SMEM] + [rev((SPAN, part))] * (2 * groups)
     in_specs += [full((STATE, part))] * (2 * groups)
     in_specs += [rev((SPAN, width))] + [rev((SPAN, 128))] * 5
@@ -708,8 +737,10 @@
             pltpu.VMEM((8, width), F32),
             pltpu.VMEM((8, 128), F32),
             pltpu.VMEM((128, 128), F32),
+            pltpu.VMEM((8, width), F32),
         ],
         compiler_params=pltpu.CompilerParams(vmem_limit_bytes=58 * 1024 * 1024),
+        cost_estimate=cost(100),
         name="back",
     )(
         sc, *[a for kind in split for a in kind],
@@ -717,12 +748,59 @@
     )
 
 
+def input_kernel(groups, *refs):
+    refs = list(refs)
+    wgs, wvs = (refs[:groups], refs[groups : 2 * groups])
+    dgate, dv, dst, dz, ws, wst, gain, hid, gout, grad_o, gain_o = refs[2 * groups :]
+
+    @pl.when(pl.program_id(0) == 0)
+    def _():
+        gain_o[...] = jnp.zeros_like(gain_o)
+
+    dn = dot_nt(dst[...], ws[...]) + dot_nt(dz[...], wst[...])
+    for k in range(groups):
+        part = wgs[k].shape[1]
+        cut = slice(k * part, (k + 1) * part)
+        dn = dn + dot_nt(dgate[:, cut], wgs[k][...]) + dot_nt(dv[:, cut], wvs[k][...])
+    u = hid[...].astype(F32)
+    scale = lax.rsqrt(jnp.mean(u * u, axis=1, keepdims=True) + EPS)
+    unit = u * scale
+    gain_o[...] += jnp.sum(dn * unit, axis=0, keepdims=True)
+    du = dn * gain[...]
+    inner = jnp.mean(du * unit, axis=1, keepdims=True)
+    grad_o[...] = (gout[...].astype(F32) + scale * (du - unit * inner)).astype(BF)
+
+
+def input_side(wgs, wvs, dgate, dv, dst, dz, ws, wst, gain, hidden, out_grad):
+    tokens, width_in = hidden.shape
+    tile = min(512, tokens)
+
+    def rows(a):
+        return pl.BlockSpec((tile, a.shape[1]), lambda i: (i, 0))
+
+    sds = jax.ShapeDtypeStruct
+    fixed = [*wgs, *wvs]
+    streams = [dgate, dv, dst, dz]
+    specs = [full(a.shape) for a in fixed] + [rows(a) for a in streams]
+    specs += [full(a.shape) for a in (ws, wst, gain)] + [rows(hidden), rows(out_grad)]
+    return pl.pallas_call(
+        functools.partial(input_kernel, len(wgs)),
+        grid=(tokens // tile,),
+        in_specs=specs,
+        out_specs=[rows(hidden), full((1, width_in))],
+        out_shape=[sds((tokens, width_in), BF), sds((1, width_in), F32)],
+        compiler_params=pltpu.CompilerParams(vmem_limit_bytes=58 * 1024 * 1024),
+        cost_estimate=cost(15),
+        name="input_side",
+    )(*fixed, *streams, ws, wst, gain, hidden, out_grad)
+
+
 def reduce_kernel(bits, lanes, mats, *refs):
     n_mats = len(mats)
     srcs, both, tiny = refs[:n_mats], refs[n_mats], refs[n_mats + 1]
-    outs = refs[n_mats + 2 : 2 * n_mats + 2]
-    both_o, tiny_o = refs[2 * n_mats + 2], refs[2 * n_mats + 3]
-    scratch = refs[2 * n_mats + 4 :]
+    paired_o, last_o, both_o, tiny_o = refs[n_mats + 2 : n_mats + 6]
+    outs = (*refs[n_mats + 6 : n_mats + 8], last_o)
+    scratch = refs[n_mats + 8 :]
     own_r, sent = scratch[0], scratch[1]
     halves, parts = scratch[2 : 2 + bits], scratch[2 + bits : 1 + 2 * bits]
     tiny_r, tiny_s, send_s, recv_s, tsend_s, trecv_s = scratch[1 + 2 * bits :]
@@ -741,24 +819,24 @@
     pl.semaphore_wait(barrier, bits + 1)
 
     chunks = [(m, s) for m in range(n_mats) for s in range(0, width, lanes)]
-    extra = len(chunks)
-    n = extra + 1
+    mains = len(chunks)
+    n = mains + both.shape[1] // lanes
     half = rows // 2
 
     def mult(v):
         return pl.multiple_of(v, 16)
 
     def source(c, which, part):
-        if c == extra:
-            return both.at[pl.ds(mult(part * half), half), :]
+        if c >= mains:
+            return both.at[pl.ds(mult(part * half), half), pl.ds((c - mains) * lanes, lanes)]
         m, s = chunks[c]
         if mats[m] == "cols":
             return srcs[m].at[pl.ds(mult(part * half), half), pl.ds(which * width + s, lanes)]
         return srcs[m].at[pl.ds(mult(which * rows + part * half), half), pl.ds(s, lanes)]
 
     def target(c, start, size):
-        if c == extra:
-            return both_o.at[pl.ds(mult(start), size), :]
+        if c >= mains:
+            return both_o.at[pl.ds(mult(start), size), pl.ds((c - mains) * lanes, lanes)]
         m, s = chunks[c]
         return outs[m].at[pl.ds(mult(start), size), pl.ds(s, lanes)]
 
@@ -777,7 +855,7 @@
         offset.append(offset[-1] + bit[k] * (half >> k))
 
     def first(c, which):
-        if c == extra and which == 0:
+        if c >= mains and which == 0:
             return None
         slot = own_r.at[c, which]
         return copy(source(c, which, 1 - bit[0]), slot, c, which, partner[0])
@@ -810,7 +888,7 @@
             second(c).start()
         elif s == 2:
             second(c).wait_recv()
-            if c == extra:
+            if c >= mains:
                 total = f32(sent.at[c]) + f32(halves[0].at[c])
             else:
                 first(c, 0).wait_recv()
@@ -847,9 +925,9 @@
 
     tiny_copy(0).start()
     last = 2 * bits + 1
-    for tick in range(n + last):
+    for tick in range(n + SLACK * last):
         for s in range(last, -1, -1):
-            c = tick - s
+            c = tick - SLACK * s
             if 0 <= c < n:
                 stage(c, s)
         if 1 <= tick <= bits + 1:
@@ -863,6 +941,15 @@
             else:
                 tiny_o[...] = total
 
+    low_half = lanes_of(rows) < HEAD_DIM
+    for p in range(width // 128):
+        sl = slice(p * 128, (p + 1) * 128)
+        g, v = f32(outs[0].at[:, sl]), f32(outs[1].at[:, sl])
+        paired_o[:, 2 * p * 128 : (2 * p + 1) * 128] = jnp.where(low_half, g, pltpu.roll(v, 64, 1))
+        paired_o[:, (2 * p + 1) * 128 : (2 * p + 2) * 128] = jnp.where(
+            low_half, pltpu.roll(g, 64, 1), v
+        )
+
     for c in range(n):
         for which in (0, 1):
             rdma = first(c, which)
@@ -883,10 +970,11 @@
     rows = arrays[0].shape[0] if kinds[0] == "cols" else arrays[0].shape[0] // 2
     width = arrays[0].shape[1] // 2 if kinds[0] == "cols" else arrays[0].shape[1]
     half = rows // 2
-    n = len(arrays) * (width // lanes) + 1
+    n = len(arrays) * (width // lanes) + both.shape[1] // lanes
     vmem = pl.BlockSpec(memory_space=pltpu.VMEM)
     sds = jax.ShapeDtypeStruct
-    scratch = [pltpu.VMEM((n, 2, half, lanes), BF), pltpu.VMEM((n, half, lanes), BF)]
+    scratch = [pltpu.VMEM((rows, width), BF)] * 2
+    scratch += [pltpu.VMEM((n, 2, half, lanes), BF), pltpu.VMEM((n, half, lanes), BF)]
     scratch += [pltpu.VMEM((n, half >> k, lanes), BF) for k in range(bits)]
     scratch += [pltpu.VMEM((n, half >> k, lanes), BF) for k in range(bits - 1)]
     scratch += [
@@ -899,10 +987,11 @@
     ]
     return pl.pallas_call(
         functools.partial(reduce_kernel, bits, lanes, kinds),
-        out_shape=[sds((rows, width), BF)] * len(arrays)
-        + [sds(both.shape, BF), sds(tiny.shape, F32)],
+        out_shape=[
+            sds((rows, 2 * width), F32), sds((rows, width), BF), sds(both.shape, BF), sds(tiny.shape, F32)
+        ],
         in_specs=[vmem] * (len(arrays) + 2),
-        out_specs=[vmem] * (len(arrays) + 2),
+        out_specs=[vmem] * 4,
         scratch_shapes=scratch,
         compiler_params=pltpu.CompilerParams(
             collective_id=0, has_side_effects=True, vmem_limit_bytes=58 * 1024 * 1024
@@ -970,25 +1059,36 @@
     def step_matrix(steps):
         return jnp.tile(jnp.pad(steps, ((0, 0), (0, GROUP - steps.shape[1]))), (1, 4))
 
-    e0, e1, e2, _ = [jnp.asarray(e, BF) for e in expanders(heads)]
+    each_map = expanders(heads)
+    e0, e1, e2, _ = [jnp.asarray(e, BF) for e in each_map]
+    e01 = jnp.asarray(by_pairs(each_map[:2], 1), BF)
     maps = (gain, state_weight, state_conv)
     if paired:
         first_core = lax.axis_index("dp") % 2 == 0
-        come = swap(jnp.where(first_core, wg, wv))
-        small_b = swap(small)
-        wstep = jnp.concatenate([step_weight, swap(step_weight)], axis=1)
-        ow_b = swap(out_weight)
+        payload, edge = lax.optimization_barrier((jnp.where(first_core, wg, wv), edge))
+        come = swap(payload)
+        small_b, wstep_b, ow_b = swap(small), swap(step_weight), swap(out_weight)
+        gate, v, xpre, ff, sbl, pb, _, _, _, _, hand, vh, normed, nedge, ps, pspre, bc, psh = project(
+            sc, hidden_in, edge, wg, wv, step_matrix(step_weight), value_conv,
+            spread_heads(step_bias), spread_heads(-jnp.exp(decay_log) * LOG2E),
+            e0[:, :local], e1[:, :local], maps=maps, final=False,
+        )
+        come, small_b, wstep_b, ow_b, nedge, hand = lax.optimization_barrier(
+            (come, small_b, wstep_b, ow_b, nedge, hand)
+        )
         also = core_swap(come)
+        enter_b = swap(hand)
         wgs = [wg, jnp.where(first_core, come, also)]
         wvs = [wv, jnp.where(first_core, also, come)]
         smalls = [small, small_b]
+        wstep = jnp.concatenate([step_weight, wstep_b], axis=1)
         ow = jnp.concatenate([out_weight, ow_b], axis=0)
     else:
         wgs = [lax.all_gather(wg, "chan", axis=1, tiled=True)]
         wvs = [lax.all_gather(wv, "chan", axis=1, tiled=True)]
         gathered = lax.all_gather(small, "chan", axis=0)
+        smalls = [gathered[k] for k in range(shards)]
         wstep = lax.all_gather(step_weight, "chan", axis=1, tiled=True)
-        smalls = [gathered[k] for k in range(shards)]
         ow = lax.all_gather(out_weight, "chan", axis=0, tiled=True)
 
     def heads_row(k, parts):
@@ -1002,12 +1102,6 @@
     nad = -jnp.exp(dlog_all)
 
     if paired:
-        gate, v, xpre, ff, sbl, pb, _, _, _, _, hand, vh, normed, nedge, ps, pspre, bc, psh = project(
-            sc, hidden_in, edge, wg, wv, step_matrix(step_weight), value_conv,
-            spread_heads(step_bias), spread_heads(-jnp.exp(decay_log) * LOG2E),
-            e0[:, :local], e1[:, :local], maps=maps, final=False,
-        )
-        enter_b = swap(hand)
         gate2, v2, xpre2, ff2, sbl2, pb2, _, _, _, _, hand2, vh2, col, row = project(
             sc, normed, nedge, wgs[1], wvs[1], step_matrix(wstep), smalls[1][:TAPS],
             spread_heads(bias_all), spread_heads(nad * LOG2E),
@@ -1031,7 +1125,7 @@
         vs, xs = [v], [xpre]
     (
         output, gnorm, dy, dgate, sf, sb, gbl, pg, dff, gft, gbt, pgf, pgb, hand, ggain_grad, skip_grad,
-    ) = mix(sc, split, bc, col, row, hidden_in, out_grad, ow, ow.T, ggain, skip, e0, e1, e2)
+    ) = mix(sc, split, bc, col, row, hidden_in, out_grad, ow, ow.T, ggain, skip, e01, e2)
     if paired:
         enter = swap(hand)
         enter = [enter[:, local:], enter[:, :local]]
@@ -1044,6 +1138,21 @@
     live = jnp.where(own_ids // length < count, 1.0, 0.0)[:, None].astype(BF)
     ow_grad = dot_tn(gnorm, out_grad * live).astype(BF)
     dwg = dot_tn(normed, dgate).astype(BF)
+
+    def absolute(parts, axis):
+        if not paired:
+            return jnp.concatenate(parts, axis=axis)
+        a = jnp.concatenate(parts, axis=axis)
+        b = jnp.concatenate(parts[::-1], axis=axis)
+        return jnp.where(channel == 0, a, b)
+
+    def shared(v, axis):
+        if paired:
+            a, b = jnp.split(v, 2, axis=axis)
+            v = (a.astype(F32) + swap(b).astype(F32)).astype(BF)
+        else:
+            v = lax.psum_scatter(v, "chan", scatter_dimension=axis, tiled=True)
+        return lax.psum(v, "dp")
 
     dv, dst, dz, cvg, csg, head_sums, edge_g, edges_g = back(
         heads, sc, [xs, vs, gfds, gbds], dy, bc, ps, pspre, col, row, sf, sb, gbl, pg, dff, skip, cv,
@@ -1078,17 +1187,9 @@
     dws = dot_tn(normed, dst)
     dwst = dot_tn(normed, dz)[:, 96 : 96 + heads]
     wst_tail = jnp.pad(wstep, ((0, 0), (96, GROUP - heads)))
-    dn = dot_nt(dst, state_weight) + dot_nt(dz, wst_tail)
-    for k, (a, b) in enumerate(zip(wgs, wvs)):
-        cut = slice(k * a.shape[1], (k + 1) * a.shape[1])
-        dn = dn + dot_nt(dgate[:, cut], a) + dot_nt(dv[:, cut], b)
-    u = hidden_in.astype(F32)
-    scale = lax.rsqrt(jnp.mean(u * u, axis=1, keepdims=True) + EPS)
-    unit = u * scale
-    norm_gain_grad = jnp.sum(dn * unit, axis=0)
-    du = dn * gain
-    inner = jnp.mean(du * unit, axis=1, keepdims=True)
-    input_grad = (out_grad.astype(F32) + scale * (du - unit * inner)).astype(BF)
+    input_grad, norm_gain_grad = input_side(
+        wgs, wvs, dgate, dv, dst, dz, state_weight, wst_tail, gain, hidden_in, out_grad
+    )
 
     bias_sum = head_sums[1, 96 : 96 + heads]
     dlog_sum = head_sums[0, 64 : 64 + heads]
@@ -1100,43 +1201,26 @@
             [cvg[:, cut].reshape(-1), ggain_grad[0, cut], bias_sum[hcut], dlog_sum[hcut], skip_sum[hcut]]
         )
 
-    def absolute(parts, axis):
-        if not paired:
-            return jnp.concatenate(parts, axis=axis)
-        a = jnp.concatenate(parts, axis=axis)
-        b = jnp.concatenate(parts[::-1], axis=axis)
-        return jnp.where(channel == 0, a, b)
-
     each = (TAPS + 1) * local + 3 * local_heads
     pad_each = -each % 128
     tiny = absolute([jnp.pad(by_shard(k), (0, pad_each)) for k in range(shards)], 0)
-    tiny = jnp.concatenate([tiny, norm_gain_grad, csg.reshape(-1)])
+    tiny = jnp.concatenate([tiny, norm_gain_grad[0], csg.reshape(-1)])
     tiny = jnp.pad(tiny, (0, -tiny.shape[0] % 1024)).reshape(-1, 128)
     dwst = absolute([dwst[:, k * local_heads : (k + 1) * local_heads] for k in range(shards)], 1)
     both = jnp.concatenate([dws, jnp.pad(dwst, ((0, 0), (0, 128 - heads)))], axis=1).astype(BF)
 
     bits = groups_dp.bit_length() - 1
     if paired and groups_dp == 2**bits and bits >= 2 and width_in % (16 * groups_dp) == 0:
-        dwg, dwv, owg, both, tiny = reduce_all(
-            bits, [(dwg, "cols"), (dwv, "cols"), (ow_grad, "rows")], both, tiny, 256
+        gvw, owg, both, tiny = reduce_all(
+            bits, [(dwg, "cols"), (dwv, "cols"), (ow_grad, "rows")], both, tiny, LANES
         )
-        dwg, dwv, owg = dwg.astype(F32), dwv.astype(F32), owg.astype(F32)
+        gvw = gvw.reshape(width_in, local_heads, 2 * HEAD_DIM)
+        owg = owg.astype(F32)
     else:
-
-        def shared(v, axis):
-            if paired:
-                parts = jnp.split(v, 2, axis=axis)
-                v = absolute(parts, axis)
-            v = lax.psum_scatter(v, "chan", scatter_dimension=axis, tiled=True)
-            return lax.psum(v, "dp").astype(F32)
-
-        dwg, dwv, owg = shared(dwg, 1), shared(dwv, 1), shared(ow_grad, 0)
+        dwg, dwv, owg = shared(dwg, 1), shared(dwv, 1), shared(ow_grad, 0).astype(F32)
         both, tiny = lax.psum((both, tiny), ("dp", "chan"))
-
-    gvw = jnp.stack(
-        [dwg.reshape(width_in, local_heads, HEAD_DIM), dwv.reshape(width_in, local_heads, HEAD_DIM)],
-        axis=2,
-    ).reshape(width_in, local_heads, 2 * HEAD_DIM)
+        pieces = [a.reshape(width_in, local_heads, HEAD_DIM) for a in (dwg, dwv)]
+        gvw = jnp.concatenate(pieces, axis=2).astype(F32)
     both = both.astype(F32)
     flat = tiny.reshape(-1)
     base = (each + pad_each) * shards

time: 561 us -> 489 us (0.87)
  matrix products: 67.3 us -> 31.2 us
  Pallas kernels: 358 us -> 342 us
  waiting for transfers between devices: 16.1 us -> 4.25 us
  other arithmetic: 33.6 us -> 23.3 us
    dot_general x6 -> x0, matrix products: 42.2 us -> none  [dot_nt(): lax.dot_general(a, b, (((1,), (1,)), ((), ())), preferred_element_type=F32)]
    pallas_call x1, Pallas kernels: 131 us -> 105 us  [back(): pl.pallas_call(functools.partial(back_kernel, heads, groups), grid=(block...]
    pallas_call x0 -> x1, Pallas kernels: none -> 19.3 us  [input_side(): pl.pallas_call(functools.partial(input_kernel, len(wgs)), grid=(tokens //...]
    ppermute x7, waiting for transfers between devices: 14.2 us -> 1.08 us  [swap(): return lax.ppermute(v, 'chan', [(0, 1), (1, 0)])]
    pallas_call x1, Pallas kernels: 94.1 us -> 85 us  [reduce_all(): pl.pallas_call(functools.partial(reduce_kernel, bits, lanes, kinds), out_...]
    convert_element_type x2 -> x1, other arithmetic: 8.75 us -> 1.58 us  [on_device(): owg = owg.astype(F32)]
    dot_general x5, matrix products: 25.1 us -> 31.2 us  [dot_tn(): lax.dot_general(a, b, (((0,), (0,)), ((), ())), preferred_element_type=F32)]
    unnamed x95 -> x83, local copies, waits for them, and re-layouts: 20 us -> 19.2 us
  transfers between devices with their start and end apart: 10 -> 10, of which waited for: 3 -> 2; matrix products, arithmetic and copies ran while one was open for 8% -> 13% of each run, Pallas kernels for 11% -> 12%
where the time goes in v3:
time: 489 us; the launch traced here: 480 us
  Pallas kernels  342 us (70%)
  local copies, waits for them, and re-layouts  62.7 us (13%)
  matrix products  31.2 us (6%)
  other arithmetic  23.3 us (5%)
  starting transfers between devices  13.7 us (3%)
    pallas_call x1, Pallas kernels, back(): pl.pallas_call(functools.partial(back_kernel, heads, groups), grid=(block...  105 us
    pallas_call x1, Pallas kernels, reduce_all(): pl.pallas_call(functools.partial(reduce_kernel, bits, lanes, kinds), out_...  85 us
    pallas_call x1, Pallas kernels, mix(): pl.pallas_call(functools.partial(mix_kernel, groups), grid=(blocks,), in_...  74.4 us
    pallas_call x2, Pallas kernels, project(): pl.pallas_call(functools.partial(project_kernel, fresh, final, tile, chun...  58.2 us
    dot_general x5, matrix products, dot_tn(): lax.dot_general(a, b, (((0,), (0,)), ((), ())), preferred_element_type=F32)  31.2 us
    pallas_call x1, Pallas kernels, input_side(): pl.pallas_call(functools.partial(input_kernel, len(wgs)), grid=(tokens //...  19.3 us
    unnamed x83, local copies, waits for them, and re-layouts  19.2 us
  transfers between devices with their start and end apart: 10, of which 2 were waited for; matrix products, arithmetic and copies ran while one was open for 13% of the time, Pallas kernels for 12%

profile of v3, /device:TPU:1, one launch (start us, length us, event | category | flops | bytes accessed | tf_op | source)
XLA Modules:
  0.0 480.5 jit_solution(8122432589142987833)
XLA Ops:
  2.2 4.5 collective-permute-start
  14.5 3.1 fusion.18
  17.6 4.0 copy.97
  21.5 2.4 copy.78.refs_4_.refs_0_
  23.9 2.1 copy.98
  26.1 1.7 copy.79.refs_5_.refs_2_
  37.6 31.4 %project.2 = (bf16[2048,768]{1,0:T(8,128)(2,1)}, bf16[2048,768]{1,0:T(8,128)(2,1)}, bf16[2048,768]{1,0:T(8,128)(2,1)}, bf16[16,64,768]{2,1,0:T(8,128)(2,1)}, bf1...) custom-call(s32[7]{0:T(128)} %stack.30.refs_0_, ...), custom_call_target="tpu_custom_call" | custom-call | flops 28000000000 | bytes 1024 | tf_op jit(solution)/shard_map/project/pallas_call | solution.py:270
  74.1 2.1 collective-permute-start.5
  79.8 3.0 fusion.16
  82.8 2.5 copy.86.refs_20_
  89.4 3.2 broadcast_select_fusion
  92.6 26.9 %project.3 = (bf16[2048,768]{1,0:T(8,128)(2,1)}, bf16[2048,768]{1,0:T(8,128)(2,1)}, bf16[2048,768]{1,0:T(8,128)(2,1)}, bf16[16,64,768]{2,1,0:T(8,128)(2,1)}, bf1...) custom-call(s32[7]{0:T(128)} %stack.30.refs_0_, ...), custom_call_target="tpu_custom_call" | custom-call | flops 28000000000 | bytes 1024 | tf_op jit(solution)/shard_map/project/pallas_call | solution.py:270
  124.7 74.4 %mix.1 = (bf16[2048,768]{1,0:T(8,128)(2,1)}, bf16[2048,1536]{1,0:T(8,128)(2,1)}, bf16[2048,1536]{1,0:T(8,128)(2,1)}, bf16[2048,1536]{1,0:T(8,128)(2,1)}, bf16[16...) custom-call(s32[7]{0:T(128)} %stack.30.refs_0_, ...), custom_call_target="tpu_custom_call" | custom-call | flops 60000002048 | bytes 1024 | tf_op jit(solution)/shard_map/mix/pallas_call | solution.py:490
  202.1 9.4 %convolution_convert_fusion.2.refs_0_ = bf16[768,1536]{1,0:T(8,128)(2,1)} fusion(bf16[2048,768]{1,0:T(8,128)(2,1)} %get-tuple-element.157.refs_1_.refs_2_, bf16[2048,1536]{1,0:T(8,128)(2,1)} %get-tuple-element.181.refs_4_), kind=kOutput, calls=%fused_computation.2 | convolution fusion | flops 4833017856 | bytes 11796480 | tf_op jit(solution)/shard_map/dot_general | solution.py:34
  211.5 6.9 %convolution_convert_fusion.refs_2_ = bf16[1536,768]{1,0:T(8,128)(2,1)} fusion(bf16[2048,1536]{1,0:T(8,128)(2,1)S(1)} %copy-done.36, bf16[2048,768]{1,0:T(8,128)(2,1)S(1)} %copy-done.31, bf16[2048]{0:T(1024)(128)(2,1)S(1)} %copy-done.18), kind=kOutput, calls=%fused_computation | convolution fusion | flops 4834590720 | bytes 11800576 | tf_op jit(solution)/shard_map/dot_general | solution.py:34
  219.1 105.4 %back.1 = (bf16[2048,1536]{1,0:T(8,128)(2,1)}, bf16[2048,128]{1,0:T(8,128)(2,1)}, bf16[2048,128]{1,0:T(8,128)(2,1)}, f32[4,1536]{1,0:T(4,128)}, f32[4,128]{1,0:T...) custom-call(s32[7]{0:T(128)} %stack.30.refs_0_, ...), custom_call_target="tpu_custom_call" | custom-call | flops 99999997952 | bytes 1024 | tf_op jit(solution)/shard_map/back/pallas_call | solution.py:729
  329.3 2.7 fusion.26
  334.2 3.2 collective-permute-done.9
  339.0 2.9 convolution_convert_fusion.3
  341.9 9.4 %convolution_convert_fusion.1.refs_1_ = bf16[768,1536]{1,0:T(8,128)(2,1)} fusion(bf16[2048,768]{1,0:T(8,128)(2,1)S(1)} %copy-done.35, bf16[2048,1536]{1,0:T(8,128)(2,1)} %fusion.5.refs_5_), kind=kOutput, calls=%fused_computation.1 | convolution fusion | flops 4833017856 | bytes 11796480 | tf_op jit(solution)/shard_map/dot_general | solution.py:34
  351.3 19.3 %input_side.1 = (bf16[2048,768]{1,0:T(8,128)(2,1)}, f32[1,768]{1,0:T(1,128)}) custom-call(bf16[768,768]{1,0:T(8,128)(2,1)} %copy.78.refs_4_.refs_0_, bf16[768,768]{1,0:T(8,128)(2,1)} %get-tuple-element.262.refs_4_.refs_1_, bf16[768,768]{1,0:T(8,128)(2,1)} %copy-done.3, bf16[768,768]{1,0:T(8,128)(2,1)} %get-tuple-element.261.refs_5_.refs_3_, ...), custom_call_target="tpu_custom_call" | custom-call | flops 15000000512 | bytes 1024 | tf_op jit(solution)/shard_map/input_side/pallas_call | solution.py:786
  372.8 85.0 %reduce_all.1 = (f32[768,1536]{1,0:T(8,128)}, bf16[768,768]{1,0:T(8,128)(2,1)}, bf16[768,256]{1,0:T(8,128)(2,1)}, f32[72,128]{1,0:T(8,128)}) custom-call(bf16[768,1536]{1,0:T(8,128)(2,1)} %convolution_convert_fusion.2.refs_0_, bf16[768,1536]{1,0:T(8,128)(2,1)} %convolution_convert_fusion.1.refs_1_, bf16[1536,768]{1,0:T(8,128)(2,1)} %convolution_convert_fusion.refs_2_, ...), custom_call_target="tpu_custom_call" | custom-call | tf_op jit(solution)/shard_map/reduce_all/pallas_call | solution.py:988
  460.3 6.1 %copy.93 = f32[768,1536]{0,1:T(8,128)} copy(f32[768,1536]{1,0:T(8,128)} %get-tuple-element.210) | data formatting | bytes 9437184 | tf_op jit(solution)/shard_map/reduce_all/pallas_call | solution.py:988
  466.4 6.1 %copy.94 = f32[768,12,128]{2,0,1:T(8,128)} copy(f32[768,12,128]{0,2,1:T(8,128)} %bitcast.54) | data formatting | bytes 9437184
  (192 shorter events, 60.1 us)
Async XLA Ops:
  0.6 13.8 %copy-start = (bf16[768,12,128]{2,0,1:T(8,128)(2,1)S(1)}, bf16[768,12,128]{2,0,1:T(8,128)(2,1)}, u32[]{:S(2)}) copy-start(bf16[768,12,128]{2,0,1:T(8,128)(2,1)} %param.42) | copy-start | bytes 7077892
  2.2 34.0 %collective-permute-start = (bf16[16,768]{1,0:T(8,128)(2,1)}, bf16[16,768]{1,0:T(8,128)(2,1)}, u32[]{:S(2)}, u32[]{:S(2)}) collective-permute-start(bf16[16,768]{1,0:T(8,128)(2,1)} %slice.290), channel_id=1, source_target_pairs={{0,1},{2,3},{4,5},{6,7},{8,9},{10,11},{12,13},{14,15},{16,17},{18,... | collective-permute-start | bytes 73736 | tf_op jit(solution)/shard_map/ppermute | solution.py:1049
  9.5 61.0 %collective-permute-start.2 = (f32[6,768]{1,0:T(8,128)}, f32[6,768]{1,0:T(8,128)}, u32[]{:S(2)}, u32[]{:S(2)}) collective-permute-start(f32[6,768]{1,0:T(8,128)} %pad_maximum_fusion.4), channel_id=1, source_target_pairs={{0,1},{1,0},{2,3},{3,2},{4,5},{5,4},{6,7},{7,6},{8,9},{9,8},{10,11... | collective-permute-start | bytes 55304 | tf_op jit(solution)/shard_map/ppermute | solution.py:1018
  11.0 59.4 %collective-permute-start.4 = (bf16[768,768]{0,1:T(8,128)(2,1)S(1)}, bf16[768,768]{0,1:T(8,128)(2,1)}, u32[]{:S(2)}, u32[]{:S(2)}) collective-permute-start(bf16[768,768]{0,1:T(8,128)(2,1)S(1)} %copy.83), channel_id=1, source_target_pairs={{0,1},{1,0},{2,3},{3,2},{4,5},{5,4},{6,7},{7,6},{8,9},{9,8},{10,11... | collective-permute-start | bytes 3538952 | tf_op jit(solution)/shard_map/ppermute | solution.py:1018
  12.6 57.9 %collective-permute-start.3 = (bf16[768,12]{0,1:T(8,128)(2,1)}, bf16[768,12]{0,1:T(8,128)(2,1)}, u32[]{:S(2)}, u32[]{:S(2)}) collective-permute-start(bf16[768,12]{0,1:T(8,128)(2,1)} %param.44), channel_id=1, source_target_pairs={{0,1},{1,0},{2,3},{3,2},{4,5},{5,4},{6,7},{7,6},{8,9},{9,8},{10,11... | collective-permute-start | bytes 55304 | tf_op jit(solution)/shard_map/ppermute | solution.py:1018
  27.7 9.9 %copy-start.3 = (bf16[768,768]{1,0:T(8,128)(2,1)}, bf16[768,768]{1,0:T(8,128)(2,1)S(1)}, u32[]{:S(2)}) copy-start(bf16[768,768]{1,0:T(8,128)(2,1)S(1)} %copy.79.refs_5_.refs_2_) | copy-start | bytes 3538948
  36.2 36.4 %copy-start.9 = (bf16[768,12]{0,1:T(8,128)(2,1)S(1)}, bf16[768,12]{0,1:T(8,128)(2,1)}, u32[]{:S(2)}) copy-start(bf16[768,12]{0,1:T(8,128)(2,1)} %param.44) | copy-start | bytes 55300
  36.2 40.9 %copy-start.22 = (f32[12]{0:T(128)S(1)}, f32[12]{0:T(128)}, u32[]{:S(2)}) copy-start(f32[12]{0:T(128)} %get-tuple-element.285) | copy-start | bytes 148
  36.2 40.9 %copy-start.23 = (f32[12]{0:T(128)S(1)}, f32[12]{0:T(128)}, u32[]{:S(2)}) copy-start(f32[12]{0:T(128)} %get-tuple-element.286) | copy-start | bytes 148
  36.2 42.9 %copy-start.27 = (f32[12]{0:T(128)S(1)}, f32[12]{0:T(128)}, u32[]{:S(2)}) copy-start(f32[12]{0:T(128)} %get-tuple-element.287) | copy-start | bytes 148
  36.2 34.3 %collective-permute-start.1 = (bf16[768,768]{1,0:T(8,128)(2,1)}, bf16[768,768]{1,0:T(8,128)(2,1)}, u32[]{:S(2)}, u32[]{:S(2)}) collective-permute-start(bf16[768,768]{1,0:T(8,128)(2,1)} %broadcast_select_fusion.2), channel_id=1, source_target_pairs={{0,1},{1,0},{2,3},{3,2},{4,5},{5,4},{6,7},{7,6},{8,9},{9,8},{10,11... | collective-permute-start | bytes 3538952 | tf_op jit(solution)/shard_map/ppermute | solution.py:1018
  71.2 17.5 %copy-start.8 = (f32[4,768]{1,0:T(4,128)}, f32[4,768]{1,0:T(4,128)S(1)}, u32[]{:S(2)}) copy-start(f32[4,768]{1,0:T(4,128)S(1)} %slice.293.refs_7_) | copy-start | bytes 36868
  74.1 15.2 %collective-permute-start.5 = (bf16[768,768]{1,0:T(8,128)(2,1)}, bf16[768,768]{1,0:T(8,128)(2,1)}, u32[]{:S(2)}, u32[]{:S(2)}) collective-permute-start(bf16[768,768]{1,0:T(8,128)(2,1)} %collective-permute-done.1), channel_id=1, source_target_pairs={{0,2},{2,0},{4,6},{6,4},{8,10},{10,8},{12,14},{14,12},{16,18},{18,... | collective-permute-start | bytes 3538952 | tf_op jit(solution)/shard_map/ppermute | solution.py:1023
  86.0 37.0 %collective-permute-start.7 = (bf16[64,768]{1,0:T(8,128)(2,1)S(1)}, bf16[64,768]{1,0:T(8,128)(2,1)S(1)}, u32[]{:S(2)}, u32[]{:S(2)}) collective-permute-start(bf16[64,768]{1,0:T(8,128)(2,1)S(1)} %copy-done.32), channel_id=1, source_target_pairs={{0,1},{1,0},{2,3},{3,2},{4,5},{5,4},{6,7},{7,6},{8,9},{9,8},{10,11... | collective-permute-start | bytes 294920 | tf_op jit(solution)/shard_map/ppermute | solution.py:1018
  92.6 29.8 %copy-start.16 = (f32[16,128]{1,0:T(8,128)S(1)}, f32[16,128]{1,0:T(8,128)}, u32[]{:S(2)}) copy-start(f32[16,128]{1,0:T(8,128)} %get-tuple-element.203) | copy-start | bytes 24580
  119.4 4.6 collective-permute-start.6
  199.1 19.3 %collective-permute-start.8 = (bf16[64,1536]{1,0:T(8,128)(2,1)}, bf16[64,1536]{1,0:T(8,128)(2,1)S(1)}, u32[]{:S(2)}, u32[]{:S(2)}) collective-permute-start(bf16[64,1536]{1,0:T(8,128)(2,1)} %get-tuple-element.184), channel_id=1, source_target_pairs={{0,1},{1,0},{2,3},{3,2},{4,5},{5,4},{6,7},{7,6},{8,9},{9,8},{10,11... | collective-permute-start | bytes 589832 | tf_op jit(solution)/shard_map/ppermute | solution.py:1018
  202.0 9.4 %copy-start.18 = (bf16[2048]{0:T(1024)(128)(2,1)S(1)}, bf16[2048]{0:T(1024)(128)(2,1)}, u32[]{:S(2)}) copy-start(bf16[2048]{0:T(1024)(128)(2,1)} %select_convert_fusion.1) | copy-start | bytes 12292
  202.1 9.4 %copy-start.31 = (bf16[2048,768]{1,0:T(8,128)(2,1)S(1)}, bf16[2048,768]{1,0:T(8,128)(2,1)}, u32[]{:S(2)}) copy-start(bf16[2048,768]{1,0:T(8,128)(2,1)} %refs_12_.1) | copy-start | bytes 9437188
  202.1 9.4 %copy-start.36 = (bf16[2048,1536]{1,0:T(8,128)(2,1)S(1)}, bf16[2048,1536]{1,0:T(8,128)(2,1)}, u32[]{:S(2)}) copy-start(bf16[2048,1536]{1,0:T(8,128)(2,1)} %get-tuple-element.199) | copy-start | bytes 18874372
  328.5 8.9 %copy-start.11 = (f32[1664]{0:T(1024)S(1)}, f32[1664]{0:T(1024)}, u32[]{:S(2)}) copy-start(f32[1664]{0:T(1024)} %get-tuple-element.253) | copy-start | bytes 19972
  328.5 8.9 %copy-start.12 = (f32[1664]{0:T(1024)S(1)}, f32[1664]{0:T(1024)}, u32[]{:S(2)}) copy-start(f32[1664]{0:T(1024)} %get-tuple-element.254) | copy-start | bytes 19972
  332.5 4.9 %collective-permute-start.9 = (f32[8,1664]{1,0:T(8,128)S(1)}, f32[8,1664]{1,0:T(8,128)S(1)}, u32[]{:S(2)}, u32[]{:S(2)}) collective-permute-start(f32[8,1664]{1,0:T(8,128)S(1)} %pad_maximum_fusion.2), channel_id=1, source_target_pairs={{1,0},{3,2},{5,4},{7,6},{9,8},{11,10},{13,12},{15,14},{17,16},{19,... | collective-permute-start | bytes 159752 | tf_op jit(solution)/shard_map/ppermute | solution.py:1169
  337.5 13.8 %copy-start.30 = (bf16[2048,128]{1,0:T(8,128)(2,1)}, bf16[2048,128]{1,0:T(8,128)(2,1)S(1)}, u32[]{:S(2)}) copy-start(bf16[2048,128]{1,0:T(8,128)(2,1)S(1)} %fusion.12.refs_6_) | copy-start | bytes 1572868
  (23 other events, 122.3 us)

commit v4 on v3

--- a/solution.py
+++ b/solution.py
@@ -79,6 +79,11 @@
     return np.concatenate([piece[p] for p in range(pairs) for piece in pieces], axis=axis)
 
 
+def unpaired(a, b):
+    low = lanes_of(a.shape[0]) < HEAD_DIM
+    return jnp.where(low, a, pltpu.roll(b, 64, 1)), jnp.where(low, pltpu.roll(a, 64, 1), b)
+
+
 def expanders(heads):
     channel = np.arange(heads * HEAD_DIM) // HEAD_DIM
     lane = np.arange(128)[:, None]
@@ -91,7 +96,7 @@
     def take(count):
         return [refs.pop(0) for _ in range(count)]
 
-    sc, tokens_r, halo, edge, wg, wv, wst, cv, bias, nal, tri, e0, e1 = take(13)
+    sc, tokens_r, halo, edge, slabs, wst, cv, bias, nal, tri, e0, e1 = take(12)
     if fresh:
         gain, ws, cs = take(3)
     else:
@@ -175,8 +180,13 @@
 
     for c in range(width // chunk):
         cl = slice(c * chunk, (c + 1) * chunk)
-        gate_o[:, cl] = dot(own, wg[:, cl]).astype(BF)
-        v = dot(normed, wv[:, cl]) * keep_rows
+        parts = []
+        for h in range(c * chunk // HEAD_DIM, (c + 1) * chunk // HEAD_DIM, 2):
+            both = dot(normed, side(slabs[h], slabs[h + 1]))
+            parts.append(unpaired(both[:, :128], both[:, 128:]))
+        gates = jnp.concatenate([part[0][PAD:] for part in parts], axis=1)
+        gate_o[:, cl] = gates.astype(BF)
+        v = jnp.concatenate([part[1] for part in parts], axis=1) * keep_rows
         v_o[:, cl] = v[PAD:].astype(BF)
 
         @pl.when(at == 0)
@@ -219,10 +229,10 @@
         hand_o[...] = jnp.where(sc[0] == 0, sf_s[...], sb_s[...]).astype(BF)
 
 
-def project(sc, source, edge, wg, wv, wst, cv, bias, nal, e0, e1, maps=None, bc=None, final=True):
+def project(sc, source, edge, slabs, wst, cv, bias, nal, e0, e1, maps=None, bc=None, final=True):
     fresh = maps is not None
     tokens, width_in = source.shape
-    width = wg.shape[1]
+    width = slabs.shape[0] * HEAD_DIM
     tile = min(256, tokens)
     tiles = tokens // tile
     per = tile // SPAN
@@ -255,7 +265,7 @@
     if final:
         outs += [narrow, narrow]
     steps = tile // PAD
-    args = [sc, source, source, edge, wg, wv, wst, cv, bias, nal, tri, e0, e1]
+    args = [sc, source, source, edge, slabs, wst, cv, bias, nal, tri, e0, e1]
     in_specs = [
         SMEM,
         back((tile, width_in)),
@@ -304,7 +314,7 @@
 
 def mix_body(
     sc, gates, xpres, ffs, sbls, pbs, sfds, sbds,
-    bc_r, col_r, row_r, hid, gout, ow, owt, ggain, skip, e01, e2,
+    bc_r, col_r, row_r, hid, gout, ow, owt, ggain, skip, e01,
     out_o, gnorm_o, dy_o, dgate_o, sf_o, sb_o, gbl_o, pg_o, dff_o,
     gft_o, gbt_o, pgf_o, pgb_o, hand_o, ggain_o, skip_o,
     sf_s, gb_s, gf_s, pg_s, q_s, y_s, dgn_s, exp_s,
@@ -315,7 +325,7 @@
     first = jnp.where(lax.rem(place, length) == 0, 0.0, 1.0)
     last = jnp.where(lax.rem(place + SPAN, length) == 0, 0.0, 1.0)
     live = jnp.where(lax.div(place, length) < sc[2], 1.0, 0.0)
-    width = e2.shape[1]
+    width = e01.shape[1] // 2
     pairs = width // 128
 
     @pl.when(i == 0)
@@ -342,11 +352,10 @@
     row = row_r[...]
     end = jnp.broadcast_to(col[SPAN - 1 : SPAN], (8, 128))
     end1 = pltpu.roll(end, GROUP, 1)
-    w = jnp.where(lane < 64, jnp.exp2(jnp.where(lane < 32, col, end1[0:1] - col)), col)
+    w = jnp.exp2(jnp.where(lane < 32, col, end1[0:1] - col))
     dec = jnp.exp2(end)
     high = dec.astype(BF).astype(F32)
-    wmix = jnp.concatenate([w, high, dec - high], axis=0).astype(BF)
-    wtok = wmix[:SPAN]
+    wmix = jnp.concatenate([w, pltpu.roll(col, 64, 1), high, dec - high], axis=0).astype(BF)
     bc = bc_r[...]
     bmf, cmf = bc[:, :STATE], bc[:, STATE:]
     cm = cmf.astype(BF)
@@ -359,10 +368,10 @@
         sl = slice(p * 128, (p + 1) * 128)
         efd = dot(wmix, e01[:, p * 256 : (p + 1) * 256])
         ef, eb = efd[:SPAN, :128], efd[:SPAN, 128:]
-        dte = dot(wtok, e2[:, sl])
+        dte = efd[SPAN : 2 * SPAN, :128]
         exp_s[0, :, sl] = ef
         exp_s[1, :, sl] = eb
-        decay = efd[SPAN : SPAN + 1, :128] + efd[SPAN + 8 : SPAN + 9, :128]
+        decay = efd[2 * SPAN : 2 * SPAN + 1, :128] + efd[2 * SPAN + 8 : 2 * SPAN + 9, :128]
         exp_s[2, 0:8, sl] = jnp.broadcast_to(decay, (8, 128))
         sf = sf_s[:, sl] * first
         sfb = sf.astype(BF)
@@ -447,10 +456,10 @@
         hand_o[...] = jnp.where(sc[0] == 0, gb_s[...], gf_s[...]).astype(BF)
 
 
-def mix(sc, split, bc, col, row, hidden, out_grad, ow, owt, ggain, skip, e01, e2):
+def mix(sc, split, bc, col, row, hidden, out_grad, ow, owt, ggain, skip, e01):
     tokens, width_in = hidden.shape
     groups = len(split[0])
-    width = e2.shape[1]
+    width = e01.shape[1] // 2
     part = width // groups
     blocks = tokens // SPAN
 
@@ -478,7 +487,7 @@
         (sds((1, width), F32), full((1, width))),
         (sds((1, width), F32), full((1, width))),
     ]
-    shared = [ow, owt, ggain, skip, e01, e2]
+    shared = [ow, owt, ggain, skip, e01]
     in_specs = [SMEM]
     for shape in (
         (SPAN, part), (SPAN, part), (1, STATE, part), (1, STATE, part), (1, 8, part),
@@ -750,18 +759,21 @@
 
 def input_kernel(groups, *refs):
     refs = list(refs)
-    wgs, wvs = (refs[:groups], refs[groups : 2 * groups])
-    dgate, dv, dst, dz, ws, wst, gain, hid, gout, grad_o, gain_o = refs[2 * groups :]
+    slabs = refs[:groups]
+    dgate, dv, dst, dz, ws, wst, gain, hid, gout, grad_o, gain_o, wg, wv = refs[groups:]
 
     @pl.when(pl.program_id(0) == 0)
     def _():
         gain_o[...] = jnp.zeros_like(gain_o)
+        pairs_in = slabs[0].shape[0] // 2
+        for p in range(groups * pairs_in):
+            slab, h = slabs[p // pairs_in], 2 * (p % pairs_in)
+            g, v = unpaired(slab[h].astype(F32), slab[h + 1].astype(F32))
+            wg[:, p * 128 : (p + 1) * 128] = g.astype(BF)
+            wv[:, p * 128 : (p + 1) * 128] = v.astype(BF)
 
     dn = dot_nt(dst[...], ws[...]) + dot_nt(dz[...], wst[...])
-    for k in range(groups):
-        part = wgs[k].shape[1]
-        cut = slice(k * part, (k + 1) * part)
-        dn = dn + dot_nt(dgate[:, cut], wgs[k][...]) + dot_nt(dv[:, cut], wvs[k][...])
+    dn = dn + dot_nt(dgate[...], wg[...]) + dot_nt(dv[...], wv[...])
     u = hid[...].astype(F32)
     scale = lax.rsqrt(jnp.mean(u * u, axis=1, keepdims=True) + EPS)
     unit = u * scale
@@ -771,7 +783,7 @@
     grad_o[...] = (gout[...].astype(F32) + scale * (du - unit * inner)).astype(BF)
 
 
-def input_side(wgs, wvs, dgate, dv, dst, dz, ws, wst, gain, hidden, out_grad):
+def input_side(slabs, dgate, dv, dst, dz, ws, wst, gain, hidden, out_grad):
     tokens, width_in = hidden.shape
     tile = min(512, tokens)
 
@@ -779,16 +791,18 @@
         return pl.BlockSpec((tile, a.shape[1]), lambda i: (i, 0))
 
     sds = jax.ShapeDtypeStruct
-    fixed = [*wgs, *wvs]
+    fixed = list(slabs)
+    width = dgate.shape[1]
     streams = [dgate, dv, dst, dz]
     specs = [full(a.shape) for a in fixed] + [rows(a) for a in streams]
     specs += [full(a.shape) for a in (ws, wst, gain)] + [rows(hidden), rows(out_grad)]
     return pl.pallas_call(
-        functools.partial(input_kernel, len(wgs)),
+        functools.partial(input_kernel, len(slabs)),
         grid=(tokens // tile,),
         in_specs=specs,
         out_specs=[rows(hidden), full((1, width_in))],
         out_shape=[sds((tokens, width_in), BF), sds((1, width_in), F32)],
+        scratch_shapes=[pltpu.VMEM((width_in, width), BF)] * 2,
         compiler_params=pltpu.CompilerParams(vmem_limit_bytes=58 * 1024 * 1024),
         cost_estimate=cost(15),
         name="input_side",
@@ -945,10 +959,8 @@
     for p in range(width // 128):
         sl = slice(p * 128, (p + 1) * 128)
         g, v = f32(outs[0].at[:, sl]), f32(outs[1].at[:, sl])
-        paired_o[:, 2 * p * 128 : (2 * p + 1) * 128] = jnp.where(low_half, g, pltpu.roll(v, 64, 1))
-        paired_o[:, (2 * p + 1) * 128 : (2 * p + 2) * 128] = jnp.where(
-            low_half, pltpu.roll(g, 64, 1), v
-        )
+        paired_o[2 * p] = jnp.where(low_half, g, pltpu.roll(v, 64, 1))
+        paired_o[2 * p + 1] = jnp.where(low_half, pltpu.roll(g, 64, 1), v)
 
     for c in range(n):
         for which in (0, 1):
@@ -988,7 +1000,7 @@
     return pl.pallas_call(
         functools.partial(reduce_kernel, bits, lanes, kinds),
         out_shape=[
-            sds((rows, 2 * width), F32), sds((rows, width), BF), sds(both.shape, BF), sds(tiny.shape, F32)
+            sds((width // HEAD_DIM, rows, 128), F32), sds((rows, width), BF), sds(both.shape, BF), sds(tiny.shape, F32)
         ],
         in_specs=[vmem] * (len(arrays) + 2),
         out_specs=[vmem] * 4,
@@ -1036,7 +1048,7 @@
     local = local_heads * HEAD_DIM
     heads = local_heads * shards
     width = heads * HEAD_DIM
-    paired = shards == 2 and local % 128 == 0 and groups_dp % 2 == 0
+    paired = shards == 2 and local_heads % 4 == 0 and groups_dp % 2 == 0
     one = jnp.ones((), jnp.int32)
     flags = [channel, 1 - channel, 1 - channel, channel] if paired else [one] * 4
     sc = jnp.stack([channel * tokens, length, count] + flags).astype(jnp.int32)
@@ -1044,8 +1056,7 @@
     downs = [(k + 1, k) for k in range(shards - 1)]
     gain = norm_gain[None]
 
-    wg = gate_value_weight[:, :, :HEAD_DIM].reshape(width_in, local)
-    wv = gate_value_weight[:, :, HEAD_DIM:].reshape(width_in, local)
+    slab = gate_value_weight.transpose(1, 0, 2)
     edge = lax.ppermute(hidden_in[tokens - PAD :], "chan", ups)
     vec = jnp.concatenate([step_bias, decay_log, skip_gain])
     small = jnp.concatenate(
@@ -1060,16 +1071,17 @@
         return jnp.tile(jnp.pad(steps, ((0, 0), (0, GROUP - steps.shape[1]))), (1, 4))
 
     each_map = expanders(heads)
-    e0, e1, e2, _ = [jnp.asarray(e, BF) for e in each_map]
+    e0, e1, _, _ = [jnp.asarray(e, BF) for e in each_map]
     e01 = jnp.asarray(by_pairs(each_map[:2], 1), BF)
     maps = (gain, state_weight, state_conv)
     if paired:
-        first_core = lax.axis_index("dp") % 2 == 0
-        payload, edge = lax.optimization_barrier((jnp.where(first_core, wg, wv), edge))
+        core = lax.axis_index("dp") % 2
+        half = lax.dynamic_slice_in_dim(slab, core * (local_heads // 2), local_heads // 2, 0)
+        payload, edge = lax.optimization_barrier((half, edge))
         come = swap(payload)
         small_b, wstep_b, ow_b = swap(small), swap(step_weight), swap(out_weight)
         gate, v, xpre, ff, sbl, pb, _, _, _, _, hand, vh, normed, nedge, ps, pspre, bc, psh = project(
-            sc, hidden_in, edge, wg, wv, step_matrix(step_weight), value_conv,
+            sc, hidden_in, edge, slab, step_matrix(step_weight), value_conv,
             spread_heads(step_bias), spread_heads(-jnp.exp(decay_log) * LOG2E),
             e0[:, :local], e1[:, :local], maps=maps, final=False,
         )
@@ -1078,14 +1090,13 @@
         )
         also = core_swap(come)
         enter_b = swap(hand)
-        wgs = [wg, jnp.where(first_core, come, also)]
-        wvs = [wv, jnp.where(first_core, also, come)]
+        halves = jnp.where(core == 0, jnp.stack([come, also]), jnp.stack([also, come]))
+        slabs = [slab, halves.reshape(slab.shape)]
         smalls = [small, small_b]
         wstep = jnp.concatenate([step_weight, wstep_b], axis=1)
         ow = jnp.concatenate([out_weight, ow_b], axis=0)
     else:
-        wgs = [lax.all_gather(wg, "chan", axis=1, tiled=True)]
-        wvs = [lax.all_gather(wv, "chan", axis=1, tiled=True)]
+        slabs = [lax.all_gather(slab, "chan", axis=0, tiled=True)]
         gathered = lax.all_gather(small, "chan", axis=0)
         smalls = [gathered[k] for k in range(shards)]
         wstep = lax.all_gather(step_weight, "chan", axis=1, tiled=True)
@@ -1103,7 +1114,7 @@
 
     if paired:
         gate2, v2, xpre2, ff2, sbl2, pb2, _, _, _, _, hand2, vh2, col, row = project(
-            sc, normed, nedge, wgs[1], wvs[1], step_matrix(wstep), smalls[1][:TAPS],
+            sc, normed, nedge, slabs[1], step_matrix(wstep), smalls[1][:TAPS],
             spread_heads(bias_all), spread_heads(nad * LOG2E),
             e0[:, local:], e1[:, local:], bc=bc, final=True,
         )
@@ -1116,7 +1127,7 @@
             gate, v, xpre, ff, sbl, pb, sft, sbt, pft, pbt, _, vh, normed, nedge, ps, pspre, bc, psh,
             col, row,
         ) = project(
-            sc, hidden_in, edge, wgs[0], wvs[0], step_matrix(wstep), cv, spread_heads(bias_all),
+            sc, hidden_in, edge, slabs[0], step_matrix(wstep), cv, spread_heads(bias_all),
             spread_heads(nad * LOG2E), e0, e1, maps=maps,
         )
         sfd = handed(sft, pft, shards, True)
@@ -1125,7 +1136,7 @@
         vs, xs = [v], [xpre]
     (
         output, gnorm, dy, dgate, sf, sb, gbl, pg, dff, gft, gbt, pgf, pgb, hand, ggain_grad, skip_grad,
-    ) = mix(sc, split, bc, col, row, hidden_in, out_grad, ow, ow.T, ggain, skip, e01, e2)
+    ) = mix(sc, split, bc, col, row, hidden_in, out_grad, ow, ow.T, ggain, skip, e01)
     if paired:
         enter = swap(hand)
         enter = [enter[:, local:], enter[:, :local]]
@@ -1188,7 +1199,7 @@
     dwst = dot_tn(normed, dz)[:, 96 : 96 + heads]
     wst_tail = jnp.pad(wstep, ((0, 0), (96, GROUP - heads)))
     input_grad, norm_gain_grad = input_side(
-        wgs, wvs, dgate, dv, dst, dz, state_weight, wst_tail, gain, hidden_in, out_grad
+        slabs, dgate, dv, dst, dz, state_weight, wst_tail, gain, hidden_in, out_grad
     )
 
     bias_sum = head_sums[1, 96 : 96 + heads]
@@ -1214,7 +1225,7 @@
         gvw, owg, both, tiny = reduce_all(
             bits, [(dwg, "cols"), (dwv, "cols"), (ow_grad, "rows")], both, tiny, LANES
         )
-        gvw = gvw.reshape(width_in, local_heads, 2 * HEAD_DIM)
+        gvw = gvw.transpose(1, 0, 2)
         owg = owg.astype(F32)
     else:
         dwg, dwv, owg = shared(dwg, 1), shared(dwv, 1), shared(ow_grad, 0).astype(F32)

time: 489 us -> 473 us (0.967)
  local copies, waits for them, and re-layouts: 62.7 us -> 45 us
    pallas_call x1, Pallas kernels: 74.4 us -> 66 us  [mix(): pl.pallas_call(functools.partial(mix_kernel, groups), grid=(blocks,), in_...]
    unnamed x83 -> x67, local copies, waits for them, and re-layouts: 19.2 us -> 11.8 us
    pallas_call x1 -> x0, local copies, waits for them, and re-layouts: 6.11 us -> none  [reduce_all(): pl.pallas_call(functools.partial(reduce_kernel, bits, lanes, kinds), out_...]
  transfers between devices with their start and end apart: 10 -> 10, of which waited for: 2 -> 3; matrix products, arithmetic and copies ran while one was open for 13% -> 12% of each run, Pallas kernels for 12% -> 13%
where the time goes in v4:
time: 473 us; the launch traced here: 465 us
  Pallas kernels  340 us (72%)
  local copies, waits for them, and re-layouts  45 us (10%)
  matrix products  31.3 us (7%)
  other arithmetic  25.8 us (5%)
  starting transfers between devices  12.3 us (3%)
  waiting for transfers between devices  8.01 us (2%)
    pallas_call x1, Pallas kernels, back(): pl.pallas_call(functools.partial(back_kernel, heads, groups), grid=(block...  106 us
    pallas_call x1, Pallas kernels, reduce_all(): pl.pallas_call(functools.partial(reduce_kernel, bits, lanes, kinds), out_...  84.4 us
    pallas_call x1, Pallas kernels, mix(): pl.pallas_call(functools.partial(mix_kernel, groups), grid=(blocks,), in_...  66 us
    pallas_call x2, Pallas kernels, project(): pl.pallas_call(functools.partial(project_kernel, fresh, final, tile, chun...  62.6 us
    dot_general x5, matrix products, dot_tn(): lax.dot_general(a, b, (((0,), (0,)), ((), ())), preferred_element_type=F32)  31.3 us
    pallas_call x1, Pallas kernels, input_side(): pl.pallas_call(functools.partial(input_kernel, len(slabs)), grid=(tokens...  21.2 us
    unnamed x67, local copies, waits for them, and re-layouts  11.8 us
  transfers between devices with their start and end apart: 10, of which 3 were waited for; matrix products, arithmetic and copies ran while one was open for 12% of the time, Pallas kernels for 13%

profile of v4, /device:TPU:1, one launch (start us, length us, event | category | flops | bytes accessed | tf_op | source)
XLA Modules:
  0.0 465.1 jit_solution(13726563825457906614)
XLA Ops:
  2.0 4.5 collective-permute-start
  9.4 1.6 copy.63
  10.9 1.5 collective-permute-start.4
  19.8 1.7 copy.62.refs_5_
  26.0 33.6 %project.2 = (bf16[2048,768]{1,0:T(8,128)(2,1)}, bf16[2048,768]{1,0:T(8,128)(2,1)}, bf16[2048,768]{1,0:T(8,128)(2,1)}, bf16[16,64,768]{2,1,0:T(8,128)(2,1)}, bf1...) custom-call(s32[7]{0:T(128)} %stack.44.refs_0_, ...), custom_call_target="tpu_custom_call" | custom-call | flops 28000000000 | bytes 1024 | tf_op jit(solution)/shard_map/project/pallas_call | solution.py:280
  61.1 2.8 collective-permute-done.1
  67.6 1.6 collective-permute-start.5
  74.1 3.0 fusion.16
  77.1 2.5 copy.66.refs_20_
  84.9 4.3 maximum_select_fusion
  89.1 29.0 %project.3 = (bf16[2048,768]{1,0:T(8,128)(2,1)}, bf16[2048,768]{1,0:T(8,128)(2,1)}, bf16[2048,768]{1,0:T(8,128)(2,1)}, bf16[16,64,768]{2,1,0:T(8,128)(2,1)}, bf1...) custom-call(s32[7]{0:T(128)} %stack.44.refs_0_, ...), custom_call_target="tpu_custom_call" | custom-call | flops 28000000000 | bytes 1024 | tf_op jit(solution)/shard_map/project/pallas_call | solution.py:280
  120.5 2.0 collective-permute-done.6.refs_11_.refs_13_
  123.1 66.0 %mix.1 = (bf16[2048,768]{1,0:T(8,128)(2,1)}, bf16[2048,1536]{1,0:T(8,128)(2,1)}, bf16[2048,1536]{1,0:T(8,128)(2,1)}, bf16[2048,1536]{1,0:T(8,128)(2,1)}, bf16[16...) custom-call(s32[7]{0:T(128)} %stack.44.refs_0_, ...), custom_call_target="tpu_custom_call" | custom-call | flops 60000002048 | bytes 1024 | tf_op jit(solution)/shard_map/mix/pallas_call | solution.py:499
  191.1 9.4 %convolution_convert_fusion.2.refs_0_ = bf16[768,1536]{1,0:T(8,128)(2,1)} fusion(bf16[2048,768]{1,0:T(8,128)(2,1)} %get-tuple-element.157.refs_1_.refs_2_, bf16[2048,1536]{1,0:T(8,128)(2,1)} %get-tuple-element.181.refs_2_), kind=kOutput, calls=%fused_computation.2 | convolution fusion | flops 4833017856 | bytes 11796480 | tf_op jit(solution)/shard_map/dot_general | solution.py:34
  200.6 6.9 %convolution_convert_fusion.refs_2_ = bf16[1536,768]{1,0:T(8,128)(2,1)} fusion(bf16[2048,1536]{1,0:T(8,128)(2,1)S(1)} %copy-done.29, bf16[2048,768]{1,0:T(8,128)(2,1)S(1)} %copy-done.24, bf16[2048]{0:T(1024)(128)(2,1)S(1)} %copy-done.14), kind=kOutput, calls=%fused_computation | convolution fusion | flops 4834590720 | bytes 11800576 | tf_op jit(solution)/shard_map/dot_general | solution.py:34
  208.2 105.6 %back.1 = (bf16[2048,1536]{1,0:T(8,128)(2,1)}, bf16[2048,128]{1,0:T(8,128)(2,1)}, bf16[2048,128]{1,0:T(8,128)(2,1)}, f32[4,1536]{1,0:T(4,128)}, f32[4,128]{1,0:T...) custom-call(s32[7]{0:T(128)} %stack.44.refs_0_, ...), custom_call_target="tpu_custom_call" | custom-call | flops 99999997952 | bytes 1024 | tf_op jit(solution)/shard_map/back/pallas_call | solution.py:738
  318.7 2.7 fusion.25
  323.6 3.2 collective-permute-done.9
  328.4 2.9 convolution_convert_fusion.3
  331.3 9.4 %convolution_convert_fusion.1.refs_1_ = bf16[768,1536]{1,0:T(8,128)(2,1)} fusion(bf16[2048,768]{1,0:T(8,128)(2,1)S(1)} %copy-done.28, bf16[2048,1536]{1,0:T(8,128)(2,1)} %fusion.5.refs_3_), kind=kOutput, calls=%fused_computation.1 | convolution fusion | flops 4833017856 | bytes 11796480 | tf_op jit(solution)/shard_map/dot_general | solution.py:34
  340.7 21.2 %input_side.1 = (bf16[2048,768]{1,0:T(8,128)(2,1)}, f32[1,768]{1,0:T(1,128)}) custom-call(bf16[12,768,128]{2,1,0:T(8,128)(2,1)} %bitcast.64, bf16[12,768,128]{2,1,0:T(8,128)(2,1)} %bitcast.60, bf16[2048,1536]{1,0:T(8,128)(2,1)} %get-tuple-element.181.refs_2_, bf16[2048,1536]{1,0:T(8,128)(2,1)} %fusion.5.refs_3_, bf16[2048,128]{1,0:T(8,128)(2,1)} %copy-done.23, ...), custom_call_target="tpu_custom_call" | custom-call | flops 15000000512 | bytes 1024 | tf_op jit(solution)/shard_map/input_side/pallas_call | solution.py:799
  364.1 84.4 %reduce_all.1 = (f32[12,768,128]{2,1,0:T(8,128)}, bf16[768,768]{1,0:T(8,128)(2,1)}, bf16[768,256]{1,0:T(8,128)(2,1)}, f32[72,128]{1,0:T(8,128)}) custom-call(bf16[768,1536]{1,0:T(8,128)(2,1)} %convolution_convert_fusion.2.refs_0_, bf16[768,1536]{1,0:T(8,128)(2,1)} %convolution_convert_fusion.1.refs_1_, bf16[1536,768]{1,0:T(8,128)(2,1)} %convolution_convert_fusion.refs_2_, ...), custom_call_target="tpu_custom_call" | custom-call | tf_op jit(solution)/shard_map/reduce_all/pallas_call | solution.py:1000
  451.1 2.8 convert_element_type.49
  459.8 4.8 %copy.82 = f32[768,12,128]{2,0,1:T(8,128)} copy(f32[768,12,128]{2,0,1:T(8,128)} %bitcast.58) | data formatting | bytes 9437184
  (172 shorter events, 54.7 us)
Async XLA Ops:
  0.6 20.9 %copy-start.21 = (f32[12]{0:T(128)S(1)}, f32[12]{0:T(128)}, u32[]{:S(2)}) copy-start(f32[12]{0:T(128)} %param.46) | copy-start | bytes 148
  0.7 17.1 %copy-start.13 = (f32[768]{0:T(1024)S(1)}, f32[768]{0:T(1024)}, u32[]{:S(2)}) copy-start(f32[768]{0:T(1024)} %param.40) | copy-start | bytes 9220
  2.0 22.6 %collective-permute-start = (bf16[16,768]{1,0:T(8,128)(2,1)}, bf16[16,768]{1,0:T(8,128)(2,1)}, u32[]{:S(2)}, u32[]{:S(2)}) collective-permute-start(bf16[16,768]{1,0:T(8,128)(2,1)} %slice.282), channel_id=1, source_target_pairs={{0,1},{2,3},{4,5},{6,7},{8,9},{10,11},{12,13},{14,15},{16,17},{18,... | collective-permute-start | bytes 73736 | tf_op jit(solution)/shard_map/ppermute | solution.py:1060
  9.3 51.7 %collective-permute-start.2 = (f32[6,768]{1,0:T(8,128)}, f32[6,768]{1,0:T(8,128)}, u32[]{:S(2)}, u32[]{:S(2)}) collective-permute-start(f32[6,768]{1,0:T(8,128)} %pad_maximum_fusion.4), channel_id=1, source_target_pairs={{0,1},{1,0},{2,3},{3,2},{4,5},{5,4},{6,7},{7,6},{8,9},{9,8},{10,11... | collective-permute-start | bytes 55304 | tf_op jit(solution)/shard_map/ppermute | solution.py:1030
  10.9 50.2 %collective-permute-start.4 = (bf16[768,768]{0,1:T(8,128)(2,1)S(1)}, bf16[768,768]{0,1:T(8,128)(2,1)S(1)}, u32[]{:S(2)}, u32[]{:S(2)}) collective-permute-start(bf16[768,768]{0,1:T(8,128)(2,1)S(1)} %copy.63), channel_id=1, source_target_pairs={{0,1},{1,0},{2,3},{3,2},{4,5},{5,4},{6,7},{7,6},{8,9},{9,8},{10,11... | collective-permute-start | bytes 3538952 | tf_op jit(solution)/shard_map/ppermute | solution.py:1030
  12.5 48.6 %collective-permute-start.3 = (bf16[768,12]{0,1:T(8,128)(2,1)}, bf16[768,12]{0,1:T(8,128)(2,1)}, u32[]{:S(2)}, u32[]{:S(2)}) collective-permute-start(bf16[768,12]{0,1:T(8,128)(2,1)} %param.43), channel_id=1, source_target_pairs={{0,1},{1,0},{2,3},{3,2},{4,5},{5,4},{6,7},{7,6},{8,9},{9,8},{10,11... | collective-permute-start | bytes 55304 | tf_op jit(solution)/shard_map/ppermute | solution.py:1030
  24.7 39.3 %collective-permute-start.1 = (bf16[6,768,128]{2,1,0:T(8,128)(2,1)S(1)}, bf16[6,768,128]{2,1,0:T(8,128)(2,1)}, u32[]{:S(2)}, u32[]{:S(2)}) collective-permute-start(bf16[6,768,128]{2,1,0:T(8,128)(2,1)S(1)} %dynamic-slice_bitcast_fusion), channel_id=1, source_target_pairs={{0,1},{1,0},{2,3},{3,2},{4,5},{5,4},{6,7},{7,6},{8,9},{9,8},{10,11... | collective-permute-start | bytes 3538952 | tf_op jit(solution)/shard_map/ppermute | solution.py:1030
  26.0 39.9 %copy-start.5 = (bf16[768,12]{0,1:T(8,128)(2,1)S(1)}, bf16[768,12]{0,1:T(8,128)(2,1)}, u32[]{:S(2)}) copy-start(bf16[768,12]{0,1:T(8,128)(2,1)} %param.43) | copy-start | bytes 55300
  61.1 12.4 %copy-start.1 = (bf16[768,768]{0,1:T(8,128)(2,1)}, bf16[768,768]{0,1:T(8,128)(2,1)S(1)}, u32[]{:S(2)}) copy-start(bf16[768,768]{0,1:T(8,128)(2,1)S(1)} %collective-permute-done.4) | copy-start | bytes 3538948
  64.6 19.6 %copy-start.4 = (f32[4,768]{1,0:T(4,128)}, f32[4,768]{1,0:T(4,128)S(1)}, u32[]{:S(2)}) copy-start(f32[4,768]{1,0:T(4,128)S(1)} %slice.285.refs_6_) | copy-start | bytes 36868
  67.6 17.3 %collective-permute-start.5 = (bf16[6,768,128]{2,1,0:T(8,128)(2,1)}, bf16[6,768,128]{2,1,0:T(8,128)(2,1)}, u32[]{:S(2)}, u32[]{:S(2)}) collective-permute-start(bf16[6,768,128]{2,1,0:T(8,128)(2,1)} %collective-permute-done.1), channel_id=1, source_target_pairs={{0,2},{2,0},{4,6},{6,4},{8,10},{10,8},{12,14},{14,12},{16,18},{18,... | collective-permute-start | bytes 3538952 | tf_op jit(solution)/shard_map/ppermute | solution.py:1035
  80.3 40.1 %collective-permute-start.7 = (bf16[64,768]{1,0:T(8,128)(2,1)S(1)}, bf16[64,768]{1,0:T(8,128)(2,1)S(1)}, u32[]{:S(2)}, u32[]{:S(2)}) collective-permute-start(bf16[64,768]{1,0:T(8,128)(2,1)S(1)} %copy-done.25), channel_id=1, source_target_pairs={{0,1},{1,0},{2,3},{3,2},{4,5},{5,4},{6,7},{7,6},{8,9},{9,8},{10,11... | collective-permute-start | bytes 294920 | tf_op jit(solution)/shard_map/ppermute | solution.py:1030
  89.1 30.8 %copy-start.12 = (f32[16,128]{1,0:T(8,128)S(1)}, f32[16,128]{1,0:T(8,128)}, u32[]{:S(2)}) copy-start(f32[16,128]{1,0:T(8,128)} %get-tuple-element.203) | copy-start | bytes 24580
  118.1 4.4 collective-permute-start.6
  189.2 18.3 %collective-permute-start.8 = (bf16[64,1536]{1,0:T(8,128)(2,1)}, bf16[64,1536]{1,0:T(8,128)(2,1)S(1)}, u32[]{:S(2)}, u32[]{:S(2)}) collective-permute-start(bf16[64,1536]{1,0:T(8,128)(2,1)} %get-tuple-element.184), channel_id=1, source_target_pairs={{0,1},{1,0},{2,3},{3,2},{4,5},{5,4},{6,7},{7,6},{8,9},{9,8},{10,11... | collective-permute-start | bytes 589832 | tf_op jit(solution)/shard_map/ppermute | solution.py:1030
  191.1 9.5 %copy-start.14 = (bf16[2048]{0:T(1024)(128)(2,1)S(1)}, bf16[2048]{0:T(1024)(128)(2,1)}, u32[]{:S(2)}) copy-start(bf16[2048]{0:T(1024)(128)(2,1)} %select_convert_fusion.1) | copy-start | bytes 12292
  191.1 9.5 %copy-start.24 = (bf16[2048,768]{1,0:T(8,128)(2,1)S(1)}, bf16[2048,768]{1,0:T(8,128)(2,1)}, u32[]{:S(2)}) copy-start(bf16[2048,768]{1,0:T(8,128)(2,1)} %refs_10_.1) | copy-start | bytes 9437188
  191.1 9.4 %copy-start.29 = (bf16[2048,1536]{1,0:T(8,128)(2,1)S(1)}, bf16[2048,1536]{1,0:T(8,128)(2,1)}, u32[]{:S(2)}) copy-start(bf16[2048,1536]{1,0:T(8,128)(2,1)} %get-tuple-element.199) | copy-start | bytes 18874372
  317.9 8.9 %copy-start.6 = (f32[1664]{0:T(1024)S(1)}, f32[1664]{0:T(1024)}, u32[]{:S(2)}) copy-start(f32[1664]{0:T(1024)} %get-tuple-element.252) | copy-start | bytes 19972
  317.9 8.9 %copy-start.7 = (f32[1664]{0:T(1024)S(1)}, f32[1664]{0:T(1024)}, u32[]{:S(2)}) copy-start(f32[1664]{0:T(1024)} %get-tuple-element.253) | copy-start | bytes 19972
  317.9 8.9 %copy-start.8 = (f32[1664]{0:T(1024)S(1)}, f32[1664]{0:T(1024)}, u32[]{:S(2)}) copy-start(f32[1664]{0:T(1024)} %get-tuple-element.254) | copy-start | bytes 19972
  318.7 8.2 %copy-start.22 = (bf16[2048,128]{1,0:T(8,128)(2,1)S(1)}, bf16[2048,128]{1,0:T(8,128)(2,1)}, u32[]{:S(2)}) copy-start(bf16[2048,128]{1,0:T(8,128)(2,1)} %get-tuple-element.196) | copy-start | bytes 1572868
  321.9 4.9 %collective-permute-start.9 = (f32[8,1664]{1,0:T(8,128)S(1)}, f32[8,1664]{1,0:T(8,128)S(1)}, u32[]{:S(2)}, u32[]{:S(2)}) collective-permute-start(f32[8,1664]{1,0:T(8,128)S(1)} %pad_maximum_fusion.2), channel_id=1, source_target_pairs={{1,0},{3,2},{5,4},{7,6},{9,8},{11,10},{13,12},{15,14},{17,16},{19,... | collective-permute-start | bytes 159752 | tf_op jit(solution)/shard_map/ppermute | solution.py:1180
  326.9 13.8 %copy-start.23 = (bf16[2048,128]{1,0:T(8,128)(2,1)}, bf16[2048,128]{1,0:T(8,128)(2,1)S(1)}, u32[]{:S(2)}) copy-start(bf16[2048,128]{1,0:T(8,128)(2,1)S(1)} %fusion.12.refs_4_) | copy-start | bytes 1572868
  (16 other events, 88.7 us)

commit v5 on v4

--- a/solution.py
+++ b/solution.py
@@ -40,6 +40,10 @@
     )
 
 
+def fine(a, b):
+    return jnp.dot(a, b, precision=lax.Precision.HIGHEST, preferred_element_type=F32)
+
+
 def sigmoid(v):
     return 0.5 + 0.5 * jnp.tanh(0.5 * v)
 
@@ -58,6 +62,12 @@
 
 
 SMEM = pl.BlockSpec(memory_space=pltpu.SMEM)
+
+
+def placing(heads, groups=range(4)):
+    lane, head = np.arange(128)[None], np.arange(heads)[:, None]
+    hits = sum((lane == GROUP * g + head).astype(np.float32) for g in groups)
+    return jnp.asarray(hits)
 
 
 def cost(micros):
@@ -96,7 +106,7 @@
     def take(count):
         return [refs.pop(0) for _ in range(count)]
 
-    sc, tokens_r, halo, edge, slabs, wst, cv, bias, nal, tri, e0, e1 = take(12)
+    sc, tokens_r, halo, edge, slabs, steps_t, cv, hv, place_r, tri, e0, e1 = take(12)
     if fresh:
         gain, ws, cs = take(3)
     else:
@@ -106,7 +116,7 @@
         normed_o, nedge_o, ps_o, pspre_o, bc_o, psh_o = take(6)
     if final:
         col_o, row_o = take(2)
-    sb_s, pb_s, sf_s, pf_s = take(4)
+    sb_s, pb_s, sf_s, pf_s, wst, hv_s = take(6)
 
     step = pl.program_id(0)
     tiles = pl.num_programs(0)
@@ -122,6 +132,10 @@
         sf_s[...] = jnp.zeros_like(sf_s)
         pb_s[...] = jnp.ones_like(pb_s)
         pf_s[...] = jnp.ones_like(pf_s)
+        wst[...] = dot_tn(steps_t[...], place_r[...].astype(BF)).astype(BF)
+        rows_hv = fine(hv[...], place_r[...])
+        hv_s[0:1] = rows_hv[0:1]
+        hv_s[1:2] = -LOG2E * jnp.exp(rows_hv[1:2])
 
     before = jnp.where(at == 0, edge[...].astype(F32), halo[...].astype(F32))
     rows = jnp.concatenate([before, tokens_r[...].astype(F32)], axis=0)
@@ -153,9 +167,9 @@
         own = tokens_r[...]
         bc = bc_r[...]
 
-    z = dot(own, wst[...]) + bias[...]
+    z = dot(own, wst[...]) + hv_s[0:1]
     dt = jnp.maximum(z, 0.0) + jnp.log1p(jnp.exp(-jnp.abs(z)))
-    a2 = dt * nal[...]
+    a2 = dt * hv_s[1:2]
     lane = lanes_of(SPAN)
     if final:
         sig = sigmoid(z)
@@ -229,7 +243,7 @@
         hand_o[...] = jnp.where(sc[0] == 0, sf_s[...], sb_s[...]).astype(BF)
 
 
-def project(sc, source, edge, slabs, wst, cv, bias, nal, e0, e1, maps=None, bc=None, final=True):
+def project(sc, source, edge, slabs, steps_t, cv, hv, e0, e1, maps=None, bc=None, final=True):
     fresh = maps is not None
     tokens, width_in = source.shape
     width = slabs.shape[0] * HEAD_DIM
@@ -265,7 +279,7 @@
     if final:
         outs += [narrow, narrow]
     steps = tile // PAD
-    args = [sc, source, source, edge, slabs, wst, cv, bias, nal, tri, e0, e1]
+    args = [sc, source, source, edge, slabs, steps_t, cv, hv, placing(hv.shape[1]), tri, e0, e1]
     in_specs = [
         SMEM,
         back((tile, width_in)),
@@ -288,6 +302,8 @@
             pltpu.VMEM((8, width), F32),
             pltpu.VMEM((STATE, width), F32),
             pltpu.VMEM((8, width), F32),
+            pltpu.VMEM((width_in, 128), BF),
+            pltpu.VMEM((8, 128), F32),
         ],
         compiler_params=pltpu.CompilerParams(vmem_limit_bytes=58 * 1024 * 1024),
         cost_estimate=cost(28),
@@ -352,8 +368,8 @@
     row = row_r[...]
     end = jnp.broadcast_to(col[SPAN - 1 : SPAN], (8, 128))
     end1 = pltpu.roll(end, GROUP, 1)
-    w = jnp.exp2(jnp.where(lane < 32, col, end1[0:1] - col))
-    dec = jnp.exp2(end)
+    w = jnp.exp2(jnp.where(lane < 32, col, jnp.where(lane < 64, end1[0:1] - col, 0.0)))
+    dec = jnp.exp2(jnp.where(lanes_of(8) < 32, end, 0.0))
     high = dec.astype(BF).astype(F32)
     wmix = jnp.concatenate([w, pltpu.roll(col, 64, 1), high, dec - high], axis=0).astype(BF)
     bc = bc_r[...]
@@ -528,9 +544,9 @@
 def back_body(
     heads, sc, xpres, vs, gfds, gbds,
     dy_r, bc_r, ps_r, pspre_r, col_r, row_r, sf_r, sb_r, gbl, pg, dff,
-    skip, cv, cs, nad, e01, seg4, seg2, segs, tris,
+    skip, cv, cs, hv, spot, e01, seg4, seg2, segs, tris,
     dv_o, dst_o, dz_o, cvg_o, csg_o, head_o, edge_o, edges_o,
-    gf_s, edge_s, edges_s, da_s, cross_s,
+    gf_s, edge_s, edges_s, da_s, cross_s, nad_s,
 ):
     step = pl.program_id(0)
     blocks = pl.num_programs(0)
@@ -550,6 +566,7 @@
         edge_s[...] = jnp.zeros_like(edge_s)
         edges_s[...] = jnp.zeros_like(edges_s)
         da_s[...] = jnp.zeros_like(da_s)
+        nad_s[...] = jnp.broadcast_to(-jnp.exp(fine(hv[...], spot[...])[1:2]), (8, 128))
         cvg_o[...] = jnp.zeros_like(cvg_o)
         csg_o[...] = jnp.zeros_like(csg_o)
         head_o[...] = jnp.zeros_like(head_o)
@@ -560,15 +577,16 @@
     row = row_r[...]
     end = jnp.broadcast_to(col[SPAN - 1 : SPAN], (8, 128))
     end1 = pltpu.roll(end, GROUP, 1)
-    w = jnp.where(lane < 64, jnp.exp2(jnp.where(lane < 32, col, end1[0:1] - col)), col)
-    dec = jnp.exp2(end)
+    w = jnp.exp2(jnp.where(lane < 32, col, jnp.where(lane < 64, end1[0:1] - col, 0.0)))
+    dec = jnp.exp2(jnp.where(lanes_of(8) < 32, end, 0.0))
     high = dec.astype(BF).astype(F32)
-    inner = jnp.exp2(jnp.where(lane < 32, end[0:1] - col, col))
+    inner = jnp.exp2(jnp.where(lane < 32, end[0:1] - col, jnp.where(lane < 64, col, 0.0)))
     steps = pltpu.roll(col, 64, 1)
     wall = jnp.concatenate([w, inner, steps, high, dec - high], axis=0).astype(BF)
     bc = bc_r[...]
     bmf, cmf = bc[:, :STATE], bc[:, STATE:]
     bm, cm = bmf.astype(BF), cmf.astype(BF)
+    nad = nad_s[0:1]
     enters_b = jnp.where(sc[6] == 1, 1.0, 0.0)
     square_r = lax.broadcasted_iota(jnp.int32, (SPAN, SPAN), 0)
     off = square_r != lane
@@ -683,10 +701,10 @@
     crossed_hi = crossed.astype(BF)
     crossed_lo = (crossed - crossed_hi.astype(F32)).astype(BF)
     da = total + (dot(crossed_hi, segs[...]) + dot(crossed_lo, segs[...]))[0:1]
-    dz = (ddt + da * nad[...]) * col
+    dz = (ddt + da * nad) * col
     dz = jnp.where((lane >= 96) & (lane < 96 + heads), dz, 0.0)
     dz_o[...] = dz.astype(BF)
-    head_o[0:1, :] += jnp.sum(da * col * nad[...], axis=0, keepdims=True)
+    head_o[0:1, :] += jnp.sum(da * col * nad, axis=0, keepdims=True)
     head_o[1:2, :] += jnp.sum(dz, axis=0, keepdims=True)
 
     @pl.when(i == 0)
@@ -695,7 +713,7 @@
         edges_o[...] = edges_s[...]
 
 
-def back(heads, sc, split, dy, bc, ps, pspre, col, row, sf, sb, gbl, pg, dff, skip, cv, cs, nad):
+def back(heads, sc, split, dy, bc, ps, pspre, col, row, sf, sb, gbl, pg, dff, skip, cv, cs, hv, spot):
     tokens, width = dy.shape
     groups = len(split[0])
     part = width // groups
@@ -728,7 +746,7 @@
         (sds((8, width), F32), full((8, width))),
         (sds((8, 128), F32), full((8, 128))),
     ]
-    shared = [skip, cv, cs, nad]
+    shared = [skip, cv, cs, hv, spot]
     shared += [jnp.asarray(m, BF) for m in (e01, seg4, seg2, segs, tris)]
     in_specs = [SMEM] + [rev((SPAN, part))] * (2 * groups)
     in_specs += [full((STATE, part))] * (2 * groups)
@@ -747,6 +765,7 @@
             pltpu.VMEM((8, 128), F32),
             pltpu.VMEM((128, 128), F32),
             pltpu.VMEM((8, width), F32),
+            pltpu.VMEM((8, 128), F32),
         ],
         compiler_params=pltpu.CompilerParams(vmem_limit_bytes=58 * 1024 * 1024),
         cost_estimate=cost(100),
@@ -760,11 +779,12 @@
 def input_kernel(groups, *refs):
     refs = list(refs)
     slabs = refs[:groups]
-    dgate, dv, dst, dz, ws, wst, gain, hid, gout, grad_o, gain_o, wg, wv = refs[groups:]
+    dgate, dv, dst, dz, ws, steps_t, gain, place, hid, gout, grad_o, gain_o, wg, wv, wst = refs[groups:]
 
     @pl.when(pl.program_id(0) == 0)
     def _():
         gain_o[...] = jnp.zeros_like(gain_o)
+        wst[...] = dot_tn(place[...].astype(BF), steps_t[...]).astype(BF)
         pairs_in = slabs[0].shape[0] // 2
         for p in range(groups * pairs_in):
             slab, h = slabs[p // pairs_in], 2 * (p % pairs_in)
@@ -772,7 +792,7 @@
             wg[:, p * 128 : (p + 1) * 128] = g.astype(BF)
             wv[:, p * 128 : (p + 1) * 128] = v.astype(BF)
 
-    dn = dot_nt(dst[...], ws[...]) + dot_nt(dz[...], wst[...])
+    dn = dot_nt(dst[...], ws[...]) + dot(dz[...], wst[...])
     dn = dn + dot_nt(dgate[...], wg[...]) + dot_nt(dv[...], wv[...])
     u = hid[...].astype(F32)
     scale = lax.rsqrt(jnp.mean(u * u, axis=1, keepdims=True) + EPS)
@@ -783,7 +803,7 @@
     grad_o[...] = (gout[...].astype(F32) + scale * (du - unit * inner)).astype(BF)
 
 
-def input_side(slabs, dgate, dv, dst, dz, ws, wst, gain, hidden, out_grad):
+def input_side(slabs, dgate, dv, dst, dz, ws, steps_t, gain, hidden, out_grad):
     tokens, width_in = hidden.shape
     tile = min(512, tokens)
 
@@ -795,18 +815,19 @@
     width = dgate.shape[1]
     streams = [dgate, dv, dst, dz]
     specs = [full(a.shape) for a in fixed] + [rows(a) for a in streams]
-    specs += [full(a.shape) for a in (ws, wst, gain)] + [rows(hidden), rows(out_grad)]
+    place = placing(steps_t.shape[0], (3,))
+    specs += [full(a.shape) for a in (ws, steps_t, gain, place)] + [rows(hidden), rows(out_grad)]
     return pl.pallas_call(
         functools.partial(input_kernel, len(slabs)),
         grid=(tokens // tile,),
         in_specs=specs,
         out_specs=[rows(hidden), full((1, width_in))],
         out_shape=[sds((tokens, width_in), BF), sds((1, width_in), F32)],
-        scratch_shapes=[pltpu.VMEM((width_in, width), BF)] * 2,
+        scratch_shapes=[pltpu.VMEM((width_in, width), BF)] * 2 + [pltpu.VMEM((128, width_in), BF)],
         compiler_params=pltpu.CompilerParams(vmem_limit_bytes=58 * 1024 * 1024),
         cost_estimate=cost(15),
         name="input_side",
-    )(*fixed, *streams, ws, wst, gain, hidden, out_grad)
+    )(*fixed, *streams, ws, steps_t, gain, place, hidden, out_grad)
 
 
 def reduce_kernel(bits, lanes, mats, *refs):
@@ -1012,11 +1033,6 @@
     )(*arrays, both, tiny)
 
 
-def spread_heads(v):
-    padded = jnp.zeros((GROUP,), F32).at[: v.shape[0]].set(v)
-    return jnp.tile(padded, 4)[None]
-
-
 def handed(total, passed, shards, up):
     pairs = [(k, k + 1) if up else (k + 1, k) for k in range(shards - 1)]
     entering = lax.ppermute(total.astype(BF), "chan", pairs)
@@ -1058,17 +1074,14 @@
 
     slab = gate_value_weight.transpose(1, 0, 2)
     edge = lax.ppermute(hidden_in[tokens - PAD :], "chan", ups)
-    vec = jnp.concatenate([step_bias, decay_log, skip_gain])
+    hv = jnp.stack([step_bias, decay_log, skip_gain])
     small = jnp.concatenate(
         [
             value_conv,
             gate_gain[None],
-            jnp.pad(vec, (0, local - 3 * local_heads))[None],
+            jnp.pad(hv, ((0, 0), (0, local - local_heads))),
         ]
     )
-
-    def step_matrix(steps):
-        return jnp.tile(jnp.pad(steps, ((0, 0), (0, GROUP - steps.shape[1]))), (1, 4))
 
     each_map = expanders(heads)
     e0, e1, _, _ = [jnp.asarray(e, BF) for e in each_map]
@@ -1081,8 +1094,7 @@
         come = swap(payload)
         small_b, wstep_b, ow_b = swap(small), swap(step_weight), swap(out_weight)
         gate, v, xpre, ff, sbl, pb, _, _, _, _, hand, vh, normed, nedge, ps, pspre, bc, psh = project(
-            sc, hidden_in, edge, slab, step_matrix(step_weight), value_conv,
-            spread_heads(step_bias), spread_heads(-jnp.exp(decay_log) * LOG2E),
+            sc, hidden_in, edge, slab, step_weight.T, value_conv, hv,
             e0[:, :local], e1[:, :local], maps=maps, final=False,
         )
         come, small_b, wstep_b, ow_b, nedge, hand = lax.optimization_barrier(
@@ -1093,29 +1105,23 @@
         halves = jnp.where(core == 0, jnp.stack([come, also]), jnp.stack([also, come]))
         slabs = [slab, halves.reshape(slab.shape)]
         smalls = [small, small_b]
-        wstep = jnp.concatenate([step_weight, wstep_b], axis=1)
+        steps_t = jnp.concatenate([step_weight.T, wstep_b.T], axis=0)
         ow = jnp.concatenate([out_weight, ow_b], axis=0)
     else:
         slabs = [lax.all_gather(slab, "chan", axis=0, tiled=True)]
         gathered = lax.all_gather(small, "chan", axis=0)
         smalls = [gathered[k] for k in range(shards)]
-        wstep = lax.all_gather(step_weight, "chan", axis=1, tiled=True)
+        steps_t = lax.all_gather(step_weight.T, "chan", axis=0, tiled=True)
         ow = lax.all_gather(out_weight, "chan", axis=0, tiled=True)
 
-    def heads_row(k, parts):
-        lo, hi = k * local_heads, (k + 1) * local_heads
-        return jnp.concatenate([p[TAPS + 1, lo:hi] for p in parts])
-
-    bias_all, dlog_all, skip_all = (heads_row(k, smalls) for k in range(3))
+    hv_all = jnp.concatenate([p[TAPS + 1 :, :local_heads] for p in smalls], axis=1)
     cv = jnp.concatenate([p[:TAPS] for p in smalls], axis=1)
     ggain = jnp.concatenate([p[TAPS : TAPS + 1] for p in smalls], axis=1)
-    skip = jnp.repeat(skip_all, HEAD_DIM)[None]
-    nad = -jnp.exp(dlog_all)
+    skip = jnp.repeat(hv_all[2:3], HEAD_DIM, axis=1)
 
     if paired:
         gate2, v2, xpre2, ff2, sbl2, pb2, _, _, _, _, hand2, vh2, col, row = project(
-            sc, normed, nedge, slabs[1], step_matrix(wstep), smalls[1][:TAPS],
-            spread_heads(bias_all), spread_heads(nad * LOG2E),
+            sc, normed, nedge, slabs[1], steps_t, smalls[1][:TAPS], hv_all,
             e0[:, local:], e1[:, local:], bc=bc, final=True,
         )
         enter = [swap(hand2), enter_b]
@@ -1127,8 +1133,7 @@
             gate, v, xpre, ff, sbl, pb, sft, sbt, pft, pbt, _, vh, normed, nedge, ps, pspre, bc, psh,
             col, row,
         ) = project(
-            sc, hidden_in, edge, slabs[0], step_matrix(wstep), cv, spread_heads(bias_all),
-            spread_heads(nad * LOG2E), e0, e1, maps=maps,
+            sc, hidden_in, edge, slabs[0], steps_t, cv, hv_all, e0, e1, maps=maps,
         )
         sfd = handed(sft, pft, shards, True)
         sbd = handed(sbt, pbt, shards, False)
@@ -1167,7 +1172,7 @@
 
     dv, dst, dz, cvg, csg, head_sums, edge_g, edges_g = back(
         heads, sc, [xs, vs, gfds, gbds], dy, bc, ps, pspre, col, row, sf, sb, gbl, pg, dff, skip, cv,
-        state_conv, spread_heads(nad),
+        state_conv, hv_all, placing(heads),
     )
 
     if paired:
@@ -1197,9 +1202,8 @@
     dwv = dot_tn(normed, dv).astype(BF)
     dws = dot_tn(normed, dst)
     dwst = dot_tn(normed, dz)[:, 96 : 96 + heads]
-    wst_tail = jnp.pad(wstep, ((0, 0), (96, GROUP - heads)))
     input_grad, norm_gain_grad = input_side(
-        slabs, dgate, dv, dst, dz, state_weight, wst_tail, gain, hidden_in, out_grad
+        slabs, dgate, dv, dst, dz, state_weight, steps_t, gain, hidden_in, out_grad
     )
 
     bias_sum = head_sums[1, 96 : 96 + heads]

time: 473 us -> 468 us (0.989)
  local copies, waits for them, and re-layouts: 45 us -> 35.4 us
  waiting for transfers between devices: 8.01 us -> 14.7 us
    another operation x15 -> x0, local copies, waits for them, and re-layouts: 6.93 us -> none  [the longest x4 3.26 us: step_matrix(): jnp.tile(jnp.pad(steps, ((0, 0), (0, GROUP - steps.shape[1]))), (1, 4))]
    ppermute x7, waiting for transfers between devices: 4.85 us -> 11.6 us  [swap(): return lax.ppermute(v, 'chan', [(0, 1), (1, 0)])]
    unnamed x67 -> x71, local copies, waits for them, and re-layouts: 11.8 us -> 11.8 us
  transfers between devices with their start and end apart: 10 -> 10, of which waited for: 3 -> 3; matrix products, arithmetic and copies ran while one was open for 12% -> 9% of each run, Pallas kernels for 13% -> 14%
where the time goes in v5:
time: 468 us; the launch traced here: 460 us
  Pallas kernels  340 us (73%)
  local copies, waits for them, and re-layouts  35.4 us (8%)
  matrix products  31.3 us (7%)
  other arithmetic  23.2 us (5%)
  waiting for transfers between devices  14.7 us (3%)
  starting transfers between devices  12.3 us (3%)
    pallas_call x1, Pallas kernels, back(): pl.pallas_call(functools.partial(back_kernel, heads, groups), grid=(block...  106 us
    pallas_call x1, Pallas kernels, reduce_all(): pl.pallas_call(functools.partial(reduce_kernel, bits, lanes, kinds), out_...  84.4 us
    pallas_call x1, Pallas kernels, mix(): pl.pallas_call(functools.partial(mix_kernel, groups), grid=(blocks,), in_...  66 us
    pallas_call x2, Pallas kernels, project(): pl.pallas_call(functools.partial(project_kernel, fresh, final, tile, chun...  63 us
    dot_general x5, matrix products, dot_tn(): lax.dot_general(a, b, (((0,), (0,)), ((), ())), preferred_element_type=F32)  31.3 us
    pallas_call x1, Pallas kernels, input_side(): pl.pallas_call(functools.partial(input_kernel, len(slabs)), grid=(tokens...  21.2 us
    unnamed x71, local copies, waits for them, and re-layouts  11.8 us
    ppermute x7, waiting for transfers between devices, swap(): return lax.ppermute(v, 'chan', [(0, 1), (1, 0)])  11.6 us
  transfers between devices with their start and end apart: 10, of which 3 were waited for; matrix products, arithmetic and copies ran while one was open for 9% of the time, Pallas kernels for 14%

profile of v5, /device:TPU:1, one launch (start us, length us, event | category | flops | bytes accessed | tf_op | source)
XLA Modules:
  0.0 459.9 jit_solution(17306971841519121310)
XLA Ops:
  2.0 4.5 collective-permute-start
  9.2 1.6 copy.50
  10.8 1.5 collective-permute-start.4
  19.1 33.8 %project.2 = (bf16[2048,768]{1,0:T(8,128)(2,1)}, bf16[2048,768]{1,0:T(8,128)(2,1)}, bf16[2048,768]{1,0:T(8,128)(2,1)}, bf16[16,64,768]{2,1,0:T(8,128)(2,1)}, bf1...) custom-call(s32[7]{0:T(128)} %stack.56.refs_0_, ...), custom_call_target="tpu_custom_call" | custom-call | flops 28000000000 | bytes 1024 | tf_op jit(solution)/shard_map/project/pallas_call | solution.py:294
  54.3 9.5 %collective-permute-done.1 = bf16[6,768,128]{2,1,0:T(8,128)(2,1)} collective-permute-done((bf16[6,768,128]{2,1,0:T(8,128)(2,1)S(1)}, bf16[6,768,128]{2,1,0:T(8,128)(2,1)}, u32[]{:S(2)}, u32[]{:S(2)}) %collective-permute-start.1) | collective-permute-done | bytes 1179680 | tf_op jit(solution)/shard_map/ppermute | solution.py:1046
  67.1 1.6 collective-permute-start.5
  68.8 3.0 fusion.14
  71.8 2.5 copy.52.refs_20_
  79.6 4.2 maximum_select_fusion
  83.8 29.2 %project.3 = (bf16[2048,768]{1,0:T(8,128)(2,1)}, bf16[2048,768]{1,0:T(8,128)(2,1)}, bf16[2048,768]{1,0:T(8,128)(2,1)}, bf16[16,64,768]{2,1,0:T(8,128)(2,1)}, bf1...) custom-call(s32[7]{0:T(128)} %stack.56.refs_0_, ...), custom_call_target="tpu_custom_call" | custom-call | flops 28000000000 | bytes 1024 | tf_op jit(solution)/shard_map/project/pallas_call | solution.py:294
  115.4 2.0 collective-permute-done.6.refs_11_.refs_13_
  118.1 66.0 %mix.1 = (bf16[2048,768]{1,0:T(8,128)(2,1)}, bf16[2048,1536]{1,0:T(8,128)(2,1)}, bf16[2048,1536]{1,0:T(8,128)(2,1)}, bf16[2048,1536]{1,0:T(8,128)(2,1)}, bf16[16...) custom-call(s32[7]{0:T(128)} %stack.56.refs_0_, ...), custom_call_target="tpu_custom_call" | custom-call | flops 60000002048 | bytes 1024 | tf_op jit(solution)/shard_map/mix/pallas_call | solution.py:515
  186.0 9.5 %convolution_convert_fusion.2.refs_0_ = bf16[768,1536]{1,0:T(8,128)(2,1)} fusion(bf16[2048,768]{1,0:T(8,128)(2,1)} %get-tuple-element.97.refs_1_.refs_2_, bf16[2048,1536]{1,0:T(8,128)(2,1)} %get-tuple-element.121.refs_2_), kind=kOutput, calls=%fused_computation.2 | convolution fusion | flops 4833017856 | bytes 11796480 | tf_op jit(solution)/shard_map/dot_general | solution.py:34
  195.5 6.8 %convolution_convert_fusion.refs_2_ = bf16[1536,768]{1,0:T(8,128)(2,1)} fusion(bf16[2048,1536]{1,0:T(8,128)(2,1)S(1)} %copy-done.31, bf16[2048,768]{1,0:T(8,128)(2,1)S(1)} %copy-done.26, bf16[2048]{0:T(1024)(128)(2,1)S(1)} %copy-done.15), kind=kOutput, calls=%fused_computation | convolution fusion | flops 4834590720 | bytes 11800576 | tf_op jit(solution)/shard_map/dot_general | solution.py:34
  203.1 105.6 %back.1 = (bf16[2048,1536]{1,0:T(8,128)(2,1)}, bf16[2048,128]{1,0:T(8,128)(2,1)}, bf16[2048,128]{1,0:T(8,128)(2,1)}, f32[4,1536]{1,0:T(4,128)}, f32[4,128]{1,0:T...) custom-call(s32[7]{0:T(128)} %stack.56.refs_0_, ...), custom_call_target="tpu_custom_call" | custom-call | flops 99999997952 | bytes 1024 | tf_op jit(solution)/shard_map/back/pallas_call | solution.py:756
  313.6 2.7 fusion.22
  318.5 3.2 collective-permute-done.9
  321.8 1.5 fusion.5.refs_3_
  323.3 2.9 convolution_convert_fusion.3
  326.2 9.4 %convolution_convert_fusion.1.refs_1_ = bf16[768,1536]{1,0:T(8,128)(2,1)} fusion(bf16[2048,768]{1,0:T(8,128)(2,1)S(1)} %copy-done.30, bf16[2048,1536]{1,0:T(8,128)(2,1)} %fusion.5.refs_3_), kind=kOutput, calls=%fused_computation.1 | convolution fusion | flops 4833017856 | bytes 11796480 | tf_op jit(solution)/shard_map/dot_general | solution.py:34
  335.6 21.2 %input_side.1 = (bf16[2048,768]{1,0:T(8,128)(2,1)}, f32[1,768]{1,0:T(1,128)}) custom-call(bf16[12,768,128]{2,1,0:T(8,128)(2,1)} %bitcast.55, bf16[12,768,128]{2,1,0:T(8,128)(2,1)} %bitcast.53, bf16[2048,1536]{1,0:T(8,128)(2,1)} %get-tuple-element.121.refs_2_, bf16[2048,1536]{1,0:T(8,128)(2,1)} %fusion.5.refs_3_, bf16[2048,128]{1,0:T(8,128)(2,1)} %copy-done.25, ...), custom_call_target="tpu_custom_call" | custom-call | flops 15000000512 | bytes 1024 | tf_op jit(solution)/shard_map/input_side/pallas_call | solution.py:820
  358.9 84.4 %reduce_all.1 = (f32[12,768,128]{2,1,0:T(8,128)}, bf16[768,768]{1,0:T(8,128)(2,1)}, bf16[768,256]{1,0:T(8,128)(2,1)}, f32[72,128]{1,0:T(8,128)}) custom-call(bf16[768,1536]{1,0:T(8,128)(2,1)} %convolution_convert_fusion.2.refs_0_, bf16[768,1536]{1,0:T(8,128)(2,1)} %convolution_convert_fusion.1.refs_1_, bf16[1536,768]{1,0:T(8,128)(2,1)} %convolution_convert_fusion.refs_2_, ...), custom_call_target="tpu_custom_call" | custom-call | tf_op jit(solution)/shard_map/reduce_all/pallas_call | solution.py:1021
  445.9 2.8 convert_element_type.43
  454.6 4.8 %copy.67 = f32[768,12,128]{2,0,1:T(8,128)} copy(f32[768,12,128]{2,0,1:T(8,128)} %bitcast.51) | data formatting | bytes 9437184
  (151 shorter events, 42.8 us)
Async XLA Ops:
  0.6 15.2 %copy-start.14 = (f32[768]{0:T(1024)S(1)}, f32[768]{0:T(1024)}, u32[]{:S(2)}) copy-start(f32[768]{0:T(1024)} %param.34) | copy-start | bytes 9220
  2.0 15.7 %collective-permute-start = (bf16[16,768]{1,0:T(8,128)(2,1)}, bf16[16,768]{1,0:T(8,128)(2,1)}, u32[]{:S(2)}, u32[]{:S(2)}) collective-permute-start(bf16[16,768]{1,0:T(8,128)(2,1)} %slice.218), channel_id=1, source_target_pairs={{0,1},{2,3},{4,5},{6,7},{8,9},{10,11},{12,13},{14,15},{16,17},{18,... | collective-permute-start | bytes 73736 | tf_op jit(solution)/shard_map/ppermute | solution.py:1076
  7.9 11.1 %copy-start.13 = (f32[3,12]{1,0:T(4,128)}, f32[3,12]{1,0:T(4,128)S(1)}, u32[]{:S(2)}) copy-start(f32[3,12]{1,0:T(4,128)S(1)} %pad_maximum_fusion.8.refs_7_) | copy-start | bytes 436
  9.2 45.0 %collective-permute-start.2 = (f32[8,768]{1,0:T(8,128)}, f32[8,768]{1,0:T(8,128)}, u32[]{:S(2)}, u32[]{:S(2)}) collective-permute-start(f32[8,768]{1,0:T(8,128)} %select_maximum_fusion), channel_id=1, source_target_pairs={{0,1},{1,0},{2,3},{3,2},{4,5},{5,4},{6,7},{7,6},{8,9},{9,8},{10,11... | collective-permute-start | bytes 73736 | tf_op jit(solution)/shard_map/ppermute | solution.py:1046
  10.8 43.4 %collective-permute-start.4 = (bf16[768,768]{0,1:T(8,128)(2,1)S(1)}, bf16[768,768]{0,1:T(8,128)(2,1)S(1)}, u32[]{:S(2)}, u32[]{:S(2)}) collective-permute-start(bf16[768,768]{0,1:T(8,128)(2,1)S(1)} %copy.50), channel_id=1, source_target_pairs={{0,1},{1,0},{2,3},{3,2},{4,5},{5,4},{6,7},{7,6},{8,9},{9,8},{10,11... | collective-permute-start | bytes 3538952 | tf_op jit(solution)/shard_map/ppermute | solution.py:1046
  12.4 41.9 %collective-permute-start.3 = (bf16[768,12]{0,1:T(8,128)(2,1)}, bf16[768,12]{0,1:T(8,128)(2,1)}, u32[]{:S(2)}, u32[]{:S(2)}) collective-permute-start(bf16[768,12]{0,1:T(8,128)(2,1)} %param.37), channel_id=1, source_target_pairs={{0,1},{1,0},{2,3},{3,2},{4,5},{5,4},{6,7},{7,6},{8,9},{9,8},{10,11... | collective-permute-start | bytes 55304 | tf_op jit(solution)/shard_map/ppermute | solution.py:1046
  17.7 46.1 %collective-permute-start.1 = (bf16[6,768,128]{2,1,0:T(8,128)(2,1)S(1)}, bf16[6,768,128]{2,1,0:T(8,128)(2,1)}, u32[]{:S(2)}, u32[]{:S(2)}) collective-permute-start(bf16[6,768,128]{2,1,0:T(8,128)(2,1)S(1)} %dynamic-slice_bitcast_fusion), channel_id=1, source_target_pairs={{0,1},{1,0},{2,3},{3,2},{4,5},{5,4},{6,7},{7,6},{8,9},{9,8},{10,11... | collective-permute-start | bytes 3538952 | tf_op jit(solution)/shard_map/ppermute | solution.py:1046
  54.3 12.9 %copy-start.1 = (bf16[768,768]{0,1:T(8,128)(2,1)}, bf16[768,768]{0,1:T(8,128)(2,1)S(1)}, u32[]{:S(2)}) copy-start(bf16[768,768]{0,1:T(8,128)(2,1)S(1)} %collective-permute-done.4) | copy-start | bytes 3538948
  64.5 14.4 %copy-start.3 = (f32[4,768]{1,0:T(4,128)}, f32[4,768]{1,0:T(4,128)S(1)}, u32[]{:S(2)}) copy-start(f32[4,768]{1,0:T(4,128)S(1)} %slice.221.refs_6_) | copy-start | bytes 36868
  67.1 12.4 %collective-permute-start.5 = (bf16[6,768,128]{2,1,0:T(8,128)(2,1)}, bf16[6,768,128]{2,1,0:T(8,128)(2,1)}, u32[]{:S(2)}, u32[]{:S(2)}) collective-permute-start(bf16[6,768,128]{2,1,0:T(8,128)(2,1)} %collective-permute-done.1), channel_id=1, source_target_pairs={{0,2},{2,0},{4,6},{6,4},{8,10},{10,8},{12,14},{14,12},{16,18},{18,... | collective-permute-start | bytes 3538952 | tf_op jit(solution)/shard_map/ppermute | solution.py:1051
  74.3 41.1 %collective-permute-start.7 = (bf16[64,768]{1,0:T(8,128)(2,1)S(1)}, bf16[64,768]{1,0:T(8,128)(2,1)S(1)}, u32[]{:S(2)}, u32[]{:S(2)}) collective-permute-start(bf16[64,768]{1,0:T(8,128)(2,1)S(1)} %copy-done.27), channel_id=1, source_target_pairs={{0,1},{1,0},{2,3},{3,2},{4,5},{5,4},{6,7},{7,6},{8,9},{9,8},{10,11... | collective-permute-start | bytes 294920 | tf_op jit(solution)/shard_map/ppermute | solution.py:1046
  75.6 8.2 %copy-start.18 = (f32[3,24]{1,0:T(4,128)}, f32[3,24]{1,0:T(4,128)S(1)}, u32[]{:S(2)}) copy-start(f32[3,24]{1,0:T(4,128)S(1)} %pad_maximum_fusion.9.refs_7_.refs_23_) | copy-start | bytes 868
  83.8 31.0 %copy-start.11 = (f32[16,128]{1,0:T(8,128)S(1)}, f32[16,128]{1,0:T(8,128)}, u32[]{:S(2)}) copy-start(f32[16,128]{1,0:T(8,128)} %get-tuple-element.143) | copy-start | bytes 24580
  113.0 4.4 collective-permute-start.6
  184.0 18.4 %collective-permute-start.8 = (bf16[64,1536]{1,0:T(8,128)(2,1)}, bf16[64,1536]{1,0:T(8,128)(2,1)S(1)}, u32[]{:S(2)}, u32[]{:S(2)}) collective-permute-start(bf16[64,1536]{1,0:T(8,128)(2,1)} %get-tuple-element.124), channel_id=1, source_target_pairs={{0,1},{1,0},{2,3},{3,2},{4,5},{5,4},{6,7},{7,6},{8,9},{9,8},{10,11... | collective-permute-start | bytes 589832 | tf_op jit(solution)/shard_map/ppermute | solution.py:1046
  186.0 9.5 %copy-start.15 = (bf16[2048]{0:T(1024)(128)(2,1)S(1)}, bf16[2048]{0:T(1024)(128)(2,1)}, u32[]{:S(2)}) copy-start(bf16[2048]{0:T(1024)(128)(2,1)} %select_convert_fusion.1) | copy-start | bytes 12292
  186.0 9.5 %copy-start.26 = (bf16[2048,768]{1,0:T(8,128)(2,1)S(1)}, bf16[2048,768]{1,0:T(8,128)(2,1)}, u32[]{:S(2)}) copy-start(bf16[2048,768]{1,0:T(8,128)(2,1)} %refs_11_.1) | copy-start | bytes 9437188
  186.0 9.5 %copy-start.31 = (bf16[2048,1536]{1,0:T(8,128)(2,1)S(1)}, bf16[2048,1536]{1,0:T(8,128)(2,1)}, u32[]{:S(2)}) copy-start(bf16[2048,1536]{1,0:T(8,128)(2,1)} %get-tuple-element.139) | copy-start | bytes 18874372
  312.8 8.9 %copy-start.4 = (f32[1664]{0:T(1024)S(1)}, f32[1664]{0:T(1024)}, u32[]{:S(2)}) copy-start(f32[1664]{0:T(1024)} %get-tuple-element.179) | copy-start | bytes 19972
  312.8 8.9 %copy-start.5 = (f32[1664]{0:T(1024)S(1)}, f32[1664]{0:T(1024)}, u32[]{:S(2)}) copy-start(f32[1664]{0:T(1024)} %get-tuple-element.180) | copy-start | bytes 19972
  312.8 8.9 %copy-start.6 = (f32[1664]{0:T(1024)S(1)}, f32[1664]{0:T(1024)}, u32[]{:S(2)}) copy-start(f32[1664]{0:T(1024)} %get-tuple-element.181) | copy-start | bytes 19972
  313.6 8.2 %copy-start.24 = (bf16[2048,128]{1,0:T(8,128)(2,1)S(1)}, bf16[2048,128]{1,0:T(8,128)(2,1)}, u32[]{:S(2)}) copy-start(bf16[2048,128]{1,0:T(8,128)(2,1)} %get-tuple-element.136) | copy-start | bytes 1572868
  316.8 4.9 %collective-permute-start.9 = (f32[8,1664]{1,0:T(8,128)S(1)}, f32[8,1664]{1,0:T(8,128)S(1)}, u32[]{:S(2)}, u32[]{:S(2)}) collective-permute-start(f32[8,1664]{1,0:T(8,128)S(1)} %pad_maximum_fusion.2), channel_id=1, source_target_pairs={{1,0},{3,2},{5,4},{7,6},{9,8},{11,10},{13,12},{15,14},{17,16},{19,... | collective-permute-start | bytes 159752 | tf_op jit(solution)/shard_map/ppermute | solution.py:1185
  321.8 13.8 %copy-start.25 = (bf16[2048,128]{1,0:T(8,128)(2,1)}, bf16[2048,128]{1,0:T(8,128)(2,1)S(1)}, u32[]{:S(2)}) copy-start(bf16[2048,128]{1,0:T(8,128)(2,1)S(1)} %fusion.12.refs_4_) | copy-start | bytes 1572868
  (18 other events, 93.6 us)
